TPU v7x, 32 devices: a whole 2x2x4 slice. The times are simulated.
32 devices in a mesh: rows: 8 (over y, x, core), cols: 4 (over z).
Axes of the slice: x: 2, y: 2, z: 4, core: 2. Of those that a mesh axis runs over, the one named last changes fastest.
Arguments:
- spectrum: bfloat16 [2, 4096, 4096], P(None, 'rows', 'cols'), may hold values from -6 to 6
- diffraction: bfloat16 [2, 32, 3, 128, 128], P(None, 'rows'), may hold values from -0.21875 to 0.21875
- order_mask: int32 [32, 3], P('rows'), may hold values from 0 to 1, as said below
- phases: float32 [2, 4096, 4096], P(None, 'rows', 'cols'), may hold values from -3.140625 to 3.140625
- transmission: float32 [4096, 4096], P('rows', 'cols'), may hold values from 0.2 to 1
- shifts: int32 [2], replicated, may hold values from 256 to 512, as said below
Outputs:
- outgoing: float32 [2, 4096, 4096], P(None, 'rows', 'cols')
Inputs may be any that keep to these rules, and one draw needn't show every extreme that they name: Each bounce's shift lies between 256 and 512; one bounce shifts by exactly 512. `order_mask`: every block carries the orders -1 and +1; the order 0 is off in some blocks.
All inputs are finite; a program needn't handle non-finite values.
Results may differ from a plain program's by a relative error of at most 0.018.
Values may be sent and summed in bfloat16 or wider, within the bound.
No kernel may reach another device: no remote copies, remote signals or barrier semaphores. Data moves between devices by JAX's collectives and lax.ppermute only.
A program may use at most 192 MiB of HBM per device.

v0:
```python
import math

import jax
import jax.numpy as jnp
from jax import lax
from jax.sharding import PartitionSpec as P

BLOCK = 128
BASE = 256
BOUNCES = 2


def shifted(value, axis, steps):
    count = lax.axis_size(axis)
    first, last = (max(0, -steps), min(count, count - steps))
    return lax.ppermute(value, axis, [(source, source + steps) for source in range(first, last)])


def twiddles(extent, sign_value, left_index, right_index):
    wrapped = left_index[:, None] * right_index[None, :] % extent
    angles = wrapped.astype(jnp.float32) * (2.0 * math.pi / extent)
    return (jnp.cos(angles), sign_value * jnp.sin(angles))


def base_tables(target, extent, sign_value):
    turn_real, turn_imag = twiddles(extent, sign_value, jnp.arange(BASE, dtype=jnp.int32), target)
    factor = 1.0 / math.sqrt(extent)
    return ((turn_real * factor).astype(jnp.bfloat16), (turn_imag * factor).astype(jnp.bfloat16))


def blocked_dft(values, axis_at, sign_value, target, extent):
    block_count = values.shape[axis_at] // BASE
    base_real, base_imag = base_tables(target, extent, sign_value)
    shaped = values.reshape(2, values.shape[1], block_count, BASE)
    form_text = "osi,ik->sok"

    def contract(left_side, right_side):
        return jnp.einsum(form_text, left_side, right_side, preferred_element_type=jnp.float32)

    inner_real = contract(shaped[0], base_real) - contract(shaped[1], base_imag)
    inner_imag = contract(shaped[0], base_imag) + contract(shaped[1], base_real)
    numbers = jnp.arange(block_count, dtype=jnp.int32) * BASE
    turn_real, turn_imag = twiddles(extent, sign_value, numbers, target)
    turn_real = turn_real[:, None, :]
    turn_imag = turn_imag[:, None, :]
    out_real = jnp.sum(turn_real * inner_real - turn_imag * inner_imag, axis=0)
    out_imag = jnp.sum(turn_real * inner_imag + turn_imag * inner_real, axis=0)
    return jnp.stack([out_real, out_imag])


def apply_blocks(left_side, right_side):
    return jnp.einsum("bjk,bkq->bjq", left_side, right_side, preferred_element_type=jnp.float32)


def diffract(current, offset_step, matrices, weights):
    below_rows = shifted(current, "rows", 1)
    above_rows = shifted(current, "rows", -1)
    widened = jnp.concatenate([below_rows, current, above_rows], axis=1)
    height = current.shape[1]
    columns = current.shape[2]
    block_count = height // BLOCK
    result_real = jnp.zeros((block_count, BLOCK, columns), jnp.float32)
    result_imag = jnp.zeros((block_count, BLOCK, columns), jnp.float32)
    for order_at in range(3):
        source = lax.dynamic_slice_in_dim(widened, height + (order_at - 1) * offset_step, height, 1)
        source = source.reshape(2, block_count, BLOCK, columns)
        kernel = matrices[:, :, order_at]
        weight_now = weights[:, order_at][:, None, None]
        result_real = result_real + weight_now * (
            apply_blocks(kernel[0], source[0]) - apply_blocks(kernel[1], source[1])
        )
        result_imag = result_imag + weight_now * (
            apply_blocks(kernel[0], source[1]) + apply_blocks(kernel[1], source[0])
        )
    return (result_real.reshape(height, columns), result_imag.reshape(height, columns))


def cross_order(received, row_count, col_count):
    width = received.shape[2]
    slab = received.shape[1] // (row_count * col_count)
    shaped = received.reshape(2, row_count, col_count, slab, width)
    return shaped.transpose(0, 4, 2, 1, 3).reshape(2, width, col_count * row_count * slab)


def cross_back(spectral, row_count, col_count):
    width = spectral.shape[1]
    slab = spectral.shape[2] // (row_count * col_count)
    shaped = spectral.reshape(2, width, col_count, row_count, slab)
    return shaped.transpose(0, 3, 2, 4, 1).reshape(2, row_count * col_count * slab, width)


def on_device(spectrum, diffraction, order_mask, phases, transmission, shifts):
    local_rows = spectrum.shape[1]
    local_cols = spectrum.shape[2]
    row_count = lax.axis_size("rows")
    col_count = lax.axis_size("cols")
    full_rows = local_rows * row_count
    full_cols = local_cols * col_count
    all_rows = jnp.arange(full_rows, dtype=jnp.int32)
    all_cols = jnp.arange(full_cols, dtype=jnp.int32)
    weights = order_mask.astype(jnp.float32)

    def row_pencil_dft(slab_values, sign_value):
        return blocked_dft(slab_values, 2, sign_value, all_rows, full_rows).astype(jnp.bfloat16)

    def column_work(column_values, mask_rows, closing):
        space = blocked_dft(column_values, 2, 1.0, all_cols, full_cols) * mask_rows[None]
        if closing:
            return space
        return blocked_dft(space.astype(jnp.bfloat16), 2, -1.0, all_cols, full_cols).astype(
            jnp.bfloat16
        )

    mask_rows = lax.all_to_all(
        transmission.astype(jnp.bfloat16), "cols", split_axis=0, concat_axis=1, tiled=True
    ).astype(transmission.dtype)
    current = spectrum
    outgoing = None
    for bounce in range(BOUNCES):
        closing = bounce == BOUNCES - 1
        diff_real, diff_imag = diffract(current, shifts[bounce], diffraction, weights)
        cosine = jnp.cos(phases[bounce])
        sine_part = jnp.sin(phases[bounce])
        wave_k = jnp.stack(
            [diff_real * cosine - diff_imag * sine_part, diff_real * sine_part + diff_imag * cosine]
        ).astype(jnp.bfloat16)
        slab_values = lax.all_to_all(
            jnp.transpose(wave_k, (0, 2, 1)), "rows", split_axis=1, concat_axis=2, tiled=True
        )
        rows_space = row_pencil_dft(slab_values, 1.0)
        received = lax.all_to_all(
            rows_space, ("rows", "cols"), split_axis=2, concat_axis=1, tiled=True
        )
        column_values = cross_order(received, row_count, col_count)
        worked = column_work(column_values, mask_rows, closing)
        if closing:
            outgoing = lax.all_to_all(
                worked.astype(jnp.bfloat16), "cols", split_axis=2, concat_axis=1, tiled=True
            ).astype(worked.dtype)
        else:
            returned = lax.all_to_all(
                cross_back(worked, row_count, col_count),
                ("rows", "cols"),
                split_axis=1,
                concat_axis=2,
                tiled=True,
            )
            back = lax.all_to_all(
                row_pencil_dft(returned, -1.0), "rows", split_axis=2, concat_axis=1, tiled=True
            )
            current = jnp.transpose(back, (0, 2, 1))
    return outgoing


def solution(mesh):
    placed = (
        P(None, "rows", "cols"),
        P(None, "rows", None, None, None),
        P("rows", None),
        P(None, "rows", "cols"),
        P("rows", "cols"),
        P(),
    )
    return jax.shard_map(
        on_device, mesh=mesh, in_specs=placed, out_specs=P(None, "rows", "cols"), check_vma=False
    )
```

profile of v0, /device:TPU:12, one launch (start us, length us, event | category | flops | bytes accessed | tf_op | source)
XLA Modules:
  0.0 1183.5 jit_solution(6509393557352233347)
XLA Ops:
  2.1 4.5 collective-permute-start.1
  14.2 34.1 %collective-permute-done = bf16[2,512,1024]{2,1,0:T(8,128)(2,1)} collective-permute-done((bf16[2,512,1024]{2,1,0:T(8,128)(2,1)}, bf16[2,512,1024]{2,1,0:T(8,128)(2,1)}, u32[]{:S(2)}, u32[]{:S(2)}) %collective-permute-start) | collective-permute-done | bytes 2097184 | tf_op jit(solution)/shard_map/ppermute | solution.py:16
  57.4 7.8 fusion.40
  65.4 4.0 copy.392
  77.7 20.9 %all-to-all-done = bf16[2,1024,512]{2,0,1:T(2,128)(2,1)S(1)} async-done(((bf16[2,1024,512]{2,0,1:T(2,128)(2,1)}), bf16[2,1024,512]{2,0,1:T(2,128)(2,1)S(1)}, u32[]{:S(2)}, u32[]{:S(2)}) %all-to-all-start) | async-done | bytes 2097184 | tf_op jit(solution)/shard_map/all_to_all | solution.py:127
  98.7 5.8 all-to-all-start.2
  107.6 22.0 %fusion.64 = f32[4096,128,16]{1,0,2:T(8,128)} fusion(bf16[128,16,256]{0,2,1:T(8,128)(2,1)S(1)} %bitcast.432), kind=kOutput, calls=%fused_computation.109 | convolution fusion | flops 4311744512 | bytes 34603008 | tf_op jit(solution)/shard_map/osi,ik->sok/dot_general | solution.py:38
  129.6 22.1 %fusion.82 = f32[4096,128,16]{1,0,2:T(8,128)} fusion(bf16[128,16,256]{0,2,1:T(8,128)(2,1)S(1)} %bitcast.433), kind=kOutput, calls=%fused_computation.118 | convolution fusion | flops 4311744512 | bytes 34603008 | tf_op jit(solution)/shard_map/osi,ik->sok/dot_general | solution.py:38
  152.3 22.0 %fusion.66 = f32[4096,128,16]{1,0,2:T(8,128)} fusion(bf16[128,16,256]{0,2,1:T(8,128)(2,1)S(1)} %bitcast.478), kind=kOutput, calls=%fused_computation.110 | convolution fusion | flops 4311744512 | bytes 34603008 | tf_op jit(solution)/shard_map/osi,ik->sok/dot_general | solution.py:38
  174.3 38.0 %fusion.21 = (bf16[128,4096]{0,1:T(8,128)(2,1)}, bf16[128,4096]{0,1:T(8,128)(2,1)S(1)}) fusion(f32[16,4096]{1,0:T(8,128)S(1)} %get-tuple-element.51, f32[16,4096]{1,0:T(8,128)S(1)} %copy-done.15, f32[4096,128,16]{1,0,2:T(8,128)} %fusion.64, f32[4096,128,16]{1,0,2:T(8,128)} %fusion.66, f32[4096,128,16]{1,0,2:T(8,128)} %fusion.82, ...), kind=kOutput, calls=%fused_computation.43 | convolution fusion | flops 4394582016 | bytes 104333312 | tf_op jit(solution)/shard_map/osi,ik->sok/dot_general | solution.py:38
  217.6 3.8 copy.402
  221.3 5.2 all-to-all-start.1
  230.1 44.3 %all-to-all-done.1 = bf16[2,128,4096]{1,0,2:T(2,128)(2,1)} async-done(((bf16[2,128,4096]{1,0,2:T(2,128)(2,1)}), bf16[2,128,4096]{1,0,2:T(2,128)(2,1)}, u32[]{:S(2)}, u32[]{:S(2)}) %all-to-all-start.1) | async-done | bytes 2097184 | tf_op jit(solution)/shard_map/all_to_all | solution.py:131
  277.6 4.1 copy.404
  283.5 22.0 %fusion.60 = f32[4096,128,16]{1,0,2:T(8,128)} fusion(bf16[128,16,256]{0,2,1:T(8,128)(2,1)S(1)} %bitcast.434), kind=kOutput, calls=%fused_computation.107 | convolution fusion | flops 4311744512 | bytes 34603008 | tf_op jit(solution)/shard_map/osi,ik->sok/dot_general | solution.py:38
  305.4 22.1 %fusion.78 = f32[4096,128,16]{1,0,2:T(8,128)} fusion(bf16[128,16,256]{0,2,1:T(8,128)(2,1)S(1)} %bitcast.435), kind=kOutput, calls=%fused_computation.116 | convolution fusion | flops 4311744512 | bytes 34603008 | tf_op jit(solution)/shard_map/osi,ik->sok/dot_general | solution.py:38
  327.6 22.0 %fusion.62 = f32[4096,128,16]{1,0,2:T(8,128)} fusion(bf16[128,16,256]{0,2,1:T(8,128)(2,1)S(1)} %bitcast.480), kind=kOutput, calls=%fused_computation.108 | convolution fusion | flops 4311744512 | bytes 34603008 | tf_op jit(solution)/shard_map/osi,ik->sok/dot_general | solution.py:38
  349.6 37.8 %fusion.17 = (f32[128,4096]{0,1:T(8,128)S(1)}, f32[128,4096]{0,1:T(8,128)S(1)}) fusion(f32[16,4096]{1,0:T(8,128)S(1)} %get-tuple-element.51, f32[16,4096]{1,0:T(8,128)S(1)} %copy-done.16, f32[4096,128,16]{1,0,2:T(8,128)} %fusion.60, f32[4096,128,16]{1,0,2:T(8,128)} %fusion.62, f32[4096,128,16]{1,0,2:T(8,128)} %fusion.78, bf16[128,16,256]{0,2,1:T(8,128)(2,1)S(1)} %bitcast.481), kind=kOutput, calls=%fused_computation.35 | convolution fusion | flops 4394582016 | bytes 106430464 | tf_op jit(solution)/shard_map/osi,ik->sok/dot_general | solution.py:38
  388.0 22.0 %fusion.56 = f32[4096,128,16]{1,0,2:T(8,128)} fusion(bf16[128,16,256]{0,2,1:T(8,128)(2,1)S(1)} %bitcast.450), kind=kOutput, calls=%fused_computation.105 | convolution fusion | flops 4311744512 | bytes 34603008 | tf_op jit(solution)/shard_map/osi,ik->sok/dot_general | solution.py:38
  410.0 22.3 %fusion.90 = f32[4096,128,16]{1,0,2:T(8,128)} fusion(bf16[128,16,256]{0,2,1:T(8,128)(2,1)S(1)} %bitcast.451), kind=kOutput, calls=%fused_computation.122 | convolution fusion | flops 4311744512 | bytes 34603008 | tf_op jit(solution)/shard_map/osi,ik->sok/dot_general | solution.py:38
  432.3 21.9 %fusion.58 = f32[4096,128,16]{1,0,2:T(8,128)} fusion(bf16[128,16,256]{0,2,1:T(8,128)(2,1)S(1)} %bitcast.484), kind=kOutput, calls=%fused_computation.106 | convolution fusion | flops 4311744512 | bytes 34603008 | tf_op jit(solution)/shard_map/osi,ik->sok/dot_general | solution.py:38
  454.2 37.8 %fusion.13 = (bf16[128,4096]{0,1:T(8,128)(2,1)S(1)}, bf16[128,4096]{0,1:T(8,128)(2,1)S(1)}) fusion(f32[16,4096]{1,0:T(8,128)S(1)} %copy-done.20, f32[16,4096]{1,0:T(8,128)S(1)} %copy-done.16, f32[4096,128,16]{1,0,2:T(8,128)} %fusion.56, f32[4096,128,16]{1,0,2:T(8,128)} %fusion.58, f32[4096,128,16]{1,0,2:T(8,128)} %fusion.90, ...), kind=kOutput, calls=%fused_computation.27 | convolution fusion | flops 4394582016 | bytes 104333312 | tf_op jit(solution)/shard_map/osi,ik->sok/dot_general | solution.py:38
  492.5 17.8 %copy.417 = bf16[2,4096,128]{2,0,1:T(2,128)(2,1)S(1)} copy(bf16[2,4096,128]{2,1,0:T(8,128)(2,1)S(1)} %bitcast.469) | data formatting | bytes 4194304 | tf_op jit(solution)/shard_map/reshape | solution.py:89
  510.3 51.9 %all_to_all.115 = bf16[2,4096,128]{2,0,1:T(2,128)(2,1)S(1)} all-to-all(bf16[2,4096,128]{2,0,1:T(2,128)(2,1)S(1)} %copy.417), channel_id=1, replica_groups=mesh['rows'=8,'cols'=4] {'rows','cols'}, dimensions={1} | all-to-all | bytes 4194304 | tf_op jit(solution)/shard_map/all_to_all | solution.py:141
  563.3 22.0 %fusion.52 = f32[4096,128,16]{1,0,2:T(8,128)} fusion(bf16[128,16,256]{0,2,1:T(8,128)(2,1)S(1)} %bitcast.436), kind=kOutput, calls=%fused_computation.103 | convolution fusion | flops 4311744512 | bytes 34603008 | tf_op jit(solution)/shard_map/osi,ik->sok/dot_general | solution.py:38
  585.3 22.1 %fusion.86 = f32[4096,128,16]{1,0,2:T(8,128)} fusion(bf16[128,16,256]{0,2,1:T(8,128)(2,1)S(1)} %bitcast.437), kind=kOutput, calls=%fused_computation.120 | convolution fusion | flops 4311744512 | bytes 34603008 | tf_op jit(solution)/shard_map/osi,ik->sok/dot_general | solution.py:38
  608.0 22.0 %fusion.54 = f32[4096,128,16]{1,0,2:T(8,128)} fusion(bf16[128,16,256]{0,2,1:T(8,128)(2,1)S(1)} %bitcast.476), kind=kOutput, calls=%fused_computation.104 | convolution fusion | flops 4311744512 | bytes 34603008 | tf_op jit(solution)/shard_map/osi,ik->sok/dot_general | solution.py:38
  630.0 38.0 %fusion.9 = (bf16[128,4096]{0,1:T(8,128)(2,1)}, bf16[128,4096]{0,1:T(8,128)(2,1)S(1)}) fusion(f32[16,4096]{1,0:T(8,128)S(1)} %copy-done.20, f32[16,4096]{1,0:T(8,128)S(1)} %copy-done.17, f32[4096,128,16]{1,0,2:T(8,128)} %fusion.52, f32[4096,128,16]{1,0,2:T(8,128)} %fusion.54, f32[4096,128,16]{1,0,2:T(8,128)} %fusion.86, bf16[128,16,256]{0,2,1:T(8,128)(2,1)S(1)} %bitcast.477), kind=kOutput, calls=%fused_computation.19 | convolution fusion | flops 4394582016 | bytes 104333312 | tf_op jit(solution)/shard_map/osi,ik->sok/dot_general | solution.py:38
  676.0 30.1 %all_to_all.116 = bf16[2,128,4096]{1,0,2:T(2,128)(2,1)S(1)} all-to-all(bf16[2,128,4096]{1,0,2:T(2,128)(2,1)} %copy.427), channel_id=1, replica_groups=mesh['rows'=8,'cols'=4] {'rows'}, dimensions={2} | all-to-all | bytes 4194304 | tf_op jit(solution)/shard_map/all_to_all | solution.py:148
  712.5 4.5 collective-permute-start.3
  734.7 23.8 %collective-permute-done.2 = bf16[2,512,1024]{1,2,0:T(8,128)(2,1)} collective-permute-done((bf16[2,512,1024]{1,2,0:T(8,128)(2,1)S(1)}, bf16[2,512,1024]{1,2,0:T(8,128)(2,1)}, u32[]{:S(2)}, u32[]{:S(2)}) %collective-permute-start.2) | collective-permute-done | bytes 2097184 | tf_op jit(solution)/shard_map/ppermute | solution.py:16
  761.6 4.0 constant_dynamic-slice_fusion.4
  781.0 4.5 multiply_add_fusion.1
  789.1 8.1 fusion.36
  797.4 4.0 copy.436
  801.5 30.5 %all_to_all.117 = bf16[2,1024,512]{2,0,1:T(2,128)(2,1)S(1)} all-to-all(bf16[2,1024,512]{2,0,1:T(2,128)(2,1)} %copy.436), channel_id=1, replica_groups=mesh['rows'=8,'cols'=4] {'rows'}, dimensions={1} | all-to-all | bytes 4194304 | tf_op jit(solution)/shard_map/all_to_all | solution.py:127
  833.2 22.0 %fusion.48 = f32[4096,128,16]{1,0,2:T(8,128)} fusion(bf16[128,16,256]{0,2,1:T(8,128)(2,1)S(1)} %bitcast.444), kind=kOutput, calls=%fused_computation.101 | convolution fusion | flops 4311744512 | bytes 34603008 | tf_op jit(solution)/shard_map/osi,ik->sok/dot_general | solution.py:38
  855.2 22.1 %fusion.74 = f32[4096,128,16]{1,0,2:T(8,128)} fusion(bf16[128,16,256]{0,2,1:T(8,128)(2,1)S(1)} %bitcast.445), kind=kOutput, calls=%fused_computation.114 | convolution fusion | flops 4311744512 | bytes 34603008 | tf_op jit(solution)/shard_map/osi,ik->sok/dot_general | solution.py:38
  877.9 22.0 %fusion.50 = f32[4096,128,16]{1,0,2:T(8,128)} fusion(bf16[128,16,256]{0,2,1:T(8,128)(2,1)S(1)} %bitcast.482), kind=kOutput, calls=%fused_computation.102 | convolution fusion | flops 4311744512 | bytes 34603008 | tf_op jit(solution)/shard_map/osi,ik->sok/dot_general | solution.py:38
  899.9 38.0 %fusion.5 = (bf16[128,4096]{0,1:T(8,128)(2,1)}, bf16[128,4096]{0,1:T(8,128)(2,1)S(1)}) fusion(f32[16,4096]{1,0:T(8,128)S(1)} %copy-done.14, f32[16,4096]{1,0:T(8,128)S(1)} %copy-done.18, f32[4096,128,16]{1,0,2:T(8,128)} %fusion.48, f32[4096,128,16]{1,0,2:T(8,128)} %fusion.50, f32[4096,128,16]{1,0,2:T(8,128)} %fusion.74, bf16[128,16,256]{0,2,1:T(8,128)(2,1)S(1)} %bitcast.483), kind=kOutput, calls=%fused_computation.11 | convolution fusion | flops 4394582016 | bytes 104333312 | tf_op jit(solution)/shard_map/osi,ik->sok/dot_general | solution.py:38
  945.9 51.3 %all_to_all.118 = bf16[2,128,4096]{1,0,2:T(2,128)(2,1)S(1)} all-to-all(bf16[2,128,4096]{1,0,2:T(2,128)(2,1)} %copy.446), channel_id=1, replica_groups=mesh['rows'=8,'cols'=4] {'rows','cols'}, dimensions={2} | all-to-all | bytes 4194304 | tf_op jit(solution)/shard_map/all_to_all | solution.py:131
  1002.2 22.0 %fusion.44 = f32[4096,128,16]{1,0,2:T(8,128)} fusion(bf16[128,16,256]{0,2,1:T(8,128)(2,1)S(1)} %bitcast.446), kind=kOutput, calls=%fused_computation.99 | convolution fusion | flops 4311744512 | bytes 34603008 | tf_op jit(solution)/shard_map/osi,ik->sok/dot_general | solution.py:38
  1024.2 22.1 %fusion.70 = f32[4096,128,16]{1,0,2:T(8,128)} fusion(bf16[128,16,256]{0,2,1:T(8,128)(2,1)S(1)} %bitcast.447), kind=kOutput, calls=%fused_computation.112 | convolution fusion | flops 4311744512 | bytes 34603008 | tf_op jit(solution)/shard_map/osi,ik->sok/dot_general | solution.py:38
  1046.4 22.0 %fusion.46 = f32[4096,128,16]{1,0,2:T(8,128)} fusion(bf16[128,16,256]{0,2,1:T(8,128)(2,1)S(1)} %bitcast.474), kind=kOutput, calls=%fused_computation.100 | convolution fusion | flops 4311744512 | bytes 34603008 | tf_op jit(solution)/shard_map/osi,ik->sok/dot_general | solution.py:38
  1068.3 38.0 %fusion.1 = (f32[128,4096]{0,1:T(8,128)S(1)}, f32[128,4096]{0,1:T(8,128)S(1)}) fusion(f32[16,4096]{1,0:T(8,128)S(1)} %copy-done.14, f32[16,4096]{1,0:T(8,128)S(1)} %copy-done.19, f32[4096,128,16]{1,0,2:T(8,128)} %fusion.44, f32[4096,128,16]{1,0,2:T(8,128)} %fusion.46, f32[4096,128,16]{1,0,2:T(8,128)} %fusion.70, bf16[128,16,256]{0,2,1:T(8,128)(2,1)S(1)} %bitcast.475), kind=kOutput, calls=%fused_computation.3 | convolution fusion | flops 4394582016 | bytes 106430464 | tf_op jit(solution)/shard_map/osi,ik->sok/dot_general | solution.py:38
  1106.7 17.8 %copy.455 = bf16[2,128,4096]{1,0,2:T(2,128)(2,1)S(1)} copy(bf16[2,128,4096]{1,2,0:T(8,128)(2,1)S(1)} %fusion.28) | data formatting | bytes 4194304 | tf_op jit(solution)/shard_map/convert_element_type | solution.py:138
  1124.5 50.8 %all_to_all.119 = bf16[2,128,4096]{1,0,2:T(2,128)(2,1)S(1)} all-to-all(bf16[2,128,4096]{1,0,2:T(2,128)(2,1)S(1)} %copy.455), channel_id=1, replica_groups=mesh['rows'=8,'cols'=4] {'cols'}, dimensions={2} | all-to-all | bytes 4194304 | tf_op jit(solution)/shard_map/all_to_all | solution.py:137
  1177.7 5.3 copy.457
  (147 shorter events, 115.3 us)
Async XLA Ops:
  0.0 12.5 %copy-start.2 = (bf16[2,4,3,128,128]{4,3,2,1,0:T(8,128)(2,1)S(1)}, bf16[2,4,3,128,128]{4,3,2,1,0:T(8,128)(2,1)}, u32[]{:S(2)}) copy-start(bf16[2,4,3,128,128]{4,3,2,1,0:T(8,128)(2,1)} %param.7) | copy-start | bytes 2359300
  0.0 48.3 %collective-permute-start = (bf16[2,512,1024]{2,1,0:T(8,128)(2,1)}, bf16[2,512,1024]{2,1,0:T(8,128)(2,1)}, u32[]{:S(2)}, u32[]{:S(2)}) collective-permute-start(bf16[2,512,1024]{2,1,0:T(8,128)(2,1)} %param.6), channel_id=1, source_target_pairs={{0,4},{4,8},{8,12},{12,16},{16,20},{20,24},{24,28},{1,5},{5,9},{9,... | collective-permute-start | bytes 6291464 | tf_op jit(solution)/shard_map/ppermute | solution.py:16
  2.1 48.3 %collective-permute-start.1 = (bf16[2,512,1024]{2,1,0:T(8,128)(2,1)}, bf16[2,512,1024]{2,1,0:T(8,128)(2,1)S(1)}, u32[]{:S(2)}, u32[]{:S(2)}) collective-permute-start(bf16[2,512,1024]{2,1,0:T(8,128)(2,1)} %param.6), channel_id=1, source_target_pairs={{4,0},{8,4},{12,8},{16,12},{20,16},{24,20},{28,24},{5,1},{9,5},{13... | collective-permute-start | bytes 6291464 | tf_op jit(solution)/shard_map/ppermute | solution.py:16
  10.8 44.5 %copy-start.21 = (f32[4]{0:T(128)}, f32[4]{0:T(128)S(1)}, u32[]{:S(2)}) copy-start(f32[4]{0:T(128)S(1)} %get-tuple-element.17) | copy-start | bytes 52
  10.8 44.5 %copy-start.23 = (f32[4]{0:T(128)}, f32[4]{0:T(128)S(1)}, u32[]{:S(2)}) copy-start(f32[4]{0:T(128)S(1)} %get-tuple-element.18) | copy-start | bytes 52
  10.8 44.5 %copy-start.25 = (f32[4]{0:T(128)}, f32[4]{0:T(128)S(1)}, u32[]{:S(2)}) copy-start(f32[4]{0:T(128)S(1)} %get-tuple-element.19) | copy-start | bytes 52
  13.8 36.3 %copy-start.5 = (bf16[2,512,1024]{2,1,0:T(8,128)(2,1)S(1)}, bf16[2,512,1024]{2,1,0:T(8,128)(2,1)}, u32[]{:S(2)}) copy-start(bf16[2,512,1024]{2,1,0:T(8,128)(2,1)} %param.6) | copy-start | bytes 6291460
  55.2 2.2 copy-start.11
  69.5 29.2 %all-to-all-start = ((bf16[2,1024,512]{2,0,1:T(2,128)(2,1)}), bf16[2,1024,512]{2,0,1:T(2,128)(2,1)S(1)}, u32[]{:S(2)}, u32[]{:S(2)}) async-start(bf16[2,1024,512]{2,0,1:T(2,128)(2,1)} %copy.392), calls=%async_computation | async-start | bytes 4194304 | tf_op jit(solution)/shard_map/all_to_all | solution.py:127
  77.7 271.9 %copy-start.13 = (f32[16,4096]{1,0:T(8,128)}, f32[16,4096]{1,0:T(8,128)S(1)}, u32[]{:S(2)}) copy-start(f32[16,4096]{1,0:T(8,128)S(1)} %get-tuple-element.51) | copy-start | bytes 786436
  98.7 122.7 %all-to-all-start.2 = ((bf16[4,128,1024]{2,1,0:T(8,128)(2,1)}), bf16[4,128,1024]{2,1,0:T(8,128)(2,1)S(1)}, u32[]{:S(2)}, u32[]{:S(2)}) async-start(bf16[4,128,1024]{2,1,0:T(8,128)(2,1)} %bitcast.45), calls=%async_computation.2 | async-start | bytes 2097152 | tf_op jit(solution)/shard_map/all_to_all | solution.py:114
  152.3 22.0 %copy-start.15 = (f32[16,4096]{1,0:T(8,128)S(1)}, f32[16,4096]{1,0:T(8,128)}, u32[]{:S(2)}) copy-start(f32[16,4096]{1,0:T(8,128)} %get-tuple-element.52) | copy-start | bytes 786436
  221.3 53.0 %all-to-all-start.1 = ((bf16[2,128,4096]{1,0,2:T(2,128)(2,1)}), bf16[2,128,4096]{1,0,2:T(2,128)(2,1)}, u32[]{:S(2)}, u32[]{:S(2)}) async-start(bf16[2,128,4096]{1,0,2:T(2,128)(2,1)} %copy.402), calls=%async_computation.1 | async-start | bytes 4194304 | tf_op jit(solution)/shard_map/all_to_all | solution.py:131
  230.1 157.4 %copy-start = (f32[128,4,1024]{0,2,1:T(8,128)}, f32[128,4,1024]{0,2,1:T(8,128)S(1)}, u32[]{:S(2)}) copy-start(f32[128,4,1024]{0,2,1:T(8,128)S(1)} %copy.411) | copy-start | bytes 6291460
  327.6 22.0 %copy-start.16 = (f32[16,4096]{1,0:T(8,128)S(1)}, f32[16,4096]{1,0:T(8,128)}, u32[]{:S(2)}) copy-start(f32[16,4096]{1,0:T(8,128)} %get-tuple-element.52) | copy-start | bytes 786436
  432.3 21.9 %copy-start.20 = (f32[16,4096]{1,0:T(8,128)S(1)}, f32[16,4096]{1,0:T(8,128)}, u32[]{:S(2)}) copy-start(f32[16,4096]{1,0:T(8,128)} %get-tuple-element.50) | copy-start | bytes 786436
  608.0 22.0 %copy-start.17 = (f32[16,4096]{1,0:T(8,128)S(1)}, f32[16,4096]{1,0:T(8,128)}, u32[]{:S(2)}) copy-start(f32[16,4096]{1,0:T(8,128)} %get-tuple-element.52) | copy-start | bytes 786436
  710.6 48.0 %collective-permute-start.2 = (bf16[2,512,1024]{1,2,0:T(8,128)(2,1)S(1)}, bf16[2,512,1024]{1,2,0:T(8,128)(2,1)}, u32[]{:S(2)}, u32[]{:S(2)}) collective-permute-start(bf16[2,512,1024]{1,2,0:T(8,128)(2,1)S(1)} %bitcast.420), channel_id=1, source_target_pairs={{0,4},{4,8},{8,12},{12,16},{16,20},{20,24},{24,28},{1,5},{5,9},{9,... | collective-permute-start | bytes 6291464 | tf_op jit(solution)/shard_map/ppermute | solution.py:16
  712.5 46.0 %collective-permute-start.3 = (bf16[2,512,1024]{1,2,0:T(8,128)(2,1)S(1)}, bf16[2,512,1024]{1,2,0:T(8,128)(2,1)}, u32[]{:S(2)}, u32[]{:S(2)}) collective-permute-start(bf16[2,512,1024]{1,2,0:T(8,128)(2,1)S(1)} %bitcast.421), channel_id=1, source_target_pairs={{4,0},{8,4},{12,8},{16,12},{20,16},{24,20},{28,24},{5,1},{9,5},{13... | collective-permute-start | bytes 6291464 | tf_op jit(solution)/shard_map/ppermute | solution.py:16
  718.9 6.2 copy-start.3
  725.2 6.0 copy-start.4
  776.1 3.7 copy-start.22
  776.1 3.7 copy-start.24
  776.2 3.7 copy-start.26
  779.4 1.6 copy-start.8
  781.0 4.5 copy-start.6
  781.0 4.7 copy-start.7
  781.0 5.3 copy-start.9
  781.0 5.9 copy-start.10
  786.9 2.2 copy-start.12
  877.9 22.0 %copy-start.14 = (f32[16,4096]{1,0:T(8,128)S(1)}, f32[16,4096]{1,0:T(8,128)}, u32[]{:S(2)}) copy-start(f32[16,4096]{1,0:T(8,128)} %copy-done.13) | copy-start | bytes 786436
  877.9 22.0 %copy-start.18 = (f32[16,4096]{1,0:T(8,128)S(1)}, f32[16,4096]{1,0:T(8,128)}, u32[]{:S(2)}) copy-start(f32[16,4096]{1,0:T(8,128)} %get-tuple-element.52) | copy-start | bytes 786436
  1046.3 22.0 %copy-start.19 = (f32[16,4096]{1,0:T(8,128)S(1)}, f32[16,4096]{1,0:T(8,128)}, u32[]{:S(2)}) copy-start(f32[16,4096]{1,0:T(8,128)} %get-tuple-element.52) | copy-start | bytes 786436
  1068.3 38.0 %copy-start.1 = (f32[128,4,1024]{0,2,1:T(8,128)S(1)}, f32[128,4,1024]{0,2,1:T(8,128)}, u32[]{:S(2)}) copy-start(f32[128,4,1024]{0,2,1:T(8,128)} %copy-done) | copy-start | bytes 6291460
where the time goes:
time: 1200 us; the launch traced here: 1180 us
  matrix products  654 us (54%)
  blocking collectives  215 us (18%)
  local copies, waits for them, and re-layouts  125 us (10%)
  waiting for transfers between devices  123 us (10%)
  other arithmetic  34 us (3%)
  starting transfers between devices  27.6 us (2%)
    dot_general x24, matrix products, contract(): jnp.einsum(form_text, left_side, right_side, preferred_element_type=jnp.f...  624 us
    ppermute x4, waiting for transfers between devices, shifted(): lax.ppermute(value, axis, [(source, source + steps) for source in range(f...  57.9 us
    all_to_all x1, blocking collectives, on_device(): lax.all_to_all(cross_back(worked, row_count, col_count), ('rows', 'cols')...  51.9 us
    all_to_all x1, blocking collectives, on_device(): lax.all_to_all(rows_space, ('rows', 'cols'), split_axis=2, concat_axis=1,...  51.3 us
    all_to_all x1, blocking collectives, on_device(): lax.all_to_all(worked.astype(jnp.bfloat16), 'cols', split_axis=2, concat_...  50.8 us
    all_to_all x1, waiting for transfers between devices, on_device(): lax.all_to_all(rows_space, ('rows', 'cols'), split_axis=2, concat_axis=1,...  44.3 us
    all_to_all x1, blocking collectives, on_device(): lax.all_to_all(jnp.transpose(wave_k, (0, 2, 1)), 'rows', split_axis=1, co...  30.5 us
    dot_general x24, matrix products, apply_blocks(): jnp.einsum('bjk,bkq->bjq', left_side, right_side, preferred_element_type=...  30.2 us
  transfers between devices with their start and end apart: 7, of which 4 were waited for; matrix products, arithmetic and copies ran while one was open for 13% of the time, Pallas kernels for 0%

commit v1 on v0

v1 whole, which is shorter than its diff:
```python
import math

import jax
import jax.numpy as jnp
import ml_dtypes
import numpy as np
from jax import lax
from jax.experimental import pallas as pl
from jax.experimental.pallas import tpu as pltpu
from jax.sharding import PartitionSpec as P

BLOCK = 128
LANES = 128
RADIX = 16
BOUNCES = 2
VMEM_LIMIT = 56 * 1024 * 1024
BF16 = jnp.bfloat16
F32 = jnp.float32


def params():
    return pltpu.CompilerParams(vmem_limit_bytes=VMEM_LIMIT)


def vmem(count):
    return [pl.BlockSpec(memory_space=pltpu.VMEM) for _ in range(count)]


def column_tables(extent):
    part = extent // RADIX
    first = np.arange(RADIX)[:, None, None]
    second = np.arange(part)[None, :, None]
    inner = np.arange(part)[None, None, :]
    angle = ((first + RADIX * second) * inner % extent) * (2.0 * np.pi / extent)
    scale = 1.0 / math.sqrt(extent)
    real, imag = np.cos(angle) * scale, np.sin(angle) * scale
    forward = np.concatenate([real, imag], axis=1)
    backward = np.concatenate([real.transpose(0, 2, 1), imag.transpose(0, 2, 1)], axis=1)
    return forward.astype(ml_dtypes.bfloat16), backward.astype(ml_dtypes.bfloat16)


def row_tables(extent, part):
    radix = extent // part
    inner = np.arange(part)
    angle = (inner[:, None] * inner[None, :] % part) * (2.0 * np.pi / part)
    scale = 1.0 / math.sqrt(extent)
    core = np.concatenate([np.cos(angle) * scale, np.sin(angle) * scale], axis=1)
    turn = (np.arange(radix)[:, None] * inner[None, :]) * (2.0 * np.pi / extent)
    turns = np.stack([np.cos(turn), np.sin(turn)], axis=1)[:, :, None, :]
    return core.astype(ml_dtypes.bfloat16), turns.astype(np.float32)


def regroup(count, fast):
    natural = np.arange(count)
    grouped = (natural % fast) * (count // fast) + natural // fast
    matrix = np.zeros((count, count), np.float32)
    matrix[natural, grouped] = 1.0
    return matrix.astype(ml_dtypes.bfloat16)


def angle_series():
    squares = np.polynomial.chebyshev.chebpts1(200) * (np.pi**2 / 2) + np.pi**2 / 2
    angles = np.sqrt(squares)

    def fit(values, degree):
        series = np.polynomial.chebyshev.Chebyshev.fit(squares, values, degree, domain=[0, np.pi**2])
        return [float(c) for c in series.convert(kind=np.polynomial.Polynomial).coef]

    return fit(np.sin(angles) / angles, 7), fit(np.cos(angles), 8)


SINE_SERIES, COSINE_SERIES = angle_series()


def cos_sin(angle):
    square = angle * angle

    def series(coefs):
        total = jnp.full_like(square, coefs[-1])
        for coef in coefs[-2::-1]:
            total = total * square + coef
        return total

    return series(COSINE_SERIES), angle * series(SINE_SERIES)


def butterfly(values, sign):
    count = len(values)
    if count == 1:
        return values
    even, odd = butterfly(values[0::2], sign), butterfly(values[1::2], sign)
    low, high = [], []
    for at in range(count // 2):
        real, imag = odd[at]
        if at == 0:
            turned = real, imag
        elif 4 * at == count:
            turned = (-imag, real) if sign > 0 else (imag, -real)
        elif 8 * at == count:
            half = math.sqrt(0.5)
            turned = (
                ((real - imag) * half, (real + imag) * half)
                if sign > 0
                else ((real + imag) * half, (imag - real) * half)
            )
        elif 8 * at == 3 * count:
            half = math.sqrt(0.5)
            turned = (
                ((real + imag) * -half, (real - imag) * half)
                if sign > 0
                else ((imag - real) * half, (real + imag) * -half)
            )
        else:
            cosine = math.cos(2 * math.pi * at / count)
            sine = sign * math.sin(2 * math.pi * at / count)
            turned = real * cosine - imag * sine, real * sine + imag * cosine
        low.append((even[at][0] + turned[0], even[at][1] + turned[1]))
        high.append((even[at][0] - turned[0], even[at][1] - turned[1]))
    return low + high


def dot(left, right):
    return jnp.dot(left, right, preferred_element_type=F32)


def loop(count, body):
    def step(at, carry):
        body(at)
        return carry

    lax.fori_loop(0, count, step, 0)


def column_body(later, cur_ref, mats_ref, mask_ref, shift_ref, phase_ref, forward_ref, backward_ref, out_ref, padded, wave, mixed):
    rows_at, cols_at, firsts, _, seconds, width = out_ref.shape
    block_rows = mats_ref.shape[2]
    extent = wave.shape[1]
    part = extent // RADIX
    height = (padded.shape[1] - extent) // 2
    blocks = extent // BLOCK
    padded[:, pl.ds(0, height)] = jnp.zeros((2, height, width), F32)
    padded[:, pl.ds(height + extent, height)] = jnp.zeros((2, height, width), F32)

    if later:

        def unfold(at):
            group, first = at // firsts, at % firsts
            real = cur_ref[:, group, first, 0].reshape(part, width)
            imag = cur_ref[:, group, first, 1].reshape(part, width)
            got = dot(backward_ref[at], jnp.concatenate([real, imag], axis=1))
            wave[0, pl.ds(at * part, part)] = got[:part, :width] + got[part:, width:]
            wave[1, pl.ds(at * part, part)] = got[:part, width:] - got[part:, :width]

        loop(RADIX, unfold)

        def gather(at):
            rows = at * 16
            values = [
                (wave[0, pl.ds(one * part + rows, 16)], wave[1, pl.ds(one * part + rows, 16)])
                for one in range(RADIX)
            ]
            for one, (real, imag) in enumerate(butterfly(values, -1)):
                padded[0, pl.ds(height + one * part + rows, 16)] = real
                padded[1, pl.ds(height + one * part + rows, 16)] = imag

        loop(part // 16, gather)
    else:

        def spread(at):
            rows = pl.ds(height + at * height, height)
            padded[0, rows] = cur_ref[at, 0].astype(F32)
            padded[1, rows] = cur_ref[at, 1].astype(F32)

        loop(extent // height, spread)

    shift = shift_ref[0]

    def diffract(at):
        owner, inner = at // block_rows, at % block_rows
        lefts, rights = [], []
        for order in range(3):
            rows = pl.ds(height + at * BLOCK + (order - 1) * shift, BLOCK)
            rights.append(jnp.concatenate([padded[0, rows], padded[1, rows]], axis=1).astype(BF16))
            weight = mask_ref[at * 3 + order].astype(F32)
            lefts.append(
                jnp.concatenate([mats_ref[owner, 0, inner, order], mats_ref[owner, 1, inner, order]], axis=0)
                * weight.astype(BF16)
            )
        got = dot(jnp.concatenate(lefts, axis=1), jnp.concatenate(rights, axis=0))
        real = got[:BLOCK, :width] - got[BLOCK:, width:]
        imag = got[:BLOCK, width:] + got[BLOCK:, :width]
        rows = pl.ds(pl.multiple_of(at * BLOCK, BLOCK), BLOCK)
        cosine, sine = cos_sin(phase_ref[rows])
        wave[0, rows] = real * cosine - imag * sine
        wave[1, rows] = real * sine + imag * cosine

    loop(blocks, diffract)

    def mix(at):
        rows = at * 16
        values = [
            (wave[0, pl.ds(one * part + rows, 16)], wave[1, pl.ds(one * part + rows, 16)]) for one in range(RADIX)
        ]
        for one, (real, imag) in enumerate(butterfly(values, 1)):
            mixed[one, pl.ds(pl.multiple_of(rows, 16), 16)] = jnp.concatenate([real, imag], axis=1).astype(BF16)

    loop(part // 16, mix)

    def fold(at):
        group, first = at // firsts, at % firsts
        got = dot(forward_ref[at], mixed[at])
        real = (got[:part, :width] - got[part:, width:]).astype(BF16)
        imag = (got[:part, width:] + got[part:, :width]).astype(BF16)
        out_ref[:, group, first, 0] = real.reshape(rows_at, seconds, width)
        out_ref[:, group, first, 1] = imag.reshape(rows_at, seconds, width)

    loop(RADIX, fold)


def column_work(later, current, mats, mask, shift, phase, tables, row_count, col_count):
    extent, width = phase.shape
    part = extent // RADIX
    height = extent // row_count

    def body(*refs):
        column_body(later, *refs)

    in_specs = vmem(7)
    in_specs[2] = pl.BlockSpec(memory_space=pltpu.SMEM)
    in_specs[3] = pl.BlockSpec(memory_space=pltpu.SMEM)
    return pl.pallas_call(
        body,
        out_shape=jax.ShapeDtypeStruct(
            (row_count, col_count, RADIX // col_count, 2, part // row_count, width), BF16
        ),
        in_specs=in_specs,
        out_specs=vmem(1)[0],
        scratch_shapes=[
            pltpu.VMEM((2, extent + 2 * height, width), F32),
            pltpu.VMEM((2, extent, width), F32),
            pltpu.VMEM((RADIX, part, 2 * width), BF16),
        ],
        compiler_params=params(),
        name="column_later" if later else "column_first",
    )(current, mats, mask, shift, phase, *tables)


def row_mix(order, in_ref, turn_ref, mixed):
    blocks, firsts, _, seconds, lanes = in_ref.shape
    radix, _, part = mixed.shape
    tiles = part // lanes
    rows = firsts * seconds

    def one_first(first):
        for tile in range(tiles):
            across = pl.ds(tile * lanes, lanes)
            for at in range(0, seconds, 16):
                values = [
                    (
                        in_ref[order[one * tiles + tile], first, 0, pl.ds(at, 16)].astype(F32),
                        in_ref[order[one * tiles + tile], first, 1, pl.ds(at, 16)].astype(F32),
                    )
                    for one in range(radix)
                ]
                for one, (real, imag) in enumerate(butterfly(values, 1)):
                    cosine, sine = turn_ref[one, 0, :, across], turn_ref[one, 1, :, across]
                    down = pl.multiple_of(first * seconds + at, 16)
                    mixed[one, pl.ds(down, 16), across] = (real * cosine - imag * sine).astype(BF16)
                    mixed[one, pl.ds(rows + down, 16), across] = (real * sine + imag * cosine).astype(BF16)

    loop(firsts, one_first)


def core_dot(left, core_ref, sign, tile):
    half, part = left.shape[0] // 2, core_ref.shape[0]
    by_real = dot(left, core_ref[:, tile : tile + 256])
    by_imag = dot(left, core_ref[:, part + tile : part + tile + 256])
    if sign > 0:
        return by_real[:half] - by_imag[half:], by_real[half:] + by_imag[:half]
    return by_real[:half] + by_imag[half:], by_real[half:] - by_imag[:half]


def row_body(order, in_ref, mask_ref, core_ref, turn_ref, out_ref, mixed, passed, back):
    blocks, firsts, _, seconds, lanes = in_ref.shape
    radix, _, part = mixed.shape
    tiles = part // lanes
    rows = firsts * seconds
    row_mix(order, in_ref, turn_ref, mixed)

    def one(at):
        for tile in range(0, part, 256):
            real, imag = core_dot(mixed[at], core_ref, 1, tile)
            for within in range(0, 256, lanes):
                number = (tile + within) // lanes
                kept = mask_ref[number, at].astype(F32)
                across = pl.ds(tile + within, lanes)
                passed[pl.ds(0, rows), across] = (real[:, within : within + lanes] * kept).astype(BF16)
                passed[pl.ds(rows, rows), across] = (imag[:, within : within + lanes] * kept).astype(BF16)
        for tile in range(0, part, 256):
            real, imag = core_dot(passed[...], core_ref, -1, tile)
            across = pl.ds(tile, 256)
            cosine, sine = turn_ref[at, 0, :, across], turn_ref[at, 1, :, across]
            back[at, 0, :, across] = real * cosine + imag * sine
            back[at, 1, :, across] = imag * cosine - real * sine

    loop(radix, one)

    def close(first):
        for tile in range(tiles):
            across = pl.ds(tile * lanes, lanes)
            for at in range(0, seconds, 16):
                down = pl.ds(pl.multiple_of(first * seconds + at, 16), 16)
                values = [(back[one, 0, down, across], back[one, 1, down, across]) for one in range(radix)]
                for one, (real, imag) in enumerate(butterfly(values, -1)):
                    out_ref[order[one * tiles + tile], first, 0, pl.ds(at, 16)] = real.astype(BF16)
                    out_ref[order[one * tiles + tile], first, 1, pl.ds(at, 16)] = imag.astype(BF16)

    loop(firsts, close)


def row_work(order, received, mask, tables):
    blocks, firsts, _, seconds, lanes = received.shape
    core, turns = tables
    radix, part = turns.shape[0], core.shape[0]
    rows = firsts * seconds

    def body(*refs):
        row_body(order, *refs)

    return pl.pallas_call(
        body,
        out_shape=jax.ShapeDtypeStruct(received.shape, BF16),
        in_specs=vmem(4),
        out_specs=vmem(1)[0],
        scratch_shapes=[
            pltpu.VMEM((radix, 2 * rows, part), BF16),
            pltpu.VMEM((2 * rows, part), BF16),
            pltpu.VMEM((radix, 2, rows, part), F32),
        ],
        compiler_params=params(),
        name="row_both",
    )(received, mask, core, turns)


def last_row_body(order, in_ref, core_ref, turn_ref, out_ref, mixed):
    blocks, firsts, _, seconds, lanes = in_ref.shape
    radix, _, part = mixed.shape
    row_mix(order, in_ref, turn_ref, mixed)

    def one(at):
        for tile in range(0, part, 256):
            real, imag = core_dot(mixed[at], core_ref, 1, tile)
            for within in range(0, 256, lanes):
                number = (tile + within) // lanes
                out_ref[number, 0, at] = real[:, within : within + lanes].astype(BF16)
                out_ref[number, 1, at] = imag[:, within : within + lanes].astype(BF16)

    loop(radix, one)


def last_row_work(order, received, tables):
    blocks, firsts, _, seconds, lanes = received.shape
    core, turns = tables
    radix, part = turns.shape[0], core.shape[0]
    rows = firsts * seconds

    def body(*refs):
        last_row_body(order, *refs)

    return pl.pallas_call(
        body,
        out_shape=jax.ShapeDtypeStruct((part // lanes, 2, radix, rows, lanes), BF16),
        in_specs=vmem(3),
        out_specs=vmem(1)[0],
        scratch_shapes=[pltpu.VMEM((radix, 2 * rows, part), BF16)],
        compiler_params=params(),
        name="row_last",
    )(received, core, turns)


def mask_body(in_ref, down_ref, across_ref, out_ref):
    groups, radix, rows, lanes = out_ref.shape
    turned = dot(down_ref[...], in_ref[...].astype(BF16)).astype(BF16)
    for tile in range(0, radix * lanes, 256):
        got = dot(turned, across_ref[:, tile : tile + 256]).astype(BF16)
        for within in range(0, 256, lanes):
            out_ref[:, (tile + within) // lanes] = got[:, within : within + lanes].reshape(groups, rows, lanes)


def mask_work(transmission, row_count, col_count, radix):
    height, width = transmission.shape
    down = regroup(height, RADIX).T
    across = regroup(width, radix)
    return pl.pallas_call(
        mask_body,
        out_shape=jax.ShapeDtypeStruct((col_count, radix, height // col_count, width // radix), BF16),
        in_specs=vmem(3),
        out_specs=vmem(1)[0],
        compiler_params=params(),
        name="mask_order",
    )(transmission, jnp.asarray(down), jnp.asarray(across))


def closing_body(in_ref, keep_ref, down_ref, across_ref, out_ref, turned):
    groups, _, radix, rows, lanes = in_ref.shape
    for number in range(2):
        for at in range(radix):
            got = dot(down_ref[...], in_ref[:, number, at].reshape(groups * rows, lanes))
            turned[:, pl.ds(at * lanes, lanes)] = got.astype(BF16)
        for tile in range(0, radix * lanes, 256):
            across = pl.ds(tile, 256)
            out_ref[number, :, across] = dot(turned[...], across_ref[:, across]) * keep_ref[:, across]


def closing_work(received, transmission):
    groups, _, radix, rows, lanes = received.shape
    height, width = transmission.shape
    down = regroup(height, RADIX)
    across = regroup(width, radix).T
    return pl.pallas_call(
        closing_body,
        out_shape=jax.ShapeDtypeStruct((2, height, width), F32),
        in_specs=vmem(4),
        out_specs=vmem(1)[0],
        scratch_shapes=[pltpu.VMEM((height, width), BF16)],
        compiler_params=params(),
        name="closing_order",
    )(received, transmission, jnp.asarray(down), jnp.asarray(across))


def exchange(value, axis):
    return lax.all_to_all(value, axis, split_axis=0, concat_axis=0, tiled=True)


def widen(value):
    short = -value.shape[-1] % LANES
    return jnp.pad(value, [(0, 0)] * (value.ndim - 1) + [(0, short)]) if short else value


def on_device(spectrum, diffraction, order_mask, phases, transmission, shifts):
    height, wide = spectrum.shape[1:]
    row_count, col_count = lax.axis_size("rows"), lax.axis_size("cols")
    devices = row_count * col_count
    full_rows, full_cols = height * row_count, wide * col_count
    width = wide // row_count
    part = LANES * col_count
    radix = full_cols // part
    forward, backward = column_tables(full_rows)
    column_all = (jnp.asarray(forward), jnp.asarray(backward))
    core, turns = row_tables(full_cols, part)
    row_all = (jnp.asarray(core), jnp.asarray(turns))

    current = exchange(spectrum.reshape(2, height, row_count, width).transpose(2, 0, 1, 3), "rows")
    mats = lax.all_gather(diffraction, "rows", axis=0)
    mask_all = lax.all_gather(order_mask, "rows", axis=0).reshape(-1)
    angles = phases.astype(jnp.float16).reshape(BOUNCES, height, row_count, width).transpose(2, 0, 1, 3)
    angles = exchange(angles, "rows").astype(F32).transpose(1, 0, 2, 3).reshape(BOUNCES, full_rows, width)
    kept = exchange(mask_work(transmission, row_count, col_count, radix), "cols")

    narrow = width < LANES
    tiles = full_cols // LANES
    if narrow:
        order = list(range(tiles))
    else:
        order = [(at % row_count) * col_count + at // row_count for at in range(tiles)]

    def to_rows(value):
        got = exchange(value[..., :width].reshape(devices, *value.shape[2:-1], width), ("rows", "cols"))
        if not narrow:
            return got
        joined = LANES // width
        got = got.reshape(row_count, col_count, *got.shape[1:]).swapaxes(0, 1).reshape(tiles, joined, *got.shape[1:])
        return jnp.moveaxis(got, 1, -2).reshape(tiles, *got.shape[2:-1], LANES)

    def to_columns(value):
        if narrow:
            joined = LANES // width
            value = jnp.moveaxis(value.reshape(*value.shape[:-1], joined, width), -2, 1)
            value = value.reshape(col_count, row_count, *value.shape[2:]).swapaxes(0, 1)
            value = value.reshape(devices, *value.shape[2:])
        got = exchange(value, ("rows", "cols"))
        return widen(got.reshape(row_count, col_count, *got.shape[1:]))

    current = widen(current)
    for bounce in range(BOUNCES):
        sent = column_work(
            bounce > 0,
            current,
            mats,
            mask_all,
            shifts[bounce : bounce + 1],
            widen(angles[bounce]),
            column_all,
            row_count,
            col_count,
        )
        received = to_rows(sent)
        if bounce < BOUNCES - 1:
            current = to_columns(row_work(order, received, kept, row_all))
    worked = exchange(last_row_work(order, received, row_all), "cols")
    return closing_work(worked, transmission)


def solution(mesh):
    placed = (
        P(None, "rows", "cols"),
        P(None, "rows", None, None, None),
        P("rows", None),
        P(None, "rows", "cols"),
        P("rows", "cols"),
        P(),
    )
    return jax.shard_map(
        on_device, mesh=mesh, in_specs=placed, out_specs=P(None, "rows", "cols"), check_vma=False
    )
```

time: 1200 us -> 405 us (0.34); the launches traced: 1180 us -> 401 us
  matrix products: 654 us -> 0 us
  local copies, waits for them, and re-layouts: 125 us -> 19.7 us
  Pallas kernels: 0 us -> 81.8 us
  waiting for transfers between devices: 123 us -> 50.6 us
  other arithmetic: 34 us -> 3 us
  starting transfers between devices: 27.6 us -> 15.1 us
    dot_general x48 -> x0, matrix products: 654 us -> none  [the longest x24 624 us: contract(): jnp.einsum(form_text, left_side, right_side, preferred_element_type=jnp.f...]
    pallas_call x0 -> x6, Pallas kernels: none -> 81.8 us  [the longest x2 46.8 us: column_work(): pl.pallas_call(body, out_shape=jax.ShapeDtypeStruct((row_count, col_count...]
    ppermute x4 -> x0, waiting for transfers between devices: 57.9 us -> none  [shifted(): lax.ppermute(value, axis, [(source, source + steps) for source in range(f...]
    slice x28 -> x2, local copies, waits for them, and re-layouts: 28.5 us -> 2.99 us  [the longest x1 2.33 us: on_device(): angles[bounce]]
    convert_element_type x3 -> x0, local copies, waits for them, and re-layouts: 25.1 us -> none  [the longest x1 17.8 us: on_device(): worked.astype(jnp.bfloat16)]
    another operation x5 -> x0, other arithmetic: 20.5 us -> none
    another operation x9 -> x0, local copies, waits for them, and re-layouts: 20.5 us -> none  [the longest x3 11.3 us: blocked_dft(): return jnp.stack([out_real, out_imag])]
    all_to_all x10 -> x0, local copies, waits for them, and re-layouts: 17.7 us -> none  [the longest x4 12 us: on_device(): lax.all_to_all(rows_space, ('rows', 'cols'), split_axis=2, concat_axis=1,...]
  transfers between devices with their start and end apart: 7 -> 4, of which waited for: 4 -> 2; matrix products, arithmetic and copies ran while one was open for 13% -> 6% of each run, Pallas kernels for 0% -> 7%
where the time goes in v1:
time: 405 us; the launch traced here: 401 us
  blocking collectives  218 us (54%)
  Pallas kernels  81.8 us (20%)
  waiting for transfers between devices  50.6 us (12%)
  local copies, waits for them, and re-layouts  19.7 us (5%)
  starting transfers between devices  15.1 us (4%)
  between operations  13.4 us (3%)
    all_to_all x4, blocking collectives, exchange(): return lax.all_to_all(value, axis, split_axis=0, concat_axis=0, tiled=True)  209 us
    all_to_all x3, waiting for transfers between devices, exchange(): return lax.all_to_all(value, axis, split_axis=0, concat_axis=0, tiled=True)  49.8 us
    pallas_call x2, Pallas kernels, column_work(): pl.pallas_call(body, out_shape=jax.ShapeDtypeStruct((row_count, col_count...  46.8 us
    all_to_all x3, starting transfers between devices, exchange(): return lax.all_to_all(value, axis, split_axis=0, concat_axis=0, tiled=True)  15.1 us
    pallas_call x1, Pallas kernels, row_work(): pl.pallas_call(body, out_shape=jax.ShapeDtypeStruct(received.shape, BF16)...  12.2 us
    pallas_call x1, Pallas kernels, closing_work(): pl.pallas_call(closing_body, out_shape=jax.ShapeDtypeStruct((2, height, w...  9.55 us
    unnamed x8, local copies, waits for them, and re-layouts  9.32 us
    all_gather x1, blocking collectives, on_device(): mask_all = lax.all_gather(order_mask, 'rows', axis=0).reshape(-1)  8.85 us
  transfers between devices with their start and end apart: 4, of which 2 were waited for; matrix products, arithmetic and copies ran while one was open for 6% of the time, Pallas kernels for 7%

profile of v1, /device:TPU:12, one launch (start us, length us, event | category | flops | bytes accessed | tf_op | source)
XLA Modules:
  0.0 401.2 jit_solution(9330097581394513008)
XLA Ops:
  6.5 0.0 all-gather.5.cloned.1.call-start
  6.5 0.7 all-gather.5.cloned.1.call-update
  7.3 5.4 %copy.23 = f32[2,512,1024]{1,2,0:T(8,128)} copy(f32[2,512,1024]{2,1,0:T(8,128)} %param.17) | data formatting | bytes 8388608 | tf_op args[3]
  12.6 2.7 convert_element_type.4
  15.3 2.8 copy.24
  18.2 4.2 %all-to-all-start.1 = ((f16[8,2,512,128]{3,2,1,0:T(8,128)(2,1)}), f16[8,2,512,128]{3,2,1,0:T(8,128)(2,1)S(1)}, u32[]{:S(2)}, u32[]{:S(2)}) async-start(f16[8,2,512,128]{3,2,1,0:T(8,128)(2,1)} %copy.24), calls=%async_computation.1 | async-start | bytes 4194304 | tf_op jit(solution)/shard_map/all_to_all | solution.py:432
  22.4 3.9 copy.21
  26.3 3.9 copy.22
  30.3 25.7 %all-to-all-done.1 = f16[8,2,512,128]{3,2,1,0:T(8,128)(2,1)S(1)} async-done(((f16[8,2,512,128]{3,2,1,0:T(8,128)(2,1)}), f16[8,2,512,128]{3,2,1,0:T(8,128)(2,1)S(1)}, u32[]{:S(2)}, u32[]{:S(2)}) %all-to-all-start.1) | async-done | bytes 2097184 | tf_op jit(solution)/shard_map/all_to_all | solution.py:432
  56.0 5.7 %all-to-all-start = ((bf16[8,2,512,128]{3,2,1,0:T(8,128)(2,1)}), bf16[8,2,512,128]{3,2,1,0:T(8,128)(2,1)}, u32[]{:S(2)}, u32[]{:S(2)}) async-start(bf16[8,2,512,128]{3,2,1,0:T(8,128)(2,1)} %bitcast.17), calls=%async_computation | async-start | bytes 4194304 | tf_op jit(solution)/shard_map/all_to_all | solution.py:432
  61.7 5.3 %mask_order.1 = bf16[4,8,128,128]{3,2,1,0:T(8,128)(2,1)} custom-call(f32[512,1024]{1,0:T(8,128)} %keep_ref.1, bf16[512,512]{1,0:T(8,128)(2,1)} %constant.20.clone.down_ref, bf16[1024,1024]{1,0:T(8,128)(2,1)} %constant.21.clone.across_ref), custom_call_target="tpu_custom_call" | custom-call | tf_op jit(solution)/shard_map/mask_order/pallas_call | solution.py:394
  67.0 0.0 copy-start.1
  67.0 0.0 copy-start.2
  67.0 24.1 %all-to-all-done.refs_0_ = bf16[8,2,512,128]{3,2,1,0:T(8,128)(2,1)} async-done(((bf16[8,2,512,128]{3,2,1,0:T(8,128)(2,1)}), bf16[8,2,512,128]{3,2,1,0:T(8,128)(2,1)}, u32[]{:S(2)}, u32[]{:S(2)}) %all-to-all-start) | async-done | bytes 2097184 | tf_op jit(solution)/shard_map/all_to_all | solution.py:432
  91.1 5.1 %all-to-all-start.3 = ((bf16[4,8,128,128]{3,2,1,0:T(8,128)(2,1)}), bf16[4,8,128,128]{3,2,1,0:T(8,128)(2,1)S(1)}, u32[]{:S(2)}, u32[]{:S(2)}) async-start(bf16[4,8,128,128]{3,2,1,0:T(8,128)(2,1)} %mask_order.1), calls=%async_computation.3 | async-start | bytes 2097152 | tf_op jit(solution)/shard_map/all_to_all | solution.py:432
  96.2 0.0 copy-done.1
  96.2 8.9 %all-gather.2 = s32[8,4,3]{2,1,0:T(4,128)S(1)} all-gather(s32[1,4,3]{2,1,0:T(4,128)S(1)} %bitcast.24), channel_id=3, replica_groups=mesh['rows'=8,'cols'=4] {'rows'}, dimensions={0}, use_global_device_ids=true | all-gather | bytes 432 | tf_op jit(solution)/shard_map/all_gather | solution.py:455
  105.1 0.6 reshape.24.refs_2_
  105.7 0.0 copy-done.2
  105.7 0.7 fusion.1
  106.4 0.3 convert_bitcast_fusion
  106.7 2.3 fusion
  109.0 0.0 all-gather.5.cloned.1.call-done
  109.0 21.3 %column_first.1 = bf16[8,4,4,2,32,128]{5,4,3,2,1,0:T(8,128)(2,1)} custom-call(bf16[8,2,512,128]{3,2,1,0:T(8,128)(2,1)} %all-to-all-done.refs_0_, bf16[8,2,4,3,128,128]{5,4,3,2,1,0:T(8,128)(2,1)} %bitcast.14, s32[96]{0:T(128)} %reshape.24.refs_2_, s32[1]{0:T(128)} %get-tuple-element.8.refs_3_, f32[4096,128]{1,0:T(8,128)} %bitcast.23, ...), custom_call_target="tpu_custom_call" | custom-call | tf_op jit(solution)/shard_map/column_first/pallas_call | solution.py:231
  130.3 0.0 all-to-all-done.3.refs_1_
  130.3 0.0 copy-start
  130.3 53.2 %all_to_all.35.refs_0_ = bf16[32,4,2,32,128]{4,3,2,1,0:T(8,128)(2,1)} all-to-all(bf16[32,4,2,32,128]{4,3,2,1,0:T(8,128)(2,1)} %bitcast.20), channel_id=1, replica_groups=mesh['rows'=8,'cols'=4] {'rows','cols'}, dimensions={0} | all-to-all | bytes 4194304 | tf_op jit(solution)/shard_map/all_to_all | solution.py:432
  183.5 0.0 copy-done
  183.5 12.2 %row_both.1 = bf16[32,4,2,32,128]{4,3,2,1,0:T(8,128)(2,1)} custom-call(bf16[32,4,2,32,128]{4,3,2,1,0:T(8,128)(2,1)} %all_to_all.35.refs_0_, bf16[4,8,128,128]{3,2,1,0:T(8,128)(2,1)} %copy-done, bf16[512,1024]{1,0:T(8,128)(2,1)} %constant.18.clone.refs_2_.refs_1_, f32[8,2,1,512]{3,2,1,0:T(1,128)} %constant.19.clone.refs_3_.refs_2_), custom_call_target="tpu_custom_call" | custom-call | tf_op jit(solution)/shard_map/row_both/pallas_call | solution.py:330
  195.7 52.1 %all_to_all.36 = bf16[32,4,2,32,128]{4,3,2,1,0:T(8,128)(2,1)} all-to-all(bf16[32,4,2,32,128]{4,3,2,1,0:T(8,128)(2,1)} %row_both.1), channel_id=1, replica_groups=mesh['rows'=8,'cols'=4] {'rows','cols'}, dimensions={0} | all-to-all | bytes 4194304 | tf_op jit(solution)/shard_map/all_to_all | solution.py:432
  247.8 25.6 %column_later.1 = bf16[8,4,4,2,32,128]{5,4,3,2,1,0:T(8,128)(2,1)} custom-call(bf16[8,4,4,2,32,128]{5,4,3,2,1,0:T(8,128)(2,1)} %bitcast.19, bf16[8,2,4,3,128,128]{5,4,3,2,1,0:T(8,128)(2,1)} %bitcast.15, s32[96]{0:T(128)} %reshape.24.refs_2_, s32[1]{0:T(128)} %get-tuple-element.7.refs_3_, f32[4096,128]{1,0:T(8,128)} %bitcast.22, ...), custom_call_target="tpu_custom_call" | custom-call | tf_op jit(solution)/shard_map/column_later/pallas_call | solution.py:231
  273.3 52.1 %all_to_all.37.refs_0_ = bf16[32,4,2,32,128]{4,3,2,1,0:T(8,128)(2,1)} all-to-all(bf16[32,4,2,32,128]{4,3,2,1,0:T(8,128)(2,1)} %bitcast.21), channel_id=1, replica_groups=mesh['rows'=8,'cols'=4] {'rows','cols'}, dimensions={0} | all-to-all | bytes 4194304 | tf_op jit(solution)/shard_map/all_to_all | solution.py:432
  325.4 8.0 %row_last.1 = bf16[4,2,8,128,128]{4,3,2,1,0:T(8,128)(2,1)} custom-call(bf16[32,4,2,32,128]{4,3,2,1,0:T(8,128)(2,1)} %all_to_all.37.refs_0_, bf16[512,1024]{1,0:T(8,128)(2,1)} %constant.18.clone.refs_2_.refs_1_, f32[8,2,1,512]{3,2,1,0:T(1,128)} %constant.19.clone.refs_3_.refs_2_), custom_call_target="tpu_custom_call" | custom-call | tf_op jit(solution)/shard_map/row_last/pallas_call | solution.py:370
  333.4 51.4 %all_to_all.38.in_ref = bf16[4,2,8,128,128]{4,3,2,1,0:T(8,128)(2,1)} all-to-all(bf16[4,2,8,128,128]{4,3,2,1,0:T(8,128)(2,1)} %row_last.1), channel_id=1, replica_groups=mesh['rows'=8,'cols'=4] {'cols'}, dimensions={0} | all-to-all | bytes 4194304 | tf_op jit(solution)/shard_map/all_to_all | solution.py:432
  384.8 9.5 %closing_order.1 = f32[2,512,1024]{2,1,0:T(8,128)} custom-call(bf16[4,2,8,128,128]{4,3,2,1,0:T(8,128)(2,1)} %all_to_all.38.in_ref, f32[512,1024]{1,0:T(8,128)} %keep_ref.1, bf16[512,512]{1,0:T(8,128)(2,1)} %constant.22.clone.down_ref, bf16[1024,1024]{1,0:T(8,128)(2,1)} %constant.23.clone.across_ref), custom_call_target="tpu_custom_call" | custom-call | tf_op jit(solution)/shard_map/closing_order/pallas_call | solution.py:420
Async XLA Ops:
  6.5 102.5 %all-gather.5.cloned.1.call-start = ((), (), s32[]{:S(2)}) async-start(), calls=%async_computation.7 | async-start | bytes 7077888 | tf_op jit(solution)/shard_map/all_gather | solution.py:454
  18.2 37.8 %all-to-all-start.1 = ((f16[8,2,512,128]{3,2,1,0:T(8,128)(2,1)}), f16[8,2,512,128]{3,2,1,0:T(8,128)(2,1)S(1)}, u32[]{:S(2)}, u32[]{:S(2)}) async-start(f16[8,2,512,128]{3,2,1,0:T(8,128)(2,1)} %copy.24), calls=%async_computation.1 | async-start | bytes 4194304 | tf_op jit(solution)/shard_map/all_to_all | solution.py:432
  56.0 35.1 %all-to-all-start = ((bf16[8,2,512,128]{3,2,1,0:T(8,128)(2,1)}), bf16[8,2,512,128]{3,2,1,0:T(8,128)(2,1)}, u32[]{:S(2)}, u32[]{:S(2)}) async-start(bf16[8,2,512,128]{3,2,1,0:T(8,128)(2,1)} %bitcast.17), calls=%async_computation | async-start | bytes 4194304 | tf_op jit(solution)/shard_map/all_to_all | solution.py:432
  67.0 29.3 %copy-start.1 = (s32[4,3]{1,0:T(4,128)S(1)}, s32[4,3]{1,0:T(4,128)}, u32[]{:S(2)}) copy-start(s32[4,3]{1,0:T(4,128)} %param.16) | copy-start | bytes 148
  67.0 38.7 %copy-start.2 = (s32[2]{0:T(128)S(1)}, s32[2]{0:T(128)}, u32[]{:S(2)}) copy-start(s32[2]{0:T(128)} %param.19) | copy-start | bytes 28
  91.1 39.2 %all-to-all-start.3 = ((bf16[4,8,128,128]{3,2,1,0:T(8,128)(2,1)}), bf16[4,8,128,128]{3,2,1,0:T(8,128)(2,1)S(1)}, u32[]{:S(2)}, u32[]{:S(2)}) async-start(bf16[4,8,128,128]{3,2,1,0:T(8,128)(2,1)} %mask_order.1), calls=%async_computation.3 | async-start | bytes 2097152 | tf_op jit(solution)/shard_map/all_to_all | solution.py:432
  130.3 53.2 %copy-start = (bf16[4,8,128,128]{3,2,1,0:T(8,128)(2,1)}, bf16[4,8,128,128]{3,2,1,0:T(8,128)(2,1)S(1)}, u32[]{:S(2)}) copy-start(bf16[4,8,128,128]{3,2,1,0:T(8,128)(2,1)S(1)} %all-to-all-done.3.refs_1_) | copy-start | bytes 3145732
Sparse Core Ops, SparseCore 0:
  9.2 66.2 all-gather.4

commit v2 on v1

v2 whole, which is shorter than its diff:
```python
import math

import jax
import jax.numpy as jnp
import ml_dtypes
import numpy as np
from jax import lax
from jax.experimental import pallas as pl
from jax.experimental.pallas import tpu as pltpu
from jax.sharding import PartitionSpec as P

BLOCK = 128
LANES = 128
RADIX = 16
BOUNCES = 2
GROUP = 4
ANGLE_STEPS = 10430.0
VMEM_LIMIT = 56 * 1024 * 1024
BF16 = jnp.bfloat16
F32 = jnp.float32


def params():
    return pltpu.CompilerParams(vmem_limit_bytes=VMEM_LIMIT)


def vmem(count):
    return [pl.BlockSpec(memory_space=pltpu.VMEM) for _ in range(count)]


def column_tables(extent):
    part = extent // RADIX
    first = np.arange(RADIX)[:, None, None]
    second = np.arange(part)[None, :, None]
    inner = np.arange(part)[None, None, :]
    angle = ((first + RADIX * second) * inner % extent) * (2.0 * np.pi / extent)
    scale = 1.0 / math.sqrt(extent)
    real, imag = np.cos(angle) * scale, np.sin(angle) * scale
    forward = np.concatenate([real, imag], axis=1)
    backward = np.concatenate([real.transpose(0, 2, 1), imag.transpose(0, 2, 1)], axis=1)
    return forward.astype(ml_dtypes.bfloat16), backward.astype(ml_dtypes.bfloat16)


def row_tables(extent, part):
    radix = extent // part
    inner = np.arange(part)
    angle = (inner[:, None] * inner[None, :] % part) * (2.0 * np.pi / part)
    scale = 1.0 / math.sqrt(extent)
    core = np.stack([np.cos(angle) * scale, np.sin(angle) * scale], axis=1)
    core = core.reshape(part, 2, part // LANES, LANES).transpose(2, 0, 1, 3).reshape(part // LANES, part, 2 * LANES)
    turn = (np.arange(radix)[:, None] * inner[None, :]) * (2.0 * np.pi / extent)
    turns = np.stack([np.cos(turn), np.sin(turn)], axis=1)[:, :, None, :]
    return core.astype(ml_dtypes.bfloat16), turns.astype(np.float32)


def regroup(count, fast):
    natural = np.arange(count)
    grouped = (natural % fast) * (count // fast) + natural // fast
    matrix = np.zeros((count, count), np.float32)
    matrix[natural, grouped] = 1.0
    return matrix.astype(ml_dtypes.bfloat16)


def half_series():
    top = (np.pi / 2) ** 2
    squares = (np.polynomial.chebyshev.chebpts1(200) + 1) * (top / 2)
    angles = np.sqrt(squares)

    def fit(values):
        series = np.polynomial.chebyshev.Chebyshev.fit(squares, values, 4, domain=[0, top])
        return [float(c) for c in series.convert(kind=np.polynomial.Polynomial).coef]

    return fit(np.sin(angles) / angles), fit(np.cos(angles))


SINE_SERIES, COSINE_SERIES = half_series()


def cos_sin(angle):
    half = angle * 0.5
    square = half * half

    def series(coefs):
        total = square * coefs[-1] + coefs[-2]
        for coef in coefs[-3::-1]:
            total = total * square + coef
        return total

    twice_sine, cosine = angle * series(SINE_SERIES), series(COSINE_SERIES)
    return 1.0 - twice_sine * twice_sine * 0.5, twice_sine * cosine


def butterfly(values, sign):
    count = len(values)
    if count == 1:
        return values
    even, odd = butterfly(values[0::2], sign), butterfly(values[1::2], sign)
    low, high = [], []
    for at in range(count // 2):
        real, imag = odd[at]
        if at == 0:
            turned = real, imag
        elif 4 * at == count:
            turned = (-imag, real) if sign > 0 else (imag, -real)
        elif 8 * at == count:
            half = math.sqrt(0.5)
            turned = (
                ((real - imag) * half, (real + imag) * half)
                if sign > 0
                else ((real + imag) * half, (imag - real) * half)
            )
        elif 8 * at == 3 * count:
            half = math.sqrt(0.5)
            turned = (
                ((real + imag) * -half, (real - imag) * half)
                if sign > 0
                else ((imag - real) * half, (real + imag) * -half)
            )
        else:
            cosine = math.cos(2 * math.pi * at / count)
            sine = sign * math.sin(2 * math.pi * at / count)
            turned = real * cosine - imag * sine, real * sine + imag * cosine
        low.append((even[at][0] + turned[0], even[at][1] + turned[1]))
        high.append((even[at][0] - turned[0], even[at][1] - turned[1]))
    return low + high


def dot(left, right):
    return jnp.dot(left, right, preferred_element_type=F32)


def loop(count, body, unroll=1):
    def step(at, carry):
        body(at)
        return carry

    lax.fori_loop(0, count, step, 0, unroll=min(unroll, count))


def aligned(start, size):
    return pl.ds(pl.multiple_of(start, size), size)


def column_body(later, peers, *refs):
    place_ref, shift_ref = refs[:2]
    current, refs = (refs[2:3], refs[3:]) if later else (refs[2 : 2 + peers], refs[2 + peers :])
    mats, refs = refs[: 2 * peers], refs[2 * peers :]
    angles, refs = refs[:peers], refs[peers:]
    tables, refs = refs[: 1 + later], refs[1 + later :]
    out_ref, padded, wave, mixed, held_mats, held_angles = refs[:6]
    held_tables, sems = refs[6:-1], refs[-1]
    rows_at, cols_at, firsts, _, seconds, width = out_ref.shape
    extent = wave.shape[1]
    part = extent // RADIX
    height = extent // peers
    half_blocks = height // BLOCK // 2

    copies = []

    def fetch(source, target):
        copy = pltpu.make_async_copy(source, target, sems.at[len(copies)])
        copy.start()
        copies.append(copy)
        return copy

    table_copies = [fetch(tables[-1], held_tables[-1])] if later else []
    mat_copies, angle_copies = [], []
    for at in range(peers):
        mat_copies.append([fetch(mats[2 * at + one], held_mats.at[at, one]) for one in range(2)])
        angle_copies.append(fetch(angles[at], held_angles.at[at]))
    table_copies.append(fetch(tables[0], held_tables[0]))

    padded[:, pl.ds(0, height)] = jnp.zeros((2, height, width), F32)
    padded[:, pl.ds(height + extent, height)] = jnp.zeros((2, height, width), F32)

    if later:
        cur_ref = current[0]
        table_copies[0].wait()

        def unfold(at):
            group, first = at // firsts, at % firsts
            real = cur_ref[:, group, first, 0].reshape(part, width)
            imag = cur_ref[:, group, first, 1].reshape(part, width)
            got = dot(held_tables[-1][at], jnp.concatenate([real, imag], axis=1))
            rows = aligned(at * part, part)
            wave[0, rows] = got[:part, :width] + got[part:, width:]
            wave[1, rows] = got[:part, width:] - got[part:, :width]

        loop(RADIX, unfold, 8)

        def gather(at):
            values = [
                (wave[0, aligned(one * part + at * 8, 8)], wave[1, aligned(one * part + at * 8, 8)])
                for one in range(RADIX)
            ]
            for one, (real, imag) in enumerate(butterfly(values, -1)):
                rows = aligned(height + one * part + at * 8, 8)
                padded[0, rows] = real
                padded[1, rows] = imag

        loop(part // 8, gather, 2)
    else:
        for at in range(peers):
            rows = aligned(height + (place_ref[0] ^ at) * height, height)
            padded[0, rows] = current[at][0].astype(F32)
            padded[1, rows] = current[at][1].astype(F32)

    shift = shift_ref[0]
    for at in range(peers):
        start = (place_ref[0] ^ at) * height
        for one in range(2):
            mat_copies[at][one].wait()
        angle_copies[at].wait()

        def diffract(block, at=at, start=start):
            within = block * BLOCK
            rights = []
            for order in range(3):
                rows = pl.ds(height + start + within + (order - 1) * shift, BLOCK)
                rights.append(jnp.concatenate([padded[0, rows], padded[1, rows]], axis=1).astype(BF16))
            left = held_mats[at, block // half_blocks, block % half_blocks]
            got = dot(left, jnp.concatenate(rights, axis=0))
            real = got[:BLOCK, :width] - got[BLOCK:, width:]
            imag = got[:BLOCK, width:] + got[BLOCK:, :width]
            cosine, sine = cos_sin(held_angles[at, aligned(within, BLOCK)].astype(F32) * (1.0 / ANGLE_STEPS))
            rows = aligned(start + within, BLOCK)
            wave[0, rows] = real * cosine - imag * sine
            wave[1, rows] = real * sine + imag * cosine

        loop(2 * half_blocks, diffract, 4)

    def mix(at):
        parts = []
        for half in range(2):
            down = at * 16 + half * 8
            values = [
                (wave[0, aligned(one * part + down, 8)], wave[1, aligned(one * part + down, 8)])
                for one in range(RADIX)
            ]
            parts.append(butterfly(values, 1))
        for one in range(RADIX):
            real, imag = (jnp.concatenate([parts[0][one][c], parts[1][one][c]], axis=0) for c in range(2))
            mixed[one, aligned(at * 16, 16)] = jnp.concatenate([real, imag], axis=1).astype(BF16)

    loop(part // 16, mix)
    table_copies[-1].wait()

    def fold(at):
        group, first = at // firsts, at % firsts
        got = dot(held_tables[0][at], mixed[at])
        real = (got[:part, :width] - got[part:, width:]).astype(BF16)
        imag = (got[:part, width:] + got[part:, :width]).astype(BF16)
        out_ref[:, group, first, 0] = real.reshape(rows_at, seconds, width)
        out_ref[:, group, first, 1] = imag.reshape(rows_at, seconds, width)

    loop(RADIX, fold, 8)


def column_work(later, place, shift, current, mats, angles, tables, col_count):
    peers = len(angles)
    height, width = angles[0].shape
    extent = height * peers
    part = extent // RADIX

    def body(*refs):
        column_body(later, peers, *refs)

    currents = [current] if later else current
    tables = tables if later else tables[:1]
    mats = [one for pair in mats for one in pair]
    smem, anywhere = pl.BlockSpec(memory_space=pltpu.SMEM), pl.BlockSpec(memory_space=pl.ANY)
    return pl.pallas_call(
        body,
        out_shape=jax.ShapeDtypeStruct((peers, col_count, RADIX // col_count, 2, part // peers, width), BF16),
        in_specs=[smem, smem] + vmem(len(currents)) + [anywhere] * (len(mats) + peers + len(tables)),
        out_specs=vmem(1)[0],
        scratch_shapes=[
            pltpu.VMEM((2, extent + 2 * height, width), F32),
            pltpu.VMEM((2, extent, width), F32),
            pltpu.VMEM((RADIX, part, 2 * width), BF16),
            pltpu.VMEM((peers, 2, *mats[0].shape), BF16),
            pltpu.VMEM((peers, height, width), angles[0].dtype),
            *[pltpu.VMEM(table.shape, BF16) for table in tables],
            pltpu.SemaphoreType.DMA((len(mats) + peers + len(tables),)),
        ],
        compiler_params=params(),
        name="column_later" if later else "column_first",
    )(place, shift, *currents, *mats, *angles, *tables)


def row_mix(order, in_ref, turn_ref, mixed):
    blocks, firsts, _, seconds, lanes = in_ref.shape
    radix, _, _, part = mixed.shape
    tiles = part // lanes

    def one_first(first):
        for tile in range(tiles):
            across = pl.ds(tile * lanes, lanes)
            for at in range(0, seconds, 16):
                values = [
                    (
                        in_ref[order[one * tiles + tile], first, 0, pl.ds(at, 16)].astype(F32),
                        in_ref[order[one * tiles + tile], first, 1, pl.ds(at, 16)].astype(F32),
                    )
                    for one in range(radix)
                ]
                for one, (real, imag) in enumerate(butterfly(values, 1)):
                    cosine, sine = turn_ref[one, 0, :, across], turn_ref[one, 1, :, across]
                    down = pl.multiple_of(first * seconds + at, 16)
                    mixed[one, 0, pl.ds(down, 16), across] = (real * cosine - imag * sine).astype(BF16)
                    mixed[one, 1, pl.ds(down, 16), across] = (real * sine + imag * cosine).astype(BF16)

    loop(firsts, one_first, 4)


def core_dot(left, tile_ref, sign):
    count, _, rows, depth = left.shape
    lanes = tile_ref.shape[1] // 2
    got = dot(left.reshape(count * 2 * rows, depth), tile_ref).reshape(count, 2, rows, 2 * lanes)
    first, second = got[:, 0], got[:, 1]
    if sign > 0:
        return first[..., :lanes] - second[..., lanes:], second[..., :lanes] + first[..., lanes:]
    return first[..., :lanes] + second[..., lanes:], second[..., :lanes] - first[..., lanes:]


def row_body(order, in_ref, mask_ref, core_ref, turn_ref, out_ref, mixed, passed, back):
    blocks, firsts, _, seconds, lanes = in_ref.shape
    radix, _, _, part = mixed.shape
    tiles = part // lanes
    rows = firsts * seconds
    row_mix(order, in_ref, turn_ref, mixed)
    at_once = min(GROUP, radix)

    for group in range(0, radix, at_once):
        these = pl.ds(group, at_once)

        def forward(tile, these=these):
            real, imag = core_dot(mixed[these], core_ref[tile], 1)
            kept = mask_ref[tile, these].astype(F32)
            across = aligned(tile * lanes, lanes)
            passed[these, 0, :, across] = (real * kept).astype(BF16)
            passed[these, 1, :, across] = (imag * kept).astype(BF16)

        loop(tiles, forward, tiles)

        def backward(tile, these=these):
            real, imag = core_dot(passed[these], core_ref[tile], -1)
            across = aligned(tile * lanes, lanes)
            cosine, sine = turn_ref[these, 0, :, across], turn_ref[these, 1, :, across]
            back[these, 0, :, across] = real * cosine + imag * sine
            back[these, 1, :, across] = imag * cosine - real * sine

        loop(tiles, backward, tiles)

    def close(first):
        for tile in range(tiles):
            across = pl.ds(tile * lanes, lanes)
            for at in range(0, seconds, 16):
                down = aligned(first * seconds + at, 16)
                values = [(back[one, 0, down, across], back[one, 1, down, across]) for one in range(radix)]
                for one, (real, imag) in enumerate(butterfly(values, -1)):
                    out_ref[order[one * tiles + tile], first, 0, pl.ds(at, 16)] = real.astype(BF16)
                    out_ref[order[one * tiles + tile], first, 1, pl.ds(at, 16)] = imag.astype(BF16)

    loop(firsts, close, 2)


def row_work(order, received, mask, tables):
    blocks, firsts, _, seconds, lanes = received.shape
    core, turns = tables
    radix, part = turns.shape[0], core.shape[1]
    rows = firsts * seconds

    def body(*refs):
        row_body(order, *refs)

    return pl.pallas_call(
        body,
        out_shape=jax.ShapeDtypeStruct(received.shape, BF16),
        in_specs=vmem(4),
        out_specs=vmem(1)[0],
        scratch_shapes=[
            pltpu.VMEM((radix, 2, rows, part), BF16),
            pltpu.VMEM((radix, 2, rows, part), BF16),
            pltpu.VMEM((radix, 2, rows, part), F32),
        ],
        compiler_params=params(),
        name="row_both",
    )(received, mask, core, turns)


def last_row_body(order, place_ref, in_ref, core_ref, turn_ref, *refs):
    mixed = refs[-1]
    radix = mixed.shape[0]
    at_once = min(GROUP, radix)
    row_mix(order, in_ref, turn_ref, mixed)
    for group in range(0, radix, at_once):
        these = pl.ds(group, at_once)
        for distance, out_ref in enumerate(refs[:-1]):
            real, imag = core_dot(mixed[these], core_ref[place_ref[0] ^ distance], 1)
            out_ref[0, these] = real.astype(BF16)
            out_ref[1, these] = imag.astype(BF16)


def last_row_work(order, place, received, tables, number, chunks):
    blocks, firsts, _, seconds, lanes = received.shape
    core, turns = tables
    radix, part = turns.shape[0], core.shape[1]
    seconds //= chunks
    rows = firsts * seconds

    def body(*refs):
        last_row_body(order, *refs)

    def whole(array):
        return pl.BlockSpec(array.shape, lambda i: (0,) * array.ndim)

    given = pl.BlockSpec((blocks, firsts, 2, seconds, lanes), lambda i: (0, 0, 0, number, 0))
    sent = jax.ShapeDtypeStruct((2, radix, rows, lanes), BF16)
    return pl.pallas_call(
        body,
        grid=(1,),
        out_shape=[sent] * (part // lanes),
        in_specs=[pl.BlockSpec(memory_space=pltpu.SMEM), given, whole(core), whole(turns)],
        out_specs=[whole(sent)] * (part // lanes),
        scratch_shapes=[pltpu.VMEM((radix, 2, rows, part), BF16)],
        compiler_params=params(),
        cost_estimate=pl.CostEstimate(flops=8 * rows * part * part * radix, bytes_accessed=2**22, transcendentals=0),
        name="row_last",
    )(place, received, core, turns)


def mask_body(in_ref, down_ref, across_ref, out_ref):
    groups, radix, rows, lanes = out_ref.shape
    turned = dot(down_ref[...], in_ref[...].astype(BF16)).astype(BF16)
    for tile in range(0, radix * lanes, 256):
        got = dot(turned, across_ref[:, tile : tile + 256]).astype(BF16)
        for within in range(0, 256, lanes):
            out_ref[:, (tile + within) // lanes] = got[:, within : within + lanes].reshape(groups, rows, lanes)


def mask_work(transmission, row_count, col_count, radix):
    height, width = transmission.shape
    down = regroup(height, RADIX).T
    across = regroup(width, radix)
    return pl.pallas_call(
        mask_body,
        out_shape=jax.ShapeDtypeStruct((col_count, radix, height // col_count, width // radix), BF16),
        in_specs=vmem(3),
        out_specs=vmem(1)[0],
        compiler_params=params(),
        name="mask_order",
    )(transmission, jnp.asarray(down), jnp.asarray(across))


def closing_body(groups, place_ref, *refs):
    given, (keep_ref, down_ref, across_ref), (out_ref, joined, turned) = refs[:groups], refs[groups : groups + 3], refs[-3:]
    _, radix, rows, lanes = given[0].shape
    for distance in range(groups):
        down = aligned((place_ref[0] ^ distance) * rows, rows)
        for number in range(2):
            for at in range(radix):
                joined[number, down, pl.ds(at * lanes, lanes)] = given[distance][number, at]
    for number in range(2):
        turned[number] = dot(down_ref[...], joined[number]).astype(BF16)
        for tile in range(0, radix * lanes, 256):
            across = pl.ds(tile, 256)
            out_ref[number, :, across] = dot(turned[number], across_ref[:, across]) * keep_ref[:, across]


def closing_work(place, received, transmission, earlier, number, chunks):
    groups = len(received)
    _, radix, rows, lanes = received[0].shape
    height, width = transmission.shape
    height //= chunks
    down = jnp.asarray(regroup(height, RADIX))
    across = jnp.asarray(regroup(width, radix).T)

    def body(*refs):
        closing_body(groups, *refs[: groups + 4], *refs[-3:])

    def whole(array):
        return pl.BlockSpec(array.shape, lambda i: (0,) * array.ndim)

    in_specs = [pl.BlockSpec(memory_space=pltpu.SMEM)] + [whole(one) for one in received]
    in_specs += [pl.BlockSpec((height, width), lambda i: (number, 0)), whole(down), whole(across)]
    arguments = [place, *received, transmission, down, across]
    aliases = {}
    if earlier is not None:
        aliases = {len(arguments): 0}
        in_specs.append(pl.BlockSpec(memory_space=pl.ANY))
        arguments.append(earlier)
    return pl.pallas_call(
        body,
        grid=(1,),
        out_shape=jax.ShapeDtypeStruct((2, height * chunks, width), F32),
        in_specs=in_specs,
        out_specs=pl.BlockSpec((2, height, width), lambda i: (0, number, 0)),
        scratch_shapes=[pltpu.VMEM((2, height, width), BF16), pltpu.VMEM((2, height, width), BF16)],
        input_output_aliases=aliases,
        compiler_params=params(),
        cost_estimate=pl.CostEstimate(flops=4 * height * width * width, bytes_accessed=2**22, transcendentals=0),
        name="closing_order",
    )(*arguments)


def exchange(value, axis):
    return lax.all_to_all(value, axis, split_axis=0, concat_axis=0, tiled=True)


def swap(value, axis, distance):
    if distance == 0:
        return value
    return lax.ppermute(value, axis, [(at, at ^ distance) for at in range(lax.axis_size(axis))])


def widen(value):
    short = -value.shape[-1] % LANES
    return jnp.pad(value, [(0, 0)] * (value.ndim - 1) + [(0, short)]) if short else value


def after(value, earlier):
    return lax.optimization_barrier((value, earlier))[0]


def gather_mats(mats):
    peers = lax.axis_size("rows")
    halves = mats[: mats.shape[0] // 2], mats[mats.shape[0] // 2 :]
    if peers != 8:
        result = [[swap(half, "rows", distance) for half in halves] for distance in range(peers)]
        return result, result[1]
    by_x = [swap(half, "rows", 2) for half in halves]
    by_y = [swap(half, "rows", 4) for half in halves]
    across = [swap(by_x[0], "rows", 4), swap(by_y[1], "rows", 2)]
    result = []
    for pair in (halves, by_x, by_y, across):
        result += [list(pair), [swap(half, "rows", 1) for half in pair]]
    return result, (by_x[0], by_y[1])


def on_device(spectrum, diffraction, order_mask, phases, transmission, shifts):
    height, wide = spectrum.shape[1:]
    row_count, col_count = lax.axis_size("rows"), lax.axis_size("cols")
    devices = row_count * col_count
    full_rows, full_cols = height * row_count, wide * col_count
    width = wide // row_count
    part = LANES * col_count
    radix = full_cols // part
    forward, backward = column_tables(full_rows)
    column_all = (jnp.asarray(forward), jnp.asarray(backward))
    core, turns = row_tables(full_cols, part)
    row_all = (jnp.asarray(core), jnp.asarray(turns))

    along, above = lax.axis_index("rows"), lax.axis_index("cols")
    place_rows, place_cols = (at.astype(jnp.int32).reshape(1) for at in (along, above))

    def spread(value):
        return [
            widen(swap(lax.dynamic_slice_in_dim(value, (along ^ distance) * width, width, value.ndim - 1), "rows", distance))
            for distance in range(row_count)
        ]

    masked = diffraction * order_mask.astype(BF16)[None, :, :, None, None]
    blocks = height // BLOCK
    masked = masked.transpose(1, 0, 3, 2, 4).reshape(blocks, 2 * BLOCK, 3 * BLOCK)
    mats, first_mats = gather_mats(masked)
    current = spread(after(spectrum, masked))
    codes = jnp.round(phases * ANGLE_STEPS).astype(jnp.int16)
    angles = [spread(after(codes[0], first_mats)), spread(codes[1])]
    kept = exchange(mask_work(transmission, row_count, col_count, radix), "cols")

    narrow = width < LANES
    tiles = full_cols // LANES
    if narrow:
        order = list(range(tiles))
    else:
        order = [(at % row_count) * col_count + at // row_count for at in range(tiles)]

    def to_rows(value):
        got = exchange(value[..., :width].reshape(devices, *value.shape[2:-1], width), ("rows", "cols"))
        if not narrow:
            return got
        joined = LANES // width
        got = got.reshape(row_count, col_count, *got.shape[1:]).swapaxes(0, 1).reshape(tiles, joined, *got.shape[1:])
        return jnp.moveaxis(got, 1, -2).reshape(tiles, *got.shape[2:-1], LANES)

    def to_columns(value):
        if narrow:
            joined = LANES // width
            value = jnp.moveaxis(value.reshape(*value.shape[:-1], joined, width), -2, 1)
            value = value.reshape(col_count, row_count, *value.shape[2:]).swapaxes(0, 1)
            value = value.reshape(devices, *value.shape[2:])
        got = exchange(value, ("rows", "cols"))
        return widen(got.reshape(row_count, col_count, *got.shape[1:]))

    for bounce in range(BOUNCES):
        sent = column_work(
            bounce > 0, place_rows, shifts[bounce : bounce + 1], current, mats, angles[bounce], column_all, col_count
        )
        received = to_rows(sent)
        if bounce < BOUNCES - 1:
            current = to_columns(row_work(order, received, kept, row_all))
    chunks = 2 if received.shape[3] % 32 == 0 else 1
    worked = [last_row_work(order, place_cols, received, row_all, number, chunks) for number in range(chunks)]
    worked = [[swap(one, "cols", distance) for distance, one in enumerate(chunk)] for chunk in worked]
    outgoing = None
    for number in range(chunks):
        outgoing = closing_work(place_cols, worked[number], transmission, outgoing, number, chunks)
    return outgoing


def solution(mesh):
    placed = (
        P(None, "rows", "cols"),
        P(None, "rows", None, None, None),
        P("rows", None),
        P(None, "rows", "cols"),
        P("rows", "cols"),
        P(),
    )
    return jax.shard_map(
        on_device, mesh=mesh, in_specs=placed, out_specs=P(None, "rows", "cols"), check_vma=False
    )
```

time: 405 us -> 341 us (0.84)
  blocking collectives: 218 us -> 52.7 us
  waiting for transfers between devices: 50.6 us -> 164 us
  starting transfers between devices: 15.1 us -> 46.1 us
  Pallas kernels: 81.8 us -> 60.3 us
  between operations: 13.4 us -> 0.42 us
  local copies, waits for them, and re-layouts: 19.7 us -> 13.8 us
    all_to_all x4 -> x1, blocking collectives: 209 us -> 52.7 us  [exchange(): return lax.all_to_all(value, axis, split_axis=0, concat_axis=0, tiled=True)]
    ppermute x0 -> x41, waiting for transfers between devices: none -> 99.3 us  [swap(): lax.ppermute(value, axis, [(at, at ^ distance) for at in range(lax.axis_s...]
    ppermute x0 -> x41, starting transfers between devices: none -> 33.1 us  [swap(): lax.ppermute(value, axis, [(at, at ^ distance) for at in range(lax.axis_s...]
    pallas_call x4 -> x6, Pallas kernels: 64.4 us -> 45.5 us  [the longest x2 26.9 us: column_work(): pl.pallas_call(body, out_shape=jax.ShapeDtypeStruct((peers, col_count, RA...]
    all_to_all x3, waiting for transfers between devices: 49.8 us -> 64.6 us  [exchange(): return lax.all_to_all(value, axis, split_axis=0, concat_axis=0, tiled=True)]
    all_gather x1 -> x0, blocking collectives: 8.85 us -> none  [on_device(): mask_all = lax.all_gather(order_mask, 'rows', axis=0).reshape(-1)]
    dynamic_slice x0 -> x3, local copies, waits for them, and re-layouts: none -> 4.68 us  [spread(): lax.dynamic_slice_in_dim(value, (along ^ distance) * width, width, value....]
    reshape x2 -> x0, local copies, waits for them, and re-layouts: 4.54 us -> none  [the longest x1 3.92 us: on_device(): spectrum.reshape(2, height, row_count, width).transpose(2, 0, 1, 3)]
  transfers between devices with their start and end apart: 4 -> 44, of which waited for: 2 -> 22; matrix products, arithmetic and copies ran while one was open for 6% -> 2% of each run, Pallas kernels for 7% -> 8%
where the time goes in v2:
time: 341 us; the launch traced here: 340 us
  waiting for transfers between devices  164 us (48%)
  Pallas kernels  60.3 us (18%)
  blocking collectives  52.7 us (15%)
  starting transfers between devices  46.1 us (14%)
  local copies, waits for them, and re-layouts  13.8 us (4%)
    ppermute x41, waiting for transfers between devices, swap(): lax.ppermute(value, axis, [(at, at ^ distance) for at in range(lax.axis_s...  99.3 us
    all_to_all x3, waiting for transfers between devices, exchange(): return lax.all_to_all(value, axis, split_axis=0, concat_axis=0, tiled=True)  64.6 us
    all_to_all x1, blocking collectives, exchange(): return lax.all_to_all(value, axis, split_axis=0, concat_axis=0, tiled=True)  52.7 us
    ppermute x41, starting transfers between devices, swap(): lax.ppermute(value, axis, [(at, at ^ distance) for at in range(lax.axis_s...  33.1 us
    pallas_call x2, Pallas kernels, column_work(): pl.pallas_call(body, out_shape=jax.ShapeDtypeStruct((peers, col_count, RA...  26.9 us
    all_to_all x3, starting transfers between devices, exchange(): return lax.all_to_all(value, axis, split_axis=0, concat_axis=0, tiled=True)  13.1 us
    pallas_call x2, Pallas kernels, closing_work(): pl.pallas_call(body, grid=(1,), out_shape=jax.ShapeDtypeStruct((2, height...  10.7 us
    pallas_call x1, Pallas kernels, row_work(): pl.pallas_call(body, out_shape=jax.ShapeDtypeStruct(received.shape, BF16)...  9.62 us
  transfers between devices with their start and end apart: 44, of which 22 were waited for; matrix products, arithmetic and copies ran while one was open for 2% of the time, Pallas kernels for 8%

profile of v2, /device:TPU:12, one launch (start us, length us, event | category | flops | bytes accessed | tf_op | source)
XLA Modules:
  0.0 340.3 jit_solution(15630528302659768917)
XLA Ops:
  0.0 2.8 constant_dynamic-slice_fusion.8
  2.8 1.5 collective-permute-start.1
  5.6 1.6 collective-permute-start.9
  7.5 1.1 reshape.33.refs_11_.refs_4_
  9.1 5.2 %mask_order.1 = bf16[4,8,128,128]{3,2,1,0:T(8,128)(2,1)} custom-call(f32[512,1024]{1,0:T(8,128)} %refs_5_.3, bf16[512,512]{1,0:T(8,128)(2,1)} %constant.59.clone.down_ref, bf16[1024,1024]{1,0:T(8,128)(2,1)} %constant.60.clone.across_ref), custom_call_target="tpu_custom_call" | custom-call | tf_op jit(solution)/shard_map/mask_order/pallas_call | solution.py:446
  14.2 5.3 %all-to-all-start.1 = ((bf16[4,8,128,128]{3,2,1,0:T(8,128)(2,1)}), bf16[4,8,128,128]{3,2,1,0:T(8,128)(2,1)S(1)}, u32[]{:S(2)}, u32[]{:S(2)}) async-start(bf16[4,8,128,128]{3,2,1,0:T(8,128)(2,1)} %mask_order.1), calls=%async_computation.1 | async-start | bytes 2097152 | tf_op jit(solution)/shard_map/all_to_all | solution.py:508
  19.6 1.5 collective-permute-start.3
  21.7 2.9 round-nearest-even_convert_fusion
  24.6 10.1 %collective-permute-done.3.refs_6_ = bf16[2,512,128]{2,1,0:T(8,128)(2,1)S(1)} collective-permute-done((bf16[2,512,128]{2,1,0:T(8,128)(2,1)}, bf16[2,512,128]{2,1,0:T(8,128)(2,1)S(1)}, u32[]{:S(2)}, u32[]{:S(2)}) %collective-permute-start.3) | collective-permute-done | bytes 262176 | tf_op jit(solution)/shard_map/ppermute | solution.py:514
  34.6 2.8 collective-permute-done.4.refs_7_
  37.5 1.1 collective-permute-start.8
  39.1 1.6 collective-permute-start.13
  42.2 1.0 constant_dynamic-slice_fusion
  43.1 12.4 %collective-permute-done.6.refs_9_ = bf16[2,512,128]{2,1,0:T(8,128)(2,1)S(1)} collective-permute-done((bf16[2,512,128]{2,1,0:T(8,128)(2,1)}, bf16[2,512,128]{2,1,0:T(8,128)(2,1)S(1)}, u32[]{:S(2)}, u32[]{:S(2)}) %collective-permute-start.6) | collective-permute-done | bytes 262176 | tf_op jit(solution)/shard_map/ppermute | solution.py:514
  59.7 2.9 collective-permute-done.22.refs_28_
  63.7 2.1 collective-permute-start.25
  65.8 7.5 %collective-permute-done.24.refs_30_ = s16[512,128]{1,0:T(8,128)(2,1)S(1)} collective-permute-done((s16[512,128]{1,0:T(8,128)(2,1)S(1)}, s16[512,128]{1,0:T(8,128)(2,1)S(1)}, u32[]{:S(2)}, u32[]{:S(2)}) %collective-permute-start.24) | collective-permute-done | bytes 131104 | tf_op jit(solution)/shard_map/ppermute | solution.py:514
  75.2 4.8 %collective-permute-done.26.refs_32_ = s16[512,128]{1,0:T(8,128)(2,1)S(1)} collective-permute-done((s16[512,128]{1,0:T(8,128)(2,1)S(1)}, s16[512,128]{1,0:T(8,128)(2,1)S(1)}, u32[]{:S(2)}, u32[]{:S(2)}) %collective-permute-start.26) | collective-permute-done | bytes 131104 | tf_op jit(solution)/shard_map/ppermute | solution.py:514
  85.7 11.6 %column_first.1 = bf16[8,4,4,2,32,128]{5,4,3,2,1,0:T(8,128)(2,1)} custom-call(s32[1]{0:T(128)} %bitcast.1.refs_0_, s32[1]{0:T(128)} %get-tuple-element.51.refs_1_, bf16[2,512,128]{2,1,0:T(8,128)(2,1)} %get-tuple-element.32.refs_2_, bf16[2,512,128]{2,1,0:T(8,128)(2,1)} %copy-done.21, bf16[2,512,128]{2,1,0:T(8,128)(2,1)} %copy-done.22, ...), custom_call_target="tpu_custom_call" | custom-call | tf_op jit(solution)/shard_map/column_first/pallas_call | solution.py:272
  97.3 52.7 %all_to_all.20.refs_0_ = bf16[32,4,2,32,128]{4,3,2,1,0:T(8,128)(2,1)} all-to-all(bf16[32,4,2,32,128]{4,3,2,1,0:T(8,128)(2,1)} %bitcast.27), channel_id=1, replica_groups=mesh['rows'=8,'cols'=4] {'rows','cols'}, dimensions={0} | all-to-all | bytes 4194304 | tf_op jit(solution)/shard_map/all_to_all | solution.py:508
  150.0 9.6 %row_both.1 = bf16[32,4,2,32,128]{4,3,2,1,0:T(8,128)(2,1)} custom-call(bf16[32,4,2,32,128]{4,3,2,1,0:T(8,128)(2,1)} %all_to_all.20.refs_0_, bf16[4,8,128,128]{3,2,1,0:T(8,128)(2,1)} %copy-done.1, bf16[4,512,256]{2,1,0:T(8,128)(2,1)} %constant.57.clone.refs_2_, f32[8,2,1,512]{3,2,1,0:T(1,128)} %constant.58.clone.refs_3_), custom_call_target="tpu_custom_call" | custom-call | tf_op jit(solution)/shard_map/row_both/pallas_call | solution.py:377
  159.6 4.1 %all-to-all-start.2 = ((bf16[32,4,2,32,128]{4,3,2,1,0:T(8,128)(2,1)}), bf16[32,4,2,32,128]{4,3,2,1,0:T(8,128)(2,1)S(1)}, u32[]{:S(2)}, u32[]{:S(2)}) async-start(bf16[32,4,2,32,128]{4,3,2,1,0:T(8,128)(2,1)} %row_both.1), calls=%async_computation.2 | async-start | bytes 4194304 | tf_op jit(solution)/shard_map/all_to_all | solution.py:508
  163.7 0.9 dynamic-slice_bitcast_fusion
  164.8 1.5 collective-permute-start.29
  167.1 1.2 collective-permute-start.32
  168.3 1.5 collective-permute-start.33
  169.8 11.9 %collective-permute-done.29.refs_21_ = s16[512,128]{1,0:T(8,128)(2,1)S(1)} collective-permute-done((s16[512,128]{1,0:T(8,128)(2,1)S(1)}, s16[512,128]{1,0:T(8,128)(2,1)S(1)}, u32[]{:S(2)}, u32[]{:S(2)}) %collective-permute-start.29) | collective-permute-done | bytes 131104 | tf_op jit(solution)/shard_map/ppermute | solution.py:514
  181.7 3.1 collective-permute-done.30.refs_22_
  184.8 7.1 %collective-permute-done.33.refs_25_ = s16[512,128]{1,0:T(8,128)(2,1)S(1)} collective-permute-done((s16[512,128]{1,0:T(8,128)(2,1)S(1)}, s16[512,128]{1,0:T(8,128)(2,1)S(1)}, u32[]{:S(2)}, u32[]{:S(2)}) %collective-permute-start.33) | collective-permute-done | bytes 131104 | tf_op jit(solution)/shard_map/ppermute | solution.py:514
  191.9 3.0 collective-permute-done.34.refs_26_
  194.9 16.7 %all-to-all-done.2 = bf16[32,4,2,32,128]{4,3,2,1,0:T(8,128)(2,1)S(1)} async-done(((bf16[32,4,2,32,128]{4,3,2,1,0:T(8,128)(2,1)}), bf16[32,4,2,32,128]{4,3,2,1,0:T(8,128)(2,1)S(1)}, u32[]{:S(2)}, u32[]{:S(2)}) %all-to-all-start.2) | async-done | bytes 2097184 | tf_op jit(solution)/shard_map/all_to_all | solution.py:508
  211.7 1.3 copy-done
  213.0 15.2 %column_later.1 = bf16[8,4,4,2,32,128]{5,4,3,2,1,0:T(8,128)(2,1)} custom-call(s32[1]{0:T(128)} %bitcast.1.refs_0_, s32[1]{0:T(128)} %get-tuple-element.52.refs_1_, bf16[8,4,4,2,32,128]{5,4,3,2,1,0:T(8,128)(2,1)} %bitcast.25, bf16[2,256,384]{2,1,0:T(8,128)(2,1)} %copy-done.2, bf16[2,256,384]{2,1,0:T(8,128)(2,1)} %reshape.33.refs_11_.refs_4_, ...), custom_call_target="tpu_custom_call" | custom-call | tf_op jit(solution)/shard_map/column_later/pallas_call | solution.py:272
  228.2 3.7 %all-to-all-start.3 = ((bf16[32,4,2,32,128]{4,3,2,1,0:T(8,128)(2,1)}), bf16[32,4,2,32,128]{4,3,2,1,0:T(8,128)(2,1)S(1)}, u32[]{:S(2)}, u32[]{:S(2)}) async-start(bf16[32,4,2,32,128]{4,3,2,1,0:T(8,128)(2,1)} %bitcast.26), calls=%async_computation.3 | async-start | bytes 4194304 | tf_op jit(solution)/shard_map/all_to_all | solution.py:508
  231.9 47.9 %all-to-all-done.3.refs_1_ = bf16[32,4,2,32,128]{4,3,2,1,0:T(8,128)(2,1)S(1)} async-done(((bf16[32,4,2,32,128]{4,3,2,1,0:T(8,128)(2,1)}), bf16[32,4,2,32,128]{4,3,2,1,0:T(8,128)(2,1)S(1)}, u32[]{:S(2)}, u32[]{:S(2)}) %all-to-all-start.3) | async-done | bytes 2097184 | tf_op jit(solution)/shard_map/all_to_all | solution.py:508
  279.9 1.3 copy-done.3
  281.2 4.0 %row_last.3 = (bf16[2,8,64,128]{3,2,1,0:T(8,128)(2,1)}, bf16[2,8,64,128]{3,2,1,0:T(8,128)(2,1)}, bf16[2,8,64,128]{3,2,1,0:T(8,128)(2,1)}, bf16[2,8,64,128]{3,2,1,0:T(8,128)(2,1)}) custom-call(s32[1]{0:T(128)} %bitcast.refs_0_, bf16[32,4,2,32,128]{4,3,2,1,0:T(8,128)(2,1)} %copy-done.3, bf16[4,512,256]{2,1,0:T(8,128)(2,1)} %constant.57.clone.refs_2_, ...), custom_call_target="tpu_custom_call" | custom-call | flops 1073741824 | bytes 4194304 | tf_op jit(solution)/shard_map/row_last/pallas_call | solution.py:420
  285.2 2.0 collective-permute-start.39
  287.2 1.5 collective-permute-start.40
  288.6 4.0 %row_last.2 = (bf16[2,8,64,128]{3,2,1,0:T(8,128)(2,1)}, bf16[2,8,64,128]{3,2,1,0:T(8,128)(2,1)}, bf16[2,8,64,128]{3,2,1,0:T(8,128)(2,1)}, bf16[2,8,64,128]{3,2,1,0:T(8,128)(2,1)}) custom-call(s32[1]{0:T(128)} %bitcast.refs_0_, bf16[32,4,2,32,128]{4,3,2,1,0:T(8,128)(2,1)} %copy-done.3, bf16[4,512,256]{2,1,0:T(8,128)(2,1)} %constant.57.clone.refs_2_, ...), custom_call_target="tpu_custom_call" | custom-call | flops 1073741824 | bytes 4194304 | tf_op jit(solution)/shard_map/row_last/pallas_call | solution.py:420
  293.5 1.1 collective-permute-start.36
  294.6 1.6 collective-permute-done.38.refs_2_
  296.2 2.5 collective-permute-start.37
  298.7 6.7 %collective-permute-done.39.refs_3_ = bf16[2,8,64,128]{3,2,1,0:T(8,128)(2,1)S(1)} collective-permute-done((bf16[2,8,64,128]{3,2,1,0:T(8,128)(2,1)}, bf16[2,8,64,128]{3,2,1,0:T(8,128)(2,1)S(1)}, u32[]{:S(2)}, u32[]{:S(2)}) %collective-permute-start.39) | collective-permute-done | bytes 262176 | tf_op jit(solution)/shard_map/ppermute | solution.py:514
  305.4 18.8 %collective-permute-done.40.refs_4_ = bf16[2,8,64,128]{3,2,1,0:T(8,128)(2,1)S(1)} collective-permute-done((bf16[2,8,64,128]{3,2,1,0:T(8,128)(2,1)}, bf16[2,8,64,128]{3,2,1,0:T(8,128)(2,1)S(1)}, u32[]{:S(2)}, u32[]{:S(2)}) %collective-permute-start.40) | collective-permute-done | bytes 262176 | tf_op jit(solution)/shard_map/ppermute | solution.py:514
  324.9 5.3 %closing_order.2.refs_8_ = f32[2,512,1024]{2,1,0:T(8,128)} custom-call(s32[1]{0:T(128)} %bitcast.refs_0_, bf16[2,8,64,128]{3,2,1,0:T(8,128)(2,1)} %get-tuple-element.19.refs_1_, bf16[2,8,64,128]{3,2,1,0:T(8,128)(2,1)} %copy-done.29, bf16[2,8,64,128]{3,2,1,0:T(8,128)(2,1)} %copy-done.31, bf16[2,8,64,128]{3,2,1,0:T(8,128)(2,1)} %copy-done.32, ...), custom_call_target="tpu_custom_call" | custom-call | flops 1073741824 | bytes 4194304 | tf_op jit(solution)/shard_map/closing_order/pallas_call | solution.py:493
  330.2 4.1 %collective-permute-done.37.refs_4_ = bf16[2,8,64,128]{3,2,1,0:T(8,128)(2,1)S(1)} collective-permute-done((bf16[2,8,64,128]{3,2,1,0:T(8,128)(2,1)}, bf16[2,8,64,128]{3,2,1,0:T(8,128)(2,1)S(1)}, u32[]{:S(2)}, u32[]{:S(2)}) %collective-permute-start.37) | collective-permute-done | bytes 262176 | tf_op jit(solution)/shard_map/ppermute | solution.py:514
  335.0 5.3 %closing_order.3 = f32[2,512,1024]{2,1,0:T(8,128)} custom-call(s32[1]{0:T(128)} %bitcast.refs_0_, bf16[2,8,64,128]{3,2,1,0:T(8,128)(2,1)} %get-tuple-element.15.refs_1_, bf16[2,8,64,128]{3,2,1,0:T(8,128)(2,1)} %copy-done.28, bf16[2,8,64,128]{3,2,1,0:T(8,128)(2,1)} %copy-done.30, bf16[2,8,64,128]{3,2,1,0:T(8,128)(2,1)} %copy-done.33, ...), custom_call_target="tpu_custom_call", output_to_operand_aliasing={{}: (8, {})} | custom-call | flops 1073741824 | bytes 4194304 | tf_op jit(solution)/shard_map/closing_order/pallas_call | solution.py:493
  (162 shorter events, 20.6 us)
Async XLA Ops:
  2.8 16.8 %collective-permute-start = (bf16[2,512,128]{2,1,0:T(8,128)(2,1)}, bf16[2,512,128]{2,1,0:T(8,128)(2,1)S(1)}, u32[]{:S(2)}, u32[]{:S(2)}) collective-permute-start(bf16[2,512,128]{2,1,0:T(8,128)(2,1)} %get-tuple-element.31), channel_id=1, source_target_pairs={{0,4},{4,0},{8,12},{12,8},{16,20},{20,16},{24,28},{28,24},{1,5},{5... | collective-permute-start | bytes 786440 | tf_op jit(solution)/shard_map/ppermute | solution.py:514
  2.8 18.3 %collective-permute-start.1 = (bf16[2,512,128]{2,1,0:T(8,128)(2,1)}, bf16[2,512,128]{2,1,0:T(8,128)(2,1)S(1)}, u32[]{:S(2)}, u32[]{:S(2)}) collective-permute-start(bf16[2,512,128]{2,1,0:T(8,128)(2,1)} %get-tuple-element.30), channel_id=1, source_target_pairs={{0,8},{4,12},{8,0},{12,4},{16,24},{20,28},{24,16},{28,20},{1,9},{5... | collective-permute-start | bytes 786440 | tf_op jit(solution)/shard_map/ppermute | solution.py:514
  4.3 16.8 %collective-permute-start.2 = (bf16[2,512,128]{2,1,0:T(8,128)(2,1)}, bf16[2,512,128]{2,1,0:T(8,128)(2,1)S(1)}, u32[]{:S(2)}, u32[]{:S(2)}) collective-permute-start(bf16[2,512,128]{2,1,0:T(8,128)(2,1)} %get-tuple-element.29), channel_id=1, source_target_pairs={{0,12},{4,8},{8,4},{12,0},{16,28},{20,24},{24,20},{28,16},{1,13},{... | collective-permute-start | bytes 786440 | tf_op jit(solution)/shard_map/ppermute | solution.py:514
  5.6 33.5 %collective-permute-start.9 = (bf16[2,256,384]{2,1,0:T(8,128)(2,1)S(1)}, bf16[2,256,384]{2,1,0:T(8,128)(2,1)S(1)}, u32[]{:S(2)}, u32[]{:S(2)}) collective-permute-start(bf16[2,256,384]{2,1,0:T(8,128)(2,1)S(1)} %reshape.32.refs_10_.refs_3_), channel_id=1, source_target_pairs={{0,8},{4,12},{8,0},{12,4},{16,24},{20,28},{24,16},{28,20},{1,9},{5... | collective-permute-start | bytes 1179656 | tf_op jit(solution)/shard_map/ppermute | solution.py:514
  8.6 32.1 %collective-permute-start.14 = (bf16[2,256,384]{2,1,0:T(8,128)(2,1)}, bf16[2,256,384]{2,1,0:T(8,128)(2,1)S(1)}, u32[]{:S(2)}, u32[]{:S(2)}) collective-permute-start(bf16[2,256,384]{2,1,0:T(8,128)(2,1)} %reshape.33.refs_11_.refs_4_), channel_id=1, source_target_pairs={{0,16},{4,20},{8,24},{12,28},{16,0},{20,4},{24,8},{28,12},{1,17},{... | collective-permute-start | bytes 1179656 | tf_op jit(solution)/shard_map/ppermute | solution.py:514
  14.2 83.1 %all-to-all-start.1 = ((bf16[4,8,128,128]{3,2,1,0:T(8,128)(2,1)}), bf16[4,8,128,128]{3,2,1,0:T(8,128)(2,1)S(1)}, u32[]{:S(2)}, u32[]{:S(2)}) async-start(bf16[4,8,128,128]{3,2,1,0:T(8,128)(2,1)} %mask_order.1), calls=%async_computation.1 | async-start | bytes 2097152 | tf_op jit(solution)/shard_map/all_to_all | solution.py:508
  19.6 15.1 %collective-permute-start.3 = (bf16[2,512,128]{2,1,0:T(8,128)(2,1)}, bf16[2,512,128]{2,1,0:T(8,128)(2,1)S(1)}, u32[]{:S(2)}, u32[]{:S(2)}) collective-permute-start(bf16[2,512,128]{2,1,0:T(8,128)(2,1)} %get-tuple-element.28), channel_id=1, source_target_pairs={{0,16},{4,20},{8,24},{12,28},{16,0},{20,4},{24,8},{28,12},{1,17},{... | collective-permute-start | bytes 786440 | tf_op jit(solution)/shard_map/ppermute | solution.py:514
  21.1 16.4 %collective-permute-start.4 = (bf16[2,512,128]{2,1,0:T(8,128)(2,1)S(1)}, bf16[2,512,128]{2,1,0:T(8,128)(2,1)S(1)}, u32[]{:S(2)}, u32[]{:S(2)}) collective-permute-start(bf16[2,512,128]{2,1,0:T(8,128)(2,1)S(1)} %get-tuple-element.27), channel_id=1, source_target_pairs={{0,20},{4,16},{8,28},{12,24},{16,4},{20,0},{24,12},{28,8},{1,21},{... | collective-permute-start | bytes 786440 | tf_op jit(solution)/shard_map/ppermute | solution.py:514
  21.1 17.4 %collective-permute-start.5 = (bf16[2,512,128]{2,1,0:T(8,128)(2,1)S(1)}, bf16[2,512,128]{2,1,0:T(8,128)(2,1)S(1)}, u32[]{:S(2)}, u32[]{:S(2)}) collective-permute-start(bf16[2,512,128]{2,1,0:T(8,128)(2,1)S(1)} %get-tuple-element.26), channel_id=1, source_target_pairs={{0,24},{4,28},{8,16},{12,20},{16,8},{20,12},{24,0},{28,4},{1,25},{... | collective-permute-start | bytes 786440 | tf_op jit(solution)/shard_map/ppermute | solution.py:514
  34.6 50.3 %copy-start.24 = (bf16[2,512,128]{2,1,0:T(8,128)(2,1)}, bf16[2,512,128]{2,1,0:T(8,128)(2,1)S(1)}, u32[]{:S(2)}) copy-start(bf16[2,512,128]{2,1,0:T(8,128)(2,1)S(1)} %collective-permute-done.3.refs_6_) | copy-start | bytes 786436
  34.6 21.6 %collective-permute-start.7 = (bf16[2,256,384]{2,1,0:T(8,128)(2,1)S(1)}, bf16[2,256,384]{2,1,0:T(8,128)(2,1)S(1)}, u32[]{:S(2)}, u32[]{:S(2)}) collective-permute-start(bf16[2,256,384]{2,1,0:T(8,128)(2,1)S(1)} %reshape.32.refs_10_.refs_3_), channel_id=1, source_target_pairs={{0,4},{4,0},{8,12},{12,8},{16,20},{20,16},{24,28},{28,24},{1,5},{5... | collective-permute-start | bytes 1179656 | tf_op jit(solution)/shard_map/ppermute | solution.py:514
  37.5 47.4 %copy-start.25 = (bf16[2,512,128]{2,1,0:T(8,128)(2,1)}, bf16[2,512,128]{2,1,0:T(8,128)(2,1)S(1)}, u32[]{:S(2)}) copy-start(bf16[2,512,128]{2,1,0:T(8,128)(2,1)S(1)} %collective-permute-done.4.refs_7_) | copy-start | bytes 786436
  37.5 19.4 %collective-permute-start.8 = (bf16[2,256,384]{2,1,0:T(8,128)(2,1)}, bf16[2,256,384]{2,1,0:T(8,128)(2,1)S(1)}, u32[]{:S(2)}, u32[]{:S(2)}) collective-permute-start(bf16[2,256,384]{2,1,0:T(8,128)(2,1)} %reshape.33.refs_11_.refs_4_), channel_id=1, source_target_pairs={{0,4},{4,0},{8,12},{12,8},{16,20},{20,16},{24,28},{28,24},{1,5},{5... | collective-permute-start | bytes 1179656 | tf_op jit(solution)/shard_map/ppermute | solution.py:514
  38.5 46.4 %copy-start.26 = (bf16[2,512,128]{2,1,0:T(8,128)(2,1)}, bf16[2,512,128]{2,1,0:T(8,128)(2,1)S(1)}, u32[]{:S(2)}) copy-start(bf16[2,512,128]{2,1,0:T(8,128)(2,1)S(1)} %collective-permute-done.5.refs_8_) | copy-start | bytes 786436
  38.5 19.2 %collective-permute-start.10 = (bf16[2,256,384]{2,1,0:T(8,128)(2,1)}, bf16[2,256,384]{2,1,0:T(8,128)(2,1)S(1)}, u32[]{:S(2)}, u32[]{:S(2)}) collective-permute-start(bf16[2,256,384]{2,1,0:T(8,128)(2,1)} %reshape.33.refs_11_.refs_4_), channel_id=1, source_target_pairs={{0,8},{4,12},{8,0},{12,4},{16,24},{20,28},{24,16},{28,20},{1,9},{5... | collective-permute-start | bytes 1179656 | tf_op jit(solution)/shard_map/ppermute | solution.py:514
  39.1 19.4 %collective-permute-start.13 = (bf16[2,256,384]{2,1,0:T(8,128)(2,1)S(1)}, bf16[2,256,384]{2,1,0:T(8,128)(2,1)S(1)}, u32[]{:S(2)}, u32[]{:S(2)}) collective-permute-start(bf16[2,256,384]{2,1,0:T(8,128)(2,1)S(1)} %reshape.32.refs_10_.refs_3_), channel_id=1, source_target_pairs={{0,16},{4,20},{8,24},{12,28},{16,0},{20,4},{24,8},{28,12},{1,17},{... | collective-permute-start | bytes 1179656 | tf_op jit(solution)/shard_map/ppermute | solution.py:514
  41.4 14.1 %collective-permute-start.6 = (bf16[2,512,128]{2,1,0:T(8,128)(2,1)}, bf16[2,512,128]{2,1,0:T(8,128)(2,1)S(1)}, u32[]{:S(2)}, u32[]{:S(2)}) collective-permute-start(bf16[2,512,128]{2,1,0:T(8,128)(2,1)} %get-tuple-element.25), channel_id=1, source_target_pairs={{0,28},{4,24},{8,20},{12,16},{16,12},{20,8},{24,4},{28,0},{1,29},{... | collective-permute-start | bytes 786440 | tf_op jit(solution)/shard_map/ppermute | solution.py:514
  55.6 3.5 %collective-permute-start.21 = (s16[512,128]{1,0:T(8,128)(2,1)S(1)}, s16[512,128]{1,0:T(8,128)(2,1)S(1)}, u32[]{:S(2)}, u32[]{:S(2)}) collective-permute-start(s16[512,128]{1,0:T(8,128)(2,1)S(1)} %get-tuple-element.47), channel_id=1, source_target_pairs={{0,4},{4,0},{8,12},{12,8},{16,20},{20,16},{24,28},{28,24},{1,5},{5... | collective-permute-start | bytes 393224 | tf_op jit(solution)/shard_map/ppermute | solution.py:514
  56.3 6.4 %collective-permute-start.22 = (s16[512,128]{1,0:T(8,128)(2,1)S(1)}, s16[512,128]{1,0:T(8,128)(2,1)S(1)}, u32[]{:S(2)}, u32[]{:S(2)}) collective-permute-start(s16[512,128]{1,0:T(8,128)(2,1)S(1)} %get-tuple-element.46), channel_id=1, source_target_pairs={{0,8},{4,12},{8,0},{12,4},{16,24},{20,28},{24,16},{28,20},{1,9},{5... | collective-permute-start | bytes 393224 | tf_op jit(solution)/shard_map/ppermute | solution.py:514
  56.9 6.8 %collective-permute-start.23 = (s16[512,128]{1,0:T(8,128)(2,1)S(1)}, s16[512,128]{1,0:T(8,128)(2,1)S(1)}, u32[]{:S(2)}, u32[]{:S(2)}) collective-permute-start(s16[512,128]{1,0:T(8,128)(2,1)S(1)} %get-tuple-element.45), channel_id=1, source_target_pairs={{0,12},{4,8},{8,4},{12,0},{16,28},{20,24},{24,20},{28,16},{1,13},{... | collective-permute-start | bytes 393224 | tf_op jit(solution)/shard_map/ppermute | solution.py:514
  57.7 24.1 %collective-permute-start.11 = (bf16[2,256,384]{2,1,0:T(8,128)(2,1)S(1)}, bf16[2,256,384]{2,1,0:T(8,128)(2,1)S(1)}, u32[]{:S(2)}, u32[]{:S(2)}) collective-permute-start(bf16[2,256,384]{2,1,0:T(8,128)(2,1)S(1)} %copy-done.5), channel_id=1, source_target_pairs={{0,4},{4,0},{8,12},{12,8},{16,20},{20,16},{24,28},{28,24},{1,5},{5... | collective-permute-start | bytes 1179656 | tf_op jit(solution)/shard_map/ppermute | solution.py:514
  58.5 23.9 %collective-permute-start.17 = (bf16[2,256,384]{2,1,0:T(8,128)(2,1)S(1)}, bf16[2,256,384]{2,1,0:T(8,128)(2,1)S(1)}, u32[]{:S(2)}, u32[]{:S(2)}) collective-permute-start(bf16[2,256,384]{2,1,0:T(8,128)(2,1)S(1)} %copy-done.5), channel_id=1, source_target_pairs={{0,16},{4,20},{8,24},{12,28},{16,0},{20,4},{24,8},{28,12},{1,17},{... | collective-permute-start | bytes 1179656 | tf_op jit(solution)/shard_map/ppermute | solution.py:514
  59.1 23.4 %collective-permute-start.18 = (bf16[2,256,384]{2,1,0:T(8,128)(2,1)S(1)}, bf16[2,256,384]{2,1,0:T(8,128)(2,1)S(1)}, u32[]{:S(2)}, u32[]{:S(2)}) collective-permute-start(bf16[2,256,384]{2,1,0:T(8,128)(2,1)S(1)} %copy-done.7), channel_id=1, source_target_pairs={{0,8},{4,12},{8,0},{12,4},{16,24},{20,28},{24,16},{28,20},{1,9},{5... | collective-permute-start | bytes 1179656 | tf_op jit(solution)/shard_map/ppermute | solution.py:514
  62.6 10.6 %collective-permute-start.24 = (s16[512,128]{1,0:T(8,128)(2,1)S(1)}, s16[512,128]{1,0:T(8,128)(2,1)S(1)}, u32[]{:S(2)}, u32[]{:S(2)}) collective-permute-start(s16[512,128]{1,0:T(8,128)(2,1)S(1)} %get-tuple-element.44), channel_id=1, source_target_pairs={{0,16},{4,20},{8,24},{12,28},{16,0},{20,4},{24,8},{28,12},{1,17},{... | collective-permute-start | bytes 393224 | tf_op jit(solution)/shard_map/ppermute | solution.py:514
  63.7 10.7 %collective-permute-start.25 = (s16[512,128]{1,0:T(8,128)(2,1)S(1)}, s16[512,128]{1,0:T(8,128)(2,1)S(1)}, u32[]{:S(2)}, u32[]{:S(2)}) collective-permute-start(s16[512,128]{1,0:T(8,128)(2,1)S(1)} %get-tuple-element.43), channel_id=1, source_target_pairs={{0,20},{4,16},{8,28},{12,24},{16,4},{20,0},{24,12},{28,8},{1,21},{... | collective-permute-start | bytes 393224 | tf_op jit(solution)/shard_map/ppermute | solution.py:514
  73.3 6.8 %collective-permute-start.26 = (s16[512,128]{1,0:T(8,128)(2,1)S(1)}, s16[512,128]{1,0:T(8,128)(2,1)S(1)}, u32[]{:S(2)}, u32[]{:S(2)}) collective-permute-start(s16[512,128]{1,0:T(8,128)(2,1)S(1)} %get-tuple-element.42), channel_id=1, source_target_pairs={{0,24},{4,28},{8,16},{12,20},{16,8},{20,12},{24,0},{28,4},{1,25},{... | collective-permute-start | bytes 393224 | tf_op jit(solution)/shard_map/ppermute | solution.py:514
  74.4 6.6 %collective-permute-start.27 = (s16[512,128]{1,0:T(8,128)(2,1)S(1)}, s16[512,128]{1,0:T(8,128)(2,1)S(1)}, u32[]{:S(2)}, u32[]{:S(2)}) collective-permute-start(s16[512,128]{1,0:T(8,128)(2,1)S(1)} %get-tuple-element.41), channel_id=1, source_target_pairs={{0,28},{4,24},{8,20},{12,16},{16,12},{20,8},{24,4},{28,0},{1,29},{... | collective-permute-start | bytes 393224 | tf_op jit(solution)/shard_map/ppermute | solution.py:514
  80.1 3.7 %collective-permute-start.16 = (bf16[2,256,384]{2,1,0:T(8,128)(2,1)S(1)}, bf16[2,256,384]{2,1,0:T(8,128)(2,1)S(1)}, u32[]{:S(2)}, u32[]{:S(2)}) collective-permute-start(bf16[2,256,384]{2,1,0:T(8,128)(2,1)S(1)} %copy-done.7), channel_id=1, source_target_pairs={{0,4},{4,0},{8,12},{12,8},{16,20},{20,16},{24,28},{28,24},{1,5},{5... | collective-permute-start | bytes 1179656 | tf_op jit(solution)/shard_map/ppermute | solution.py:514
  81.0 2.6 collective-permute-start.12
  81.8 2.0 collective-permute-start.15
  82.4 1.9 collective-permute-start.19
  82.5 2.4 collective-permute-start.20
  97.3 52.7 %copy-start.1 = (bf16[4,8,128,128]{3,2,1,0:T(8,128)(2,1)}, bf16[4,8,128,128]{3,2,1,0:T(8,128)(2,1)S(1)}, u32[]{:S(2)}) copy-start(bf16[4,8,128,128]{3,2,1,0:T(8,128)(2,1)S(1)} %all-to-all-done.1.refs_1_) | copy-start | bytes 3145732
  159.6 52.0 %all-to-all-start.2 = ((bf16[32,4,2,32,128]{4,3,2,1,0:T(8,128)(2,1)}), bf16[32,4,2,32,128]{4,3,2,1,0:T(8,128)(2,1)S(1)}, u32[]{:S(2)}, u32[]{:S(2)}) async-start(bf16[32,4,2,32,128]{4,3,2,1,0:T(8,128)(2,1)} %row_both.1), calls=%async_computation.2 | async-start | bytes 4194304 | tf_op jit(solution)/shard_map/all_to_all | solution.py:508
  164.7 3.7 %collective-permute-start.28 = (s16[512,128]{1,0:T(8,128)(2,1)S(1)}, s16[512,128]{1,0:T(8,128)(2,1)S(1)}, u32[]{:S(2)}, u32[]{:S(2)}) collective-permute-start(s16[512,128]{1,0:T(8,128)(2,1)S(1)} %get-tuple-element.39), channel_id=1, source_target_pairs={{0,4},{4,0},{8,12},{12,8},{16,20},{20,16},{24,28},{28,24},{1,5},{5... | collective-permute-start | bytes 393224 | tf_op jit(solution)/shard_map/ppermute | solution.py:514
  164.8 16.8 %collective-permute-start.29 = (s16[512,128]{1,0:T(8,128)(2,1)S(1)}, s16[512,128]{1,0:T(8,128)(2,1)S(1)}, u32[]{:S(2)}, u32[]{:S(2)}) collective-permute-start(s16[512,128]{1,0:T(8,128)(2,1)S(1)} %get-tuple-element.38), channel_id=1, source_target_pairs={{0,8},{4,12},{8,0},{12,4},{16,24},{20,28},{24,16},{28,20},{1,9},{5... | collective-permute-start | bytes 393224 | tf_op jit(solution)/shard_map/ppermute | solution.py:514
  166.3 18.5 %collective-permute-start.30 = (s16[512,128]{1,0:T(8,128)(2,1)S(1)}, s16[512,128]{1,0:T(8,128)(2,1)S(1)}, u32[]{:S(2)}, u32[]{:S(2)}) collective-permute-start(s16[512,128]{1,0:T(8,128)(2,1)S(1)} %get-tuple-element.37), channel_id=1, source_target_pairs={{0,12},{4,8},{8,4},{12,0},{16,28},{20,24},{24,20},{28,16},{1,13},{... | collective-permute-start | bytes 393224 | tf_op jit(solution)/shard_map/ppermute | solution.py:514
  166.5 18.2 %collective-permute-start.31 = (s16[512,128]{1,0:T(8,128)(2,1)S(1)}, s16[512,128]{1,0:T(8,128)(2,1)S(1)}, u32[]{:S(2)}, u32[]{:S(2)}) collective-permute-start(s16[512,128]{1,0:T(8,128)(2,1)S(1)} %get-tuple-element.36), channel_id=1, source_target_pairs={{0,16},{4,20},{8,24},{12,28},{16,0},{20,4},{24,8},{28,12},{1,17},{... | collective-permute-start | bytes 393224 | tf_op jit(solution)/shard_map/ppermute | solution.py:514
  167.1 17.7 %collective-permute-start.32 = (s16[512,128]{1,0:T(8,128)(2,1)S(1)}, s16[512,128]{1,0:T(8,128)(2,1)S(1)}, u32[]{:S(2)}, u32[]{:S(2)}) collective-permute-start(s16[512,128]{1,0:T(8,128)(2,1)S(1)} %get-tuple-element.35), channel_id=1, source_target_pairs={{0,20},{4,16},{8,28},{12,24},{16,4},{20,0},{24,12},{28,8},{1,21},{... | collective-permute-start | bytes 393224 | tf_op jit(solution)/shard_map/ppermute | solution.py:514
  168.3 23.6 %collective-permute-start.33 = (s16[512,128]{1,0:T(8,128)(2,1)S(1)}, s16[512,128]{1,0:T(8,128)(2,1)S(1)}, u32[]{:S(2)}, u32[]{:S(2)}) collective-permute-start(s16[512,128]{1,0:T(8,128)(2,1)S(1)} %get-tuple-element.34), channel_id=1, source_target_pairs={{0,24},{4,28},{8,16},{12,20},{16,8},{20,12},{24,0},{28,4},{1,25},{... | collective-permute-start | bytes 393224 | tf_op jit(solution)/shard_map/ppermute | solution.py:514
  181.6 13.3 %collective-permute-start.34 = (s16[512,128]{1,0:T(8,128)(2,1)S(1)}, s16[512,128]{1,0:T(8,128)(2,1)S(1)}, u32[]{:S(2)}, u32[]{:S(2)}) collective-permute-start(s16[512,128]{1,0:T(8,128)(2,1)S(1)} %get-tuple-element.33), channel_id=1, source_target_pairs={{0,28},{4,24},{8,20},{12,16},{16,12},{20,8},{24,4},{28,0},{1,29},{... | collective-permute-start | bytes 393224 | tf_op jit(solution)/shard_map/ppermute | solution.py:514
  228.2 51.6 %all-to-all-start.3 = ((bf16[32,4,2,32,128]{4,3,2,1,0:T(8,128)(2,1)}), bf16[32,4,2,32,128]{4,3,2,1,0:T(8,128)(2,1)S(1)}, u32[]{:S(2)}, u32[]{:S(2)}) async-start(bf16[32,4,2,32,128]{4,3,2,1,0:T(8,128)(2,1)} %bitcast.26), calls=%async_computation.3 | async-start | bytes 4194304 | tf_op jit(solution)/shard_map/all_to_all | solution.py:508
  285.1 11.1 %collective-permute-start.38 = (bf16[2,8,64,128]{3,2,1,0:T(8,128)(2,1)}, bf16[2,8,64,128]{3,2,1,0:T(8,128)(2,1)S(1)}, u32[]{:S(2)}, u32[]{:S(2)}) collective-permute-start(bf16[2,8,64,128]{3,2,1,0:T(8,128)(2,1)} %get-tuple-element.20), channel_id=1, source_target_pairs={{0,1},{1,0},{2,3},{3,2},{4,5},{5,4},{6,7},{7,6},{8,9},{9,8},{10,11... | collective-permute-start | bytes 786440 | tf_op jit(solution)/shard_map/ppermute | solution.py:514
  285.2 20.2 %collective-permute-start.39 = (bf16[2,8,64,128]{3,2,1,0:T(8,128)(2,1)}, bf16[2,8,64,128]{3,2,1,0:T(8,128)(2,1)S(1)}, u32[]{:S(2)}, u32[]{:S(2)}) collective-permute-start(bf16[2,8,64,128]{3,2,1,0:T(8,128)(2,1)} %get-tuple-element.21), channel_id=1, source_target_pairs={{0,2},{1,3},{2,0},{3,1},{4,6},{5,7},{6,4},{7,5},{8,10},{9,11},{10,... | collective-permute-start | bytes 786440 | tf_op jit(solution)/shard_map/ppermute | solution.py:514
  287.2 37.0 %collective-permute-start.40 = (bf16[2,8,64,128]{3,2,1,0:T(8,128)(2,1)}, bf16[2,8,64,128]{3,2,1,0:T(8,128)(2,1)S(1)}, u32[]{:S(2)}, u32[]{:S(2)}) collective-permute-start(bf16[2,8,64,128]{3,2,1,0:T(8,128)(2,1)} %get-tuple-element.22), channel_id=1, source_target_pairs={{0,3},{1,2},{2,1},{3,0},{4,7},{5,6},{6,5},{7,4},{8,11},{9,10},{10,... | collective-permute-start | bytes 786440 | tf_op jit(solution)/shard_map/ppermute | solution.py:514
  292.6 37.6 %collective-permute-start.35 = (bf16[2,8,64,128]{3,2,1,0:T(8,128)(2,1)}, bf16[2,8,64,128]{3,2,1,0:T(8,128)(2,1)S(1)}, u32[]{:S(2)}, u32[]{:S(2)}) collective-permute-start(bf16[2,8,64,128]{3,2,1,0:T(8,128)(2,1)} %get-tuple-element.16), channel_id=1, source_target_pairs={{0,1},{1,0},{2,3},{3,2},{4,5},{5,4},{6,7},{7,6},{8,9},{9,8},{10,11... | collective-permute-start | bytes 786440 | tf_op jit(solution)/shard_map/ppermute | solution.py:514
  293.5 36.7 %collective-permute-start.36 = (bf16[2,8,64,128]{3,2,1,0:T(8,128)(2,1)}, bf16[2,8,64,128]{3,2,1,0:T(8,128)(2,1)S(1)}, u32[]{:S(2)}, u32[]{:S(2)}) collective-permute-start(bf16[2,8,64,128]{3,2,1,0:T(8,128)(2,1)} %get-tuple-element.17), channel_id=1, source_target_pairs={{0,2},{1,3},{2,0},{3,1},{4,6},{5,7},{6,4},{7,5},{8,10},{9,11},{10,... | collective-permute-start | bytes 786440 | tf_op jit(solution)/shard_map/ppermute | solution.py:514
  296.2 38.1 %collective-permute-start.37 = (bf16[2,8,64,128]{3,2,1,0:T(8,128)(2,1)}, bf16[2,8,64,128]{3,2,1,0:T(8,128)(2,1)S(1)}, u32[]{:S(2)}, u32[]{:S(2)}) collective-permute-start(bf16[2,8,64,128]{3,2,1,0:T(8,128)(2,1)} %get-tuple-element.18), channel_id=1, source_target_pairs={{0,3},{1,2},{2,1},{3,0},{4,7},{5,6},{6,5},{7,4},{8,11},{9,10},{10,... | collective-permute-start | bytes 786440 | tf_op jit(solution)/shard_map/ppermute | solution.py:514
  (46 other events, 597.3 us)

commit v3 on v2

--- a/solution.py
+++ b/solution.py
@@ -141,19 +141,24 @@
     return pl.ds(pl.multiple_of(start, size), size)
 
 
-def column_body(later, peers, *refs):
-    place_ref, shift_ref = refs[:2]
-    current, refs = (refs[2:3], refs[3:]) if later else (refs[2 : 2 + peers], refs[2 + peers :])
-    mats, refs = refs[: 2 * peers], refs[2 * peers :]
-    angles, refs = refs[:peers], refs[peers:]
-    tables, refs = refs[: 1 + later], refs[1 + later :]
+def by_distance(pieces, distance):
+    return pieces[-1].at[distance // 2] if distance % 2 else pieces[distance // 2]
+
+
+def column_body(later, peers, counts, *refs):
+    (place_ref, shift_ref), refs = refs[:2], refs[2:]
+    groups = []
+    for count in counts:
+        groups.append(refs[:count])
+        refs = refs[count:]
+    current, *mats, angles, tables = groups
     out_ref, padded, wave, mixed, held_mats, held_angles = refs[:6]
     held_tables, sems = refs[6:-1], refs[-1]
     rows_at, cols_at, firsts, _, seconds, width = out_ref.shape
     extent = wave.shape[1]
     part = extent // RADIX
     height = extent // peers
-    half_blocks = height // BLOCK // 2
+    own_blocks = height // BLOCK
 
     copies = []
 
@@ -166,8 +171,12 @@
     table_copies = [fetch(tables[-1], held_tables[-1])] if later else []
     mat_copies, angle_copies = [], []
     for at in range(peers):
-        mat_copies.append([fetch(mats[2 * at + one], held_mats.at[at, one]) for one in range(2)])
-        angle_copies.append(fetch(angles[at], held_angles.at[at]))
+        first, some = 0, []
+        for piece in mats[at]:
+            some.append(fetch(piece, held_mats.at[at, pl.ds(first, piece.shape[0])]))
+            first += piece.shape[0]
+        mat_copies.append(some)
+        angle_copies.append(fetch(by_distance(angles, at), held_angles.at[at]))
     table_copies.append(fetch(tables[0], held_tables[0]))
 
     padded[:, pl.ds(0, height)] = jnp.zeros((2, height, width), F32)
@@ -202,14 +211,15 @@
     else:
         for at in range(peers):
             rows = aligned(height + (place_ref[0] ^ at) * height, height)
-            padded[0, rows] = current[at][0].astype(F32)
-            padded[1, rows] = current[at][1].astype(F32)
+            piece = by_distance(current, at)
+            padded[0, rows] = piece[0].astype(F32)
+            padded[1, rows] = piece[1].astype(F32)
 
     shift = shift_ref[0]
     for at in range(peers):
         start = (place_ref[0] ^ at) * height
-        for one in range(2):
-            mat_copies[at][one].wait()
+        for copy in mat_copies[at]:
+            copy.wait()
         angle_copies[at].wait()
 
         def diffract(block, at=at, start=start):
@@ -218,8 +228,7 @@
             for order in range(3):
                 rows = pl.ds(height + start + within + (order - 1) * shift, BLOCK)
                 rights.append(jnp.concatenate([padded[0, rows], padded[1, rows]], axis=1).astype(BF16))
-            left = held_mats[at, block // half_blocks, block % half_blocks]
-            got = dot(left, jnp.concatenate(rights, axis=0))
+            got = dot(held_mats[at, block], jnp.concatenate(rights, axis=0))
             real = got[:BLOCK, :width] - got[BLOCK:, width:]
             imag = got[:BLOCK, width:] + got[BLOCK:, :width]
             cosine, sine = cos_sin(held_angles[at, aligned(within, BLOCK)].astype(F32) * (1.0 / ANGLE_STEPS))
@@ -227,7 +236,7 @@
             wave[0, rows] = real * cosine - imag * sine
             wave[1, rows] = real * sine + imag * cosine
 
-        loop(2 * half_blocks, diffract, 4)
+        loop(own_blocks, diffract, 4)
 
     def mix(at):
         parts = []
@@ -257,35 +266,35 @@
 
 
 def column_work(later, place, shift, current, mats, angles, tables, col_count):
-    peers = len(angles)
+    peers = len(mats)
     height, width = angles[0].shape
     extent = height * peers
     part = extent // RADIX
+    groups = [[current] if later else current, *mats, angles, tables if later else tables[:1]]
+    counts = [len(group) for group in groups]
+    copies = sum(counts[1:-2]) + peers + counts[-1]
 
     def body(*refs):
-        column_body(later, peers, *refs)
-
-    currents = [current] if later else current
-    tables = tables if later else tables[:1]
-    mats = [one for pair in mats for one in pair]
+        column_body(later, peers, counts, *refs)
+
     smem, anywhere = pl.BlockSpec(memory_space=pltpu.SMEM), pl.BlockSpec(memory_space=pl.ANY)
     return pl.pallas_call(
         body,
         out_shape=jax.ShapeDtypeStruct((peers, col_count, RADIX // col_count, 2, part // peers, width), BF16),
-        in_specs=[smem, smem] + vmem(len(currents)) + [anywhere] * (len(mats) + peers + len(tables)),
+        in_specs=[smem, smem] + vmem(counts[0]) + [anywhere] * sum(counts[1:]),
         out_specs=vmem(1)[0],
         scratch_shapes=[
             pltpu.VMEM((2, extent + 2 * height, width), F32),
             pltpu.VMEM((2, extent, width), F32),
             pltpu.VMEM((RADIX, part, 2 * width), BF16),
-            pltpu.VMEM((peers, 2, *mats[0].shape), BF16),
+            pltpu.VMEM((peers, height // BLOCK, 2 * BLOCK, 3 * BLOCK), BF16),
             pltpu.VMEM((peers, height, width), angles[0].dtype),
-            *[pltpu.VMEM(table.shape, BF16) for table in tables],
-            pltpu.SemaphoreType.DMA((len(mats) + peers + len(tables),)),
+            *[pltpu.VMEM(table.shape, BF16) for table in groups[-1]],
+            pltpu.SemaphoreType.DMA((copies,)),
         ],
         compiler_params=params(),
         name="column_later" if later else "column_first",
-    )(place, shift, *currents, *mats, *angles, *tables)
+    )(place, shift, *[one for group in groups for one in group])
 
 
 def row_mix(order, in_ref, turn_ref, mixed):
@@ -525,17 +534,32 @@
 
 def gather_mats(mats):
     peers = lax.axis_size("rows")
-    halves = mats[: mats.shape[0] // 2], mats[mats.shape[0] // 2 :]
     if peers != 8:
-        result = [[swap(half, "rows", distance) for half in halves] for distance in range(peers)]
+        result = [[swap(mats, "rows", distance)] for distance in range(peers)]
         return result, result[1]
-    by_x = [swap(half, "rows", 2) for half in halves]
-    by_y = [swap(half, "rows", 4) for half in halves]
-    across = [swap(by_x[0], "rows", 4), swap(by_y[1], "rows", 2)]
+    half = mats.shape[0] // 2
+    by_x, by_y = swap(mats, "rows", 2), swap(mats, "rows", 4)
+    across = [swap(by_x[:half], "rows", 4), swap(by_y[half:], "rows", 2)]
     result = []
-    for pair in (halves, by_x, by_y, across):
-        result += [list(pair), [swap(half, "rows", 1) for half in pair]]
-    return result, (by_x[0], by_y[1])
+    for pieces in ([mats], [by_x], [by_y], across):
+        result += [pieces, [swap(piece, "rows", 1) for piece in pieces]]
+    return result, (by_x, by_y)
+
+
+def spread(value, width):
+    peers, along = lax.axis_size("rows"), lax.axis_index("rows")
+    chips = []
+    for distance in range(0, peers, 2):
+        start = ((along ^ distance) // 2) * (2 * width)
+        piece = lax.dynamic_slice_in_dim(value, start, 2 * width, value.ndim - 1)
+        chips.append(swap(piece, "rows", distance))
+
+    def part(piece, core):
+        return lax.dynamic_slice_in_dim(piece, core * width, width, value.ndim - 1)
+
+    core = along % 2
+    other = swap(jnp.stack([part(piece, 1 - core) for piece in chips]), "rows", 1)
+    return [widen(part(piece, core)) for piece in chips] + [widen(other)]
 
 
 def on_device(spectrum, diffraction, order_mask, phases, transmission, shifts):
@@ -554,19 +578,13 @@
     along, above = lax.axis_index("rows"), lax.axis_index("cols")
     place_rows, place_cols = (at.astype(jnp.int32).reshape(1) for at in (along, above))
 
-    def spread(value):
-        return [
-            widen(swap(lax.dynamic_slice_in_dim(value, (along ^ distance) * width, width, value.ndim - 1), "rows", distance))
-            for distance in range(row_count)
-        ]
-
     masked = diffraction * order_mask.astype(BF16)[None, :, :, None, None]
     blocks = height // BLOCK
     masked = masked.transpose(1, 0, 3, 2, 4).reshape(blocks, 2 * BLOCK, 3 * BLOCK)
     mats, first_mats = gather_mats(masked)
-    current = spread(after(spectrum, masked))
+    current = spread(spectrum, width)
     codes = jnp.round(phases * ANGLE_STEPS).astype(jnp.int16)
-    angles = [spread(after(codes[0], first_mats)), spread(codes[1])]
+    angles = [spread(codes[0], width), spread(codes[1], width)]
     kept = exchange(mask_work(transmission, row_count, col_count, radix), "cols")
 
     narrow = width < LANES

time: 341 us -> 330 us (0.968)
  waiting for transfers between devices: 164 us -> 149 us
  local copies, waits for them, and re-layouts: 13.8 us -> 26.9 us
  starting transfers between devices: 46.1 us -> 35.6 us
    another operation x0 -> x10, local copies, waits for them, and re-layouts: none -> 13.5 us  [spread(): jnp.stack([part(piece, 1 - core) for piece in chips])]
    ppermute x41 -> x27, waiting for transfers between devices: 99.3 us -> 87.8 us  [swap(): lax.ppermute(value, axis, [(at, at ^ distance) for at in range(lax.axis_s...]
    ppermute x41 -> x27, starting transfers between devices: 33.1 us -> 22.4 us  [swap(): lax.ppermute(value, axis, [(at, at ^ distance) for at in range(lax.axis_s...]
    all_to_all x3, waiting for transfers between devices: 64.6 us -> 60.9 us  [exchange(): return lax.all_to_all(value, axis, split_axis=0, concat_axis=0, tiled=True)]
  transfers between devices with their start and end apart: 44 -> 30, of which waited for: 22 -> 15; matrix products, arithmetic and copies ran while one was open for 2% -> 7% of each run, Pallas kernels for 8% -> 8%
where the time goes in v3:
time: 330 us; the launch traced here: 329 us
  waiting for transfers between devices  149 us (45%)
  Pallas kernels  60 us (18%)
  blocking collectives  52.9 us (16%)
  starting transfers between devices  35.6 us (11%)
  local copies, waits for them, and re-layouts  26.9 us (8%)
  other arithmetic  4.09 us (1%)
    ppermute x27, waiting for transfers between devices, swap(): lax.ppermute(value, axis, [(at, at ^ distance) for at in range(lax.axis_s...  87.8 us
    all_to_all x3, waiting for transfers between devices, exchange(): return lax.all_to_all(value, axis, split_axis=0, concat_axis=0, tiled=True)  60.9 us
    all_to_all x1, blocking collectives, exchange(): return lax.all_to_all(value, axis, split_axis=0, concat_axis=0, tiled=True)  52.9 us
    pallas_call x2, Pallas kernels, column_work(): pl.pallas_call(body, out_shape=jax.ShapeDtypeStruct((peers, col_count, RA...  26.6 us
    ppermute x27, starting transfers between devices, swap(): lax.ppermute(value, axis, [(at, at ^ distance) for at in range(lax.axis_s...  22.4 us
    another operation x10, local copies, waits for them, and re-layouts, spread(): jnp.stack([part(piece, 1 - core) for piece in chips])  13.5 us
    all_to_all x3, starting transfers between devices, exchange(): return lax.all_to_all(value, axis, split_axis=0, concat_axis=0, tiled=True)  13.2 us
    pallas_call x2, Pallas kernels, closing_work(): pl.pallas_call(body, grid=(1,), out_shape=jax.ShapeDtypeStruct((2, height...  10.7 us
  transfers between devices with their start and end apart: 30, of which 15 were waited for; matrix products, arithmetic and copies ran while one was open for 7% of the time, Pallas kernels for 8%

profile of v3, /device:TPU:12, one launch (start us, length us, event | category | flops | bytes accessed | tf_op | source)
XLA Modules:
  0.0 328.6 jit_solution(1952685926572528108)
XLA Ops:
  0.0 2.6 constant_dynamic-slice_fusion.9
  2.6 1.5 collective-permute-start
  4.6 2.9 round-nearest-even_convert_fusion
  7.5 1.2 fusion
  10.1 1.5 collective-permute-start.14
  11.6 1.4 collective-permute-start.15
  13.0 5.2 %mask_order.1 = bf16[4,8,128,128]{3,2,1,0:T(8,128)(2,1)} custom-call(f32[512,1024]{1,0:T(8,128)} %refs_5_.3, bf16[512,512]{1,0:T(8,128)(2,1)} %constant.199.clone.down_ref, bf16[1024,1024]{1,0:T(8,128)(2,1)} %constant.200.clone.across_ref), custom_call_target="tpu_custom_call" | custom-call | tf_op jit(solution)/shard_map/mask_order/pallas_call | solution.py:455
  18.2 5.4 %all-to-all-start.1 = ((bf16[4,8,128,128]{3,2,1,0:T(8,128)(2,1)}), bf16[4,8,128,128]{3,2,1,0:T(8,128)(2,1)S(1)}, u32[]{:S(2)}, u32[]{:S(2)}) async-start(bf16[4,8,128,128]{3,2,1,0:T(8,128)(2,1)} %mask_order.1), calls=%async_computation.1 | async-start | bytes 2097152 | tf_op jit(solution)/shard_map/all_to_all | solution.py:517
  24.7 2.2 dynamic-slice_bitcast_fusion.9
  29.1 1.6 collective-permute-start.2
  30.7 1.6 dynamic-slice_bitcast_fusion.16
  32.3 1.6 dynamic-slice_bitcast_fusion.15
  34.0 1.5 collective-permute-start.5
  35.5 1.6 dynamic-slice_bitcast_fusion.14
  37.7 1.8 dynamic-slice_bitcast_fusion.8
  39.5 1.8 dynamic-slice_bitcast_fusion.7
  41.2 4.0 %collective-permute-done.2 = bf16[2,512,256]{2,1,0:T(8,128)(2,1)S(1)} collective-permute-done((bf16[2,512,256]{2,1,0:T(8,128)(2,1)}, bf16[2,512,256]{2,1,0:T(8,128)(2,1)S(1)}, u32[]{:S(2)}, u32[]{:S(2)}) %collective-permute-start.2) | collective-permute-done | bytes 524320 | tf_op jit(solution)/shard_map/ppermute | solution.py:523
  46.2 12.7 %collective-permute-done.5.refs_9_.refs_5_ = bf16[4,256,384]{2,1,0:T(8,128)(2,1)S(1)} collective-permute-done((bf16[4,256,384]{2,1,0:T(8,128)(2,1)S(1)}, bf16[4,256,384]{2,1,0:T(8,128)(2,1)S(1)}, u32[]{:S(2)}, u32[]{:S(2)}) %collective-permute-start.5) | collective-permute-done | bytes 786464 | tf_op jit(solution)/shard_map/ppermute | solution.py:523
  60.9 7.0 %collective-permute-done.9.refs_13_.refs_9_ = bf16[2,256,384]{2,1,0:T(8,128)(2,1)S(1)} collective-permute-done((bf16[2,256,384]{2,1,0:T(8,128)(2,1)S(1)}, bf16[2,256,384]{2,1,0:T(8,128)(2,1)S(1)}, u32[]{:S(2)}, u32[]{:S(2)}) %collective-permute-start.9) | collective-permute-done | bytes 393248 | tf_op jit(solution)/shard_map/ppermute | solution.py:523
  67.8 3.6 %collective-permute-done.10.refs_14_.refs_10_ = bf16[2,256,384]{2,1,0:T(8,128)(2,1)S(1)} collective-permute-done((bf16[2,256,384]{2,1,0:T(8,128)(2,1)S(1)}, bf16[2,256,384]{2,1,0:T(8,128)(2,1)S(1)}, u32[]{:S(2)}, u32[]{:S(2)}) %collective-permute-start.10) | collective-permute-done | bytes 393248 | tf_op jit(solution)/shard_map/ppermute | solution.py:523
  72.2 1.0 collective-permute-done.12.refs_16_.refs_12_
  74.0 11.4 %column_first.1 = bf16[8,4,4,2,32,128]{5,4,3,2,1,0:T(8,128)(2,1)} custom-call(s32[1]{0:T(128)} %bitcast.1.refs_0_, s32[1]{0:T(128)} %get-tuple-element.56.refs_1_, bf16[2,512,128]{2,1,0:T(8,128)(2,1)} %get-tuple-element.24.refs_2_, bf16[2,512,128]{2,1,0:T(8,128)(2,1)} %get-tuple-element.39.refs_3_, bf16[2,512,128]{2,1,0:T(8,128)(2,1)} %get-tuple-element.41.refs_4_, ...), custom_call_target="tpu_custom_call" | custom-call | tf_op jit(solution)/shard_map/column_first/pallas_call | solution.py:281
  85.4 52.9 %all_to_all.20.refs_0_ = bf16[32,4,2,32,128]{4,3,2,1,0:T(8,128)(2,1)} all-to-all(bf16[32,4,2,32,128]{4,3,2,1,0:T(8,128)(2,1)} %bitcast.45), channel_id=1, replica_groups=mesh['rows'=8,'cols'=4] {'rows','cols'}, dimensions={0} | all-to-all | bytes 4194304 | tf_op jit(solution)/shard_map/all_to_all | solution.py:517
  138.3 9.6 %row_both.1 = bf16[32,4,2,32,128]{4,3,2,1,0:T(8,128)(2,1)} custom-call(bf16[32,4,2,32,128]{4,3,2,1,0:T(8,128)(2,1)} %all_to_all.20.refs_0_, bf16[4,8,128,128]{3,2,1,0:T(8,128)(2,1)} %copy-done.5, bf16[4,512,256]{2,1,0:T(8,128)(2,1)} %constant.197.clone.refs_2_, f32[8,2,1,512]{3,2,1,0:T(1,128)} %constant.198.clone.refs_3_), custom_call_target="tpu_custom_call" | custom-call | tf_op jit(solution)/shard_map/row_both/pallas_call | solution.py:386
  148.0 4.1 %all-to-all-start.2 = ((bf16[32,4,2,32,128]{4,3,2,1,0:T(8,128)(2,1)}), bf16[32,4,2,32,128]{4,3,2,1,0:T(8,128)(2,1)S(1)}, u32[]{:S(2)}, u32[]{:S(2)}) async-start(bf16[32,4,2,32,128]{4,3,2,1,0:T(8,128)(2,1)} %row_both.1), calls=%async_computation.2 | async-start | bytes 4194304 | tf_op jit(solution)/shard_map/all_to_all | solution.py:517
  152.2 1.5 collective-permute-start.17
  154.2 1.5 collective-permute-start.19
  156.6 17.5 %collective-permute-done.17 = s16[512,256]{1,0:T(8,128)(2,1)S(1)} collective-permute-done((s16[512,256]{1,0:T(8,128)(2,1)S(1)}, s16[512,256]{1,0:T(8,128)(2,1)S(1)}, u32[]{:S(2)}, u32[]{:S(2)}) %collective-permute-start.17) | collective-permute-done | bytes 262176 | tf_op jit(solution)/shard_map/ppermute | solution.py:523
  175.4 8.9 %collective-permute-done.19 = s16[512,256]{1,0:T(8,128)(2,1)S(1)} collective-permute-done((s16[512,256]{1,0:T(8,128)(2,1)S(1)}, s16[512,256]{1,0:T(8,128)(2,1)S(1)}, u32[]{:S(2)}, u32[]{:S(2)}) %collective-permute-start.19) | collective-permute-done | bytes 262176 | tf_op jit(solution)/shard_map/ppermute | solution.py:523
  185.0 1.9 collective-permute-done.20.refs_17_
  186.9 13.0 %all-to-all-done.2 = bf16[32,4,2,32,128]{4,3,2,1,0:T(8,128)(2,1)S(1)} async-done(((bf16[32,4,2,32,128]{4,3,2,1,0:T(8,128)(2,1)}), bf16[32,4,2,32,128]{4,3,2,1,0:T(8,128)(2,1)S(1)}, u32[]{:S(2)}, u32[]{:S(2)}) %all-to-all-start.2) | async-done | bytes 2097184 | tf_op jit(solution)/shard_map/all_to_all | solution.py:517
  199.9 1.3 copy-done
  201.3 15.2 %column_later.1 = bf16[8,4,4,2,32,128]{5,4,3,2,1,0:T(8,128)(2,1)} custom-call(s32[1]{0:T(128)} %bitcast.1.refs_0_, s32[1]{0:T(128)} %get-tuple-element.57.refs_1_, bf16[8,4,4,2,32,128]{5,4,3,2,1,0:T(8,128)(2,1)} %bitcast.43, bf16[4,256,384]{2,1,0:T(8,128)(2,1)} %copy-done.1, bf16[4,256,384]{2,1,0:T(8,128)(2,1)} %copy-done.6, bf16[4,256,384]{2,1,0:T(8,128)(2,1)} %copy-done.2, ...), custom_call_target="tpu_custom_call" | custom-call | tf_op jit(solution)/shard_map/column_later/pallas_call | solution.py:281
  216.5 3.7 %all-to-all-start.3 = ((bf16[32,4,2,32,128]{4,3,2,1,0:T(8,128)(2,1)}), bf16[32,4,2,32,128]{4,3,2,1,0:T(8,128)(2,1)S(1)}, u32[]{:S(2)}, u32[]{:S(2)}) async-start(bf16[32,4,2,32,128]{4,3,2,1,0:T(8,128)(2,1)} %bitcast.44), calls=%async_computation.3 | async-start | bytes 4194304 | tf_op jit(solution)/shard_map/all_to_all | solution.py:517
  220.2 47.9 %all-to-all-done.3.refs_1_ = bf16[32,4,2,32,128]{4,3,2,1,0:T(8,128)(2,1)S(1)} async-done(((bf16[32,4,2,32,128]{4,3,2,1,0:T(8,128)(2,1)}), bf16[32,4,2,32,128]{4,3,2,1,0:T(8,128)(2,1)S(1)}, u32[]{:S(2)}, u32[]{:S(2)}) %all-to-all-start.3) | async-done | bytes 2097184 | tf_op jit(solution)/shard_map/all_to_all | solution.py:517
  268.1 1.3 copy-done.10
  269.4 4.0 %row_last.3 = (bf16[2,8,64,128]{3,2,1,0:T(8,128)(2,1)}, bf16[2,8,64,128]{3,2,1,0:T(8,128)(2,1)}, bf16[2,8,64,128]{3,2,1,0:T(8,128)(2,1)}, bf16[2,8,64,128]{3,2,1,0:T(8,128)(2,1)}) custom-call(s32[1]{0:T(128)} %bitcast.refs_0_, bf16[32,4,2,32,128]{4,3,2,1,0:T(8,128)(2,1)} %copy-done.10, bf16[4,512,256]{2,1,0:T(8,128)(2,1)} %constant.197.clone.refs_2_, ...), custom_call_target="tpu_custom_call" | custom-call | flops 1073741824 | bytes 4194304 | tf_op jit(solution)/shard_map/row_last/pallas_call | solution.py:429
  273.4 2.0 collective-permute-start.25
  275.5 1.5 collective-permute-start.26
  276.9 4.0 %row_last.2 = (bf16[2,8,64,128]{3,2,1,0:T(8,128)(2,1)}, bf16[2,8,64,128]{3,2,1,0:T(8,128)(2,1)}, bf16[2,8,64,128]{3,2,1,0:T(8,128)(2,1)}, bf16[2,8,64,128]{3,2,1,0:T(8,128)(2,1)}) custom-call(s32[1]{0:T(128)} %bitcast.refs_0_, bf16[32,4,2,32,128]{4,3,2,1,0:T(8,128)(2,1)} %copy-done.10, bf16[4,512,256]{2,1,0:T(8,128)(2,1)} %constant.197.clone.refs_2_, ...), custom_call_target="tpu_custom_call" | custom-call | flops 1073741824 | bytes 4194304 | tf_op jit(solution)/shard_map/row_last/pallas_call | solution.py:429
  281.8 1.1 collective-permute-start.22
  283.0 1.5 collective-permute-done.24.refs_2_
  284.5 2.5 collective-permute-start.23
  287.0 6.7 %collective-permute-done.25.refs_3_ = bf16[2,8,64,128]{3,2,1,0:T(8,128)(2,1)S(1)} collective-permute-done((bf16[2,8,64,128]{3,2,1,0:T(8,128)(2,1)}, bf16[2,8,64,128]{3,2,1,0:T(8,128)(2,1)S(1)}, u32[]{:S(2)}, u32[]{:S(2)}) %collective-permute-start.25) | collective-permute-done | bytes 262176 | tf_op jit(solution)/shard_map/ppermute | solution.py:523
  293.7 18.7 %collective-permute-done.26.refs_4_ = bf16[2,8,64,128]{3,2,1,0:T(8,128)(2,1)S(1)} collective-permute-done((bf16[2,8,64,128]{3,2,1,0:T(8,128)(2,1)}, bf16[2,8,64,128]{3,2,1,0:T(8,128)(2,1)S(1)}, u32[]{:S(2)}, u32[]{:S(2)}) %collective-permute-start.26) | collective-permute-done | bytes 262176 | tf_op jit(solution)/shard_map/ppermute | solution.py:523
  313.1 5.3 %closing_order.2.refs_8_ = f32[2,512,1024]{2,1,0:T(8,128)} custom-call(s32[1]{0:T(128)} %bitcast.refs_0_, bf16[2,8,64,128]{3,2,1,0:T(8,128)(2,1)} %get-tuple-element.17.refs_1_, bf16[2,8,64,128]{3,2,1,0:T(8,128)(2,1)} %copy-done.19, bf16[2,8,64,128]{3,2,1,0:T(8,128)(2,1)} %copy-done.21, bf16[2,8,64,128]{3,2,1,0:T(8,128)(2,1)} %copy-done.22, ...), custom_call_target="tpu_custom_call" | custom-call | flops 1073741824 | bytes 4194304 | tf_op jit(solution)/shard_map/closing_order/pallas_call | solution.py:502
  318.5 4.1 %collective-permute-done.23.refs_4_ = bf16[2,8,64,128]{3,2,1,0:T(8,128)(2,1)S(1)} collective-permute-done((bf16[2,8,64,128]{3,2,1,0:T(8,128)(2,1)}, bf16[2,8,64,128]{3,2,1,0:T(8,128)(2,1)S(1)}, u32[]{:S(2)}, u32[]{:S(2)}) %collective-permute-start.23) | collective-permute-done | bytes 262176 | tf_op jit(solution)/shard_map/ppermute | solution.py:523
  323.3 5.3 %closing_order.3 = f32[2,512,1024]{2,1,0:T(8,128)} custom-call(s32[1]{0:T(128)} %bitcast.refs_0_, bf16[2,8,64,128]{3,2,1,0:T(8,128)(2,1)} %get-tuple-element.13.refs_1_, bf16[2,8,64,128]{3,2,1,0:T(8,128)(2,1)} %copy-done.18, bf16[2,8,64,128]{3,2,1,0:T(8,128)(2,1)} %copy-done.20, bf16[2,8,64,128]{3,2,1,0:T(8,128)(2,1)} %copy-done.23, ...), custom_call_target="tpu_custom_call", output_to_operand_aliasing={{}: (8, {})} | custom-call | flops 1073741824 | bytes 4194304 | tf_op jit(solution)/shard_map/closing_order/pallas_call | solution.py:502
  (100 shorter events, 16.1 us)
Async XLA Ops:
  2.6 34.5 %collective-permute-start = (bf16[2,512,256]{2,1,0:T(8,128)(2,1)}, bf16[2,512,256]{2,1,0:T(8,128)(2,1)}, u32[]{:S(2)}, u32[]{:S(2)}) collective-permute-start(bf16[2,512,256]{2,1,0:T(8,128)(2,1)} %get-tuple-element.27), channel_id=1, source_target_pairs={{0,8},{4,12},{8,0},{12,4},{16,24},{20,28},{24,16},{28,20},{1,9},{5... | collective-permute-start | bytes 1572872 | tf_op jit(solution)/shard_map/ppermute | solution.py:523
  4.1 35.4 %collective-permute-start.1 = (bf16[2,512,256]{2,1,0:T(8,128)(2,1)}, bf16[2,512,256]{2,1,0:T(8,128)(2,1)}, u32[]{:S(2)}, u32[]{:S(2)}) collective-permute-start(bf16[2,512,256]{2,1,0:T(8,128)(2,1)} %get-tuple-element.26), channel_id=1, source_target_pairs={{0,16},{4,20},{8,24},{12,28},{16,0},{20,4},{24,8},{28,12},{1,17},{... | collective-permute-start | bytes 1572872 | tf_op jit(solution)/shard_map/ppermute | solution.py:523
  9.5 19.6 %collective-permute-start.13 = (s16[512,256]{1,0:T(8,128)(2,1)}, s16[512,256]{1,0:T(8,128)(2,1)}, u32[]{:S(2)}, u32[]{:S(2)}) collective-permute-start(s16[512,256]{1,0:T(8,128)(2,1)} %get-tuple-element.37), channel_id=1, source_target_pairs={{0,8},{4,12},{8,0},{12,4},{16,24},{20,28},{24,16},{28,20},{1,9},{5... | collective-permute-start | bytes 786440 | tf_op jit(solution)/shard_map/ppermute | solution.py:523
  10.1 22.3 %collective-permute-start.14 = (s16[512,256]{1,0:T(8,128)(2,1)}, s16[512,256]{1,0:T(8,128)(2,1)}, u32[]{:S(2)}, u32[]{:S(2)}) collective-permute-start(s16[512,256]{1,0:T(8,128)(2,1)} %get-tuple-element.36), channel_id=1, source_target_pairs={{0,16},{4,20},{8,24},{12,28},{16,0},{20,4},{24,8},{28,12},{1,17},{... | collective-permute-start | bytes 786440 | tf_op jit(solution)/shard_map/ppermute | solution.py:523
  11.6 22.4 %collective-permute-start.15 = (s16[512,256]{1,0:T(8,128)(2,1)S(1)}, s16[512,256]{1,0:T(8,128)(2,1)}, u32[]{:S(2)}, u32[]{:S(2)}) collective-permute-start(s16[512,256]{1,0:T(8,128)(2,1)S(1)} %get-tuple-element.35), channel_id=1, source_target_pairs={{0,24},{4,28},{8,16},{12,20},{16,8},{20,12},{24,0},{28,4},{1,25},{... | collective-permute-start | bytes 786440 | tf_op jit(solution)/shard_map/ppermute | solution.py:523
  18.2 5.5 %copy-start.24 = (s32[4,3]{1,0:T(4,128)S(1)}, s32[4,3]{1,0:T(4,128)}, u32[]{:S(2)}) copy-start(s32[4,3]{1,0:T(4,128)} %param.18) | copy-start | bytes 148
  18.2 5.5 %copy-start.16 = (bf16[2,4,3,128,128]{4,3,2,1,0:T(8,128)(2,1)S(1)}, bf16[2,4,3,128,128]{4,3,2,1,0:T(8,128)(2,1)}, u32[]{:S(2)}) copy-start(bf16[2,4,3,128,128]{4,3,2,1,0:T(8,128)(2,1)} %param.17) | copy-start | bytes 2359300
  18.2 67.2 %all-to-all-start.1 = ((bf16[4,8,128,128]{3,2,1,0:T(8,128)(2,1)}), bf16[4,8,128,128]{3,2,1,0:T(8,128)(2,1)S(1)}, u32[]{:S(2)}, u32[]{:S(2)}) async-start(bf16[4,8,128,128]{3,2,1,0:T(8,128)(2,1)} %mask_order.1), calls=%async_computation.1 | async-start | bytes 2097152 | tf_op jit(solution)/shard_map/all_to_all | solution.py:517
  24.7 3.1 copy-start.9
  29.1 12.1 %copy-start.1 = (bf16[4,256,384]{2,1,0:T(8,128)(2,1)}, bf16[4,256,384]{2,1,0:T(8,128)(2,1)S(1)}, u32[]{:S(2)}) copy-start(bf16[4,256,384]{2,1,0:T(8,128)(2,1)S(1)} %reshape.39.refs_7_.refs_3_) | copy-start | bytes 2359300
  29.1 16.0 %collective-permute-start.2 = (bf16[2,512,256]{2,1,0:T(8,128)(2,1)}, bf16[2,512,256]{2,1,0:T(8,128)(2,1)S(1)}, u32[]{:S(2)}, u32[]{:S(2)}) collective-permute-start(bf16[2,512,256]{2,1,0:T(8,128)(2,1)} %get-tuple-element.25), channel_id=1, source_target_pairs={{0,24},{4,28},{8,16},{12,20},{16,8},{20,12},{24,0},{28,4},{1,25},{... | collective-permute-start | bytes 1572872 | tf_op jit(solution)/shard_map/ppermute | solution.py:523
  32.3 28.0 %collective-permute-start.4 = (bf16[4,256,384]{2,1,0:T(8,128)(2,1)S(1)}, bf16[4,256,384]{2,1,0:T(8,128)(2,1)S(1)}, u32[]{:S(2)}, u32[]{:S(2)}) collective-permute-start(bf16[4,256,384]{2,1,0:T(8,128)(2,1)S(1)} %reshape.39.refs_7_.refs_3_), channel_id=1, source_target_pairs={{0,4},{4,0},{8,12},{12,8},{16,20},{20,16},{24,28},{28,24},{1,5},{5... | collective-permute-start | bytes 2359304 | tf_op jit(solution)/shard_map/ppermute | solution.py:523
  34.0 24.9 %collective-permute-start.5 = (bf16[4,256,384]{2,1,0:T(8,128)(2,1)S(1)}, bf16[4,256,384]{2,1,0:T(8,128)(2,1)S(1)}, u32[]{:S(2)}, u32[]{:S(2)}) collective-permute-start(bf16[4,256,384]{2,1,0:T(8,128)(2,1)S(1)} %reshape.39.refs_7_.refs_3_), channel_id=1, source_target_pairs={{0,8},{4,12},{8,0},{12,4},{16,24},{20,28},{24,16},{28,20},{1,9},{5... | collective-permute-start | bytes 2359304 | tf_op jit(solution)/shard_map/ppermute | solution.py:523
  37.1 22.6 %collective-permute-start.7 = (bf16[4,256,384]{2,1,0:T(8,128)(2,1)S(1)}, bf16[4,256,384]{2,1,0:T(8,128)(2,1)S(1)}, u32[]{:S(2)}, u32[]{:S(2)}) collective-permute-start(bf16[4,256,384]{2,1,0:T(8,128)(2,1)S(1)} %reshape.39.refs_7_.refs_3_), channel_id=1, source_target_pairs={{0,16},{4,20},{8,24},{12,28},{16,0},{20,4},{24,8},{28,12},{1,17},{... | collective-permute-start | bytes 2359304 | tf_op jit(solution)/shard_map/ppermute | solution.py:523
  39.5 20.3 %collective-permute-start.16 = (s16[4,512,128]{2,1,0:T(8,128)(2,1)S(1)}, s16[4,512,128]{2,1,0:T(8,128)(2,1)}, u32[]{:S(2)}, u32[]{:S(2)}) collective-permute-start(s16[4,512,128]{2,1,0:T(8,128)(2,1)S(1)} %pad_add_fusion), channel_id=1, source_target_pairs={{0,4},{4,0},{8,12},{12,8},{16,20},{20,16},{24,28},{28,24},{1,5},{5... | collective-permute-start | bytes 1572872 | tf_op jit(solution)/shard_map/ppermute | solution.py:523
  46.0 25.5 %copy-start.25 = (s32[2]{0:T(128)S(1)}, s32[2]{0:T(128)}, u32[]{:S(2)}) copy-start(s32[2]{0:T(128)} %param.21) | copy-start | bytes 28
  46.1 26.0 %collective-permute-start.3 = (bf16[4,2,512,128]{3,2,1,0:T(8,128)(2,1)S(1)}, bf16[4,2,512,128]{3,2,1,0:T(8,128)(2,1)S(1)}, u32[]{:S(2)}, u32[]{:S(2)}) collective-permute-start(bf16[4,2,512,128]{3,2,1,0:T(8,128)(2,1)S(1)} %pad_maximum_fusion), channel_id=1, source_target_pairs={{0,4},{4,0},{8,12},{12,8},{16,20},{20,16},{24,28},{28,24},{1,5},{5... | collective-permute-start | bytes 3145736 | tf_op jit(solution)/shard_map/ppermute | solution.py:523
  58.9 14.3 %copy-start.2 = (bf16[4,256,384]{2,1,0:T(8,128)(2,1)}, bf16[4,256,384]{2,1,0:T(8,128)(2,1)S(1)}, u32[]{:S(2)}) copy-start(bf16[4,256,384]{2,1,0:T(8,128)(2,1)S(1)} %collective-permute-done.5.refs_9_.refs_5_) | copy-start | bytes 2359300
  59.0 8.9 %collective-permute-start.9 = (bf16[2,256,384]{2,1,0:T(8,128)(2,1)S(1)}, bf16[2,256,384]{2,1,0:T(8,128)(2,1)S(1)}, u32[]{:S(2)}, u32[]{:S(2)}) collective-permute-start(bf16[2,256,384]{2,1,0:T(8,128)(2,1)S(1)} %slice.24), channel_id=1, source_target_pairs={{0,16},{4,20},{8,24},{12,28},{16,0},{20,4},{24,8},{28,12},{1,17},{... | collective-permute-start | bytes 1179656 | tf_op jit(solution)/shard_map/ppermute | solution.py:523
  59.7 13.5 %copy-start.3 = (bf16[4,256,384]{2,1,0:T(8,128)(2,1)}, bf16[4,256,384]{2,1,0:T(8,128)(2,1)S(1)}, u32[]{:S(2)}) copy-start(bf16[4,256,384]{2,1,0:T(8,128)(2,1)S(1)} %collective-permute-done.7.refs_11_.refs_7_) | copy-start | bytes 2359300
  59.7 12.4 %collective-permute-start.6 = (bf16[4,256,384]{2,1,0:T(8,128)(2,1)S(1)}, bf16[4,256,384]{2,1,0:T(8,128)(2,1)S(1)}, u32[]{:S(2)}, u32[]{:S(2)}) collective-permute-start(bf16[4,256,384]{2,1,0:T(8,128)(2,1)S(1)} %collective-permute-done.5.refs_9_.refs_5_), channel_id=1, source_target_pairs={{0,4},{4,0},{8,12},{12,8},{16,20},{20,16},{24,28},{28,24},{1,5},{5... | collective-permute-start | bytes 2359304 | tf_op jit(solution)/shard_map/ppermute | solution.py:523
  59.8 12.4 %collective-permute-start.8 = (bf16[4,256,384]{2,1,0:T(8,128)(2,1)S(1)}, bf16[4,256,384]{2,1,0:T(8,128)(2,1)S(1)}, u32[]{:S(2)}, u32[]{:S(2)}) collective-permute-start(bf16[4,256,384]{2,1,0:T(8,128)(2,1)S(1)} %collective-permute-done.7.refs_11_.refs_7_), channel_id=1, source_target_pairs={{0,4},{4,0},{8,12},{12,8},{16,20},{20,16},{24,28},{28,24},{1,5},{5... | collective-permute-start | bytes 2359304 | tf_op jit(solution)/shard_map/ppermute | solution.py:523
  60.4 12.9 %copy-start.6 = (bf16[4,256,384]{2,1,0:T(8,128)(2,1)}, bf16[4,256,384]{2,1,0:T(8,128)(2,1)S(1)}, u32[]{:S(2)}) copy-start(bf16[4,256,384]{2,1,0:T(8,128)(2,1)S(1)} %collective-permute-done.4.refs_8_.refs_4_) | copy-start | bytes 2359300
  60.4 11.1 %collective-permute-start.10 = (bf16[2,256,384]{2,1,0:T(8,128)(2,1)S(1)}, bf16[2,256,384]{2,1,0:T(8,128)(2,1)S(1)}, u32[]{:S(2)}, u32[]{:S(2)}) collective-permute-start(bf16[2,256,384]{2,1,0:T(8,128)(2,1)S(1)} %slice.25), channel_id=1, source_target_pairs={{0,8},{4,12},{8,0},{12,4},{16,24},{20,28},{24,16},{28,20},{1,9},{5... | collective-permute-start | bytes 1179656 | tf_op jit(solution)/shard_map/ppermute | solution.py:523
  67.8 5.4 %copy-start.11 = (bf16[2,256,384]{2,1,0:T(8,128)(2,1)}, bf16[2,256,384]{2,1,0:T(8,128)(2,1)S(1)}, u32[]{:S(2)}) copy-start(bf16[2,256,384]{2,1,0:T(8,128)(2,1)S(1)} %collective-permute-done.9.refs_13_.refs_9_) | copy-start | bytes 1179652
  67.8 4.3 %collective-permute-start.11 = (bf16[2,256,384]{2,1,0:T(8,128)(2,1)S(1)}, bf16[2,256,384]{2,1,0:T(8,128)(2,1)S(1)}, u32[]{:S(2)}, u32[]{:S(2)}) collective-permute-start(bf16[2,256,384]{2,1,0:T(8,128)(2,1)S(1)} %collective-permute-done.9.refs_13_.refs_9_), channel_id=1, source_target_pairs={{0,4},{4,0},{8,12},{12,8},{16,20},{20,16},{24,28},{28,24},{1,5},{5... | collective-permute-start | bytes 1179656 | tf_op jit(solution)/shard_map/ppermute | solution.py:523
  71.5 1.8 copy-start.12
  71.5 1.7 collective-permute-start.12
  72.2 1.6 copy-start.13
  85.4 52.9 %copy-start.5 = (bf16[4,8,128,128]{3,2,1,0:T(8,128)(2,1)}, bf16[4,8,128,128]{3,2,1,0:T(8,128)(2,1)S(1)}, u32[]{:S(2)}) copy-start(bf16[4,8,128,128]{3,2,1,0:T(8,128)(2,1)S(1)} %all-to-all-done.1.refs_1_) | copy-start | bytes 3145732
  147.9 4.1 %copy-start.4 = (s16[1,512,1024]{2,1,0:T(8,128)(2,1)S(1)}, s16[1,512,1024]{2,1,0:T(8,128)(2,1)}, u32[]{:S(2)}) copy-start(s16[1,512,1024]{2,1,0:T(8,128)(2,1)} %get-tuple-element.21) | copy-start | bytes 3145732
  148.0 52.0 %all-to-all-start.2 = ((bf16[32,4,2,32,128]{4,3,2,1,0:T(8,128)(2,1)}), bf16[32,4,2,32,128]{4,3,2,1,0:T(8,128)(2,1)S(1)}, u32[]{:S(2)}, u32[]{:S(2)}) async-start(bf16[32,4,2,32,128]{4,3,2,1,0:T(8,128)(2,1)} %row_both.1), calls=%async_computation.2 | async-start | bytes 4194304 | tf_op jit(solution)/shard_map/all_to_all | solution.py:517
  152.2 21.9 %collective-permute-start.17 = (s16[512,256]{1,0:T(8,128)(2,1)S(1)}, s16[512,256]{1,0:T(8,128)(2,1)S(1)}, u32[]{:S(2)}, u32[]{:S(2)}) collective-permute-start(s16[512,256]{1,0:T(8,128)(2,1)S(1)} %get-tuple-element.32), channel_id=1, source_target_pairs={{0,8},{4,12},{8,0},{12,4},{16,24},{20,28},{24,16},{28,20},{1,9},{5... | collective-permute-start | bytes 786440 | tf_op jit(solution)/shard_map/ppermute | solution.py:523
  153.7 21.0 %collective-permute-start.18 = (s16[512,256]{1,0:T(8,128)(2,1)S(1)}, s16[512,256]{1,0:T(8,128)(2,1)S(1)}, u32[]{:S(2)}, u32[]{:S(2)}) collective-permute-start(s16[512,256]{1,0:T(8,128)(2,1)S(1)} %get-tuple-element.31), channel_id=1, source_target_pairs={{0,16},{4,20},{8,24},{12,28},{16,0},{20,4},{24,8},{28,12},{1,17},{... | collective-permute-start | bytes 786440 | tf_op jit(solution)/shard_map/ppermute | solution.py:523
  154.2 30.0 %collective-permute-start.19 = (s16[512,256]{1,0:T(8,128)(2,1)S(1)}, s16[512,256]{1,0:T(8,128)(2,1)S(1)}, u32[]{:S(2)}, u32[]{:S(2)}) collective-permute-start(s16[512,256]{1,0:T(8,128)(2,1)S(1)} %get-tuple-element.30), channel_id=1, source_target_pairs={{0,24},{4,28},{8,16},{12,20},{16,8},{20,12},{24,0},{28,4},{1,25},{... | collective-permute-start | bytes 786440 | tf_op jit(solution)/shard_map/ppermute | solution.py:523
  185.0 2.0 collective-permute-start.20
  186.9 13.0 %copy-start.17 = (s16[4,512,128]{2,1,0:T(8,128)(2,1)}, s16[4,512,128]{2,1,0:T(8,128)(2,1)S(1)}, u32[]{:S(2)}) copy-start(s16[4,512,128]{2,1,0:T(8,128)(2,1)S(1)} %collective-permute-done.20.refs_17_) | copy-start | bytes 1572868
  216.5 51.6 %all-to-all-start.3 = ((bf16[32,4,2,32,128]{4,3,2,1,0:T(8,128)(2,1)}), bf16[32,4,2,32,128]{4,3,2,1,0:T(8,128)(2,1)S(1)}, u32[]{:S(2)}, u32[]{:S(2)}) async-start(bf16[32,4,2,32,128]{4,3,2,1,0:T(8,128)(2,1)} %bitcast.44), calls=%async_computation.3 | async-start | bytes 4194304 | tf_op jit(solution)/shard_map/all_to_all | solution.py:517
  273.4 11.1 %collective-permute-start.24 = (bf16[2,8,64,128]{3,2,1,0:T(8,128)(2,1)}, bf16[2,8,64,128]{3,2,1,0:T(8,128)(2,1)S(1)}, u32[]{:S(2)}, u32[]{:S(2)}) collective-permute-start(bf16[2,8,64,128]{3,2,1,0:T(8,128)(2,1)} %get-tuple-element.18), channel_id=1, source_target_pairs={{0,1},{1,0},{2,3},{3,2},{4,5},{5,4},{6,7},{7,6},{8,9},{9,8},{10,11... | collective-permute-start | bytes 786440 | tf_op jit(solution)/shard_map/ppermute | solution.py:523
  273.4 20.3 %collective-permute-start.25 = (bf16[2,8,64,128]{3,2,1,0:T(8,128)(2,1)}, bf16[2,8,64,128]{3,2,1,0:T(8,128)(2,1)S(1)}, u32[]{:S(2)}, u32[]{:S(2)}) collective-permute-start(bf16[2,8,64,128]{3,2,1,0:T(8,128)(2,1)} %get-tuple-element.19), channel_id=1, source_target_pairs={{0,2},{1,3},{2,0},{3,1},{4,6},{5,7},{6,4},{7,5},{8,10},{9,11},{10,... | collective-permute-start | bytes 786440 | tf_op jit(solution)/shard_map/ppermute | solution.py:523
  275.5 37.0 %collective-permute-start.26 = (bf16[2,8,64,128]{3,2,1,0:T(8,128)(2,1)}, bf16[2,8,64,128]{3,2,1,0:T(8,128)(2,1)S(1)}, u32[]{:S(2)}, u32[]{:S(2)}) collective-permute-start(bf16[2,8,64,128]{3,2,1,0:T(8,128)(2,1)} %get-tuple-element.20), channel_id=1, source_target_pairs={{0,3},{1,2},{2,1},{3,0},{4,7},{5,6},{6,5},{7,4},{8,11},{9,10},{10,... | collective-permute-start | bytes 786440 | tf_op jit(solution)/shard_map/ppermute | solution.py:523
  280.9 37.5 %collective-permute-start.21 = (bf16[2,8,64,128]{3,2,1,0:T(8,128)(2,1)}, bf16[2,8,64,128]{3,2,1,0:T(8,128)(2,1)S(1)}, u32[]{:S(2)}, u32[]{:S(2)}) collective-permute-start(bf16[2,8,64,128]{3,2,1,0:T(8,128)(2,1)} %get-tuple-element.14), channel_id=1, source_target_pairs={{0,1},{1,0},{2,3},{3,2},{4,5},{5,4},{6,7},{7,6},{8,9},{9,8},{10,11... | collective-permute-start | bytes 786440 | tf_op jit(solution)/shard_map/ppermute | solution.py:523
  281.8 36.6 %collective-permute-start.22 = (bf16[2,8,64,128]{3,2,1,0:T(8,128)(2,1)}, bf16[2,8,64,128]{3,2,1,0:T(8,128)(2,1)S(1)}, u32[]{:S(2)}, u32[]{:S(2)}) collective-permute-start(bf16[2,8,64,128]{3,2,1,0:T(8,128)(2,1)} %get-tuple-element.15), channel_id=1, source_target_pairs={{0,2},{1,3},{2,0},{3,1},{4,6},{5,7},{6,4},{7,5},{8,10},{9,11},{10,... | collective-permute-start | bytes 786440 | tf_op jit(solution)/shard_map/ppermute | solution.py:523
  284.5 27.9 %copy-start.19 = (bf16[2,8,64,128]{3,2,1,0:T(8,128)(2,1)}, bf16[2,8,64,128]{3,2,1,0:T(8,128)(2,1)S(1)}, u32[]{:S(2)}) copy-start(bf16[2,8,64,128]{3,2,1,0:T(8,128)(2,1)S(1)} %collective-permute-done.24.refs_2_) | copy-start | bytes 786436
  284.5 38.1 %collective-permute-start.23 = (bf16[2,8,64,128]{3,2,1,0:T(8,128)(2,1)}, bf16[2,8,64,128]{3,2,1,0:T(8,128)(2,1)S(1)}, u32[]{:S(2)}, u32[]{:S(2)}) collective-permute-start(bf16[2,8,64,128]{3,2,1,0:T(8,128)(2,1)} %get-tuple-element.16), channel_id=1, source_target_pairs={{0,3},{1,2},{2,1},{3,0},{4,7},{5,6},{6,5},{7,4},{8,11},{9,10},{10,... | collective-permute-start | bytes 786440 | tf_op jit(solution)/shard_map/ppermute | solution.py:523
  293.7 18.8 %copy-start.21 = (bf16[2,8,64,128]{3,2,1,0:T(8,128)(2,1)}, bf16[2,8,64,128]{3,2,1,0:T(8,128)(2,1)S(1)}, u32[]{:S(2)}) copy-start(bf16[2,8,64,128]{3,2,1,0:T(8,128)(2,1)S(1)} %collective-permute-done.25.refs_3_) | copy-start | bytes 786436
  318.5 4.1 %copy-start.18 = (bf16[2,8,64,128]{3,2,1,0:T(8,128)(2,1)}, bf16[2,8,64,128]{3,2,1,0:T(8,128)(2,1)S(1)}, u32[]{:S(2)}) copy-start(bf16[2,8,64,128]{3,2,1,0:T(8,128)(2,1)S(1)} %collective-permute-done.21.refs_2_) | copy-start | bytes 786436
  318.5 4.1 %copy-start.20 = (bf16[2,8,64,128]{3,2,1,0:T(8,128)(2,1)}, bf16[2,8,64,128]{3,2,1,0:T(8,128)(2,1)S(1)}, u32[]{:S(2)}) copy-start(bf16[2,8,64,128]{3,2,1,0:T(8,128)(2,1)S(1)} %collective-permute-done.22.refs_3_) | copy-start | bytes 786436
  (8 other events, 8.7 us)

commit v4 on v3

--- a/solution.py
+++ b/solution.py
@@ -15,7 +15,7 @@
 BOUNCES = 2
 GROUP = 4
 ANGLE_STEPS = 10430.0
-VMEM_LIMIT = 56 * 1024 * 1024
+VMEM_LIMIT = 62 * 1024 * 1024
 BF16 = jnp.bfloat16
 F32 = jnp.float32
 
@@ -152,8 +152,8 @@
         groups.append(refs[:count])
         refs = refs[count:]
     current, *mats, angles, tables = groups
-    out_ref, padded, wave, mixed, held_mats, held_angles = refs[:6]
-    held_tables, sems = refs[6:-1], refs[-1]
+    out_ref, padded, wave, mixed, held_current, held_mats, held_angles, held_out = refs[:8]
+    held_tables, sems = refs[8:-1], refs[-1]
     rows_at, cols_at, firsts, _, seconds, width = out_ref.shape
     extent = wave.shape[1]
     part = extent // RADIX
@@ -168,7 +168,19 @@
         copies.append(copy)
         return copy
 
-    table_copies = [fetch(tables[-1], held_tables[-1])] if later else []
+    def fetch_table(number, group):
+        mine = pl.ds(group * firsts, firsts)
+        return fetch(tables[number].at[mine], held_tables[number].at[mine])
+
+    if later:
+        current_copies = []
+        for group in range(cols_at):
+            some = [fetch(current[0].at[:, group], held_current.at[:, group]), fetch_table(1, group)]
+            current_copies.append(some)
+    else:
+        current_copies = [
+            fetch(by_distance(current, at), held_current.at[at]) for at in range(peers)
+        ]
     mat_copies, angle_copies = [], []
     for at in range(peers):
         first, some = 0, []
@@ -177,25 +189,26 @@
             first += piece.shape[0]
         mat_copies.append(some)
         angle_copies.append(fetch(by_distance(angles, at), held_angles.at[at]))
-    table_copies.append(fetch(tables[0], held_tables[0]))
+    table_copies = [fetch_table(0, group) for group in range(cols_at)]
 
     padded[:, pl.ds(0, height)] = jnp.zeros((2, height, width), F32)
     padded[:, pl.ds(height + extent, height)] = jnp.zeros((2, height, width), F32)
 
     if later:
-        cur_ref = current[0]
-        table_copies[0].wait()
-
-        def unfold(at):
-            group, first = at // firsts, at % firsts
-            real = cur_ref[:, group, first, 0].reshape(part, width)
-            imag = cur_ref[:, group, first, 1].reshape(part, width)
-            got = dot(held_tables[-1][at], jnp.concatenate([real, imag], axis=1))
-            rows = aligned(at * part, part)
-            wave[0, rows] = got[:part, :width] + got[part:, width:]
-            wave[1, rows] = got[:part, width:] - got[part:, :width]
-
-        loop(RADIX, unfold, 8)
+        for group in range(cols_at):
+            for copy in current_copies[group]:
+                copy.wait()
+
+            def unfold(first, group=group):
+                at = group * firsts + first
+                real = held_current[:, group, first, 0].reshape(part, width)
+                imag = held_current[:, group, first, 1].reshape(part, width)
+                got = dot(held_tables[-1][at], jnp.concatenate([real, imag], axis=1))
+                rows = aligned(at * part, part)
+                wave[0, rows] = got[:part, :width] + got[part:, width:]
+                wave[1, rows] = got[:part, width:] - got[part:, :width]
+
+            loop(firsts, unfold, firsts)
 
         def gather(at):
             values = [
@@ -211,9 +224,9 @@
     else:
         for at in range(peers):
             rows = aligned(height + (place_ref[0] ^ at) * height, height)
-            piece = by_distance(current, at)
-            padded[0, rows] = piece[0].astype(F32)
-            padded[1, rows] = piece[1].astype(F32)
+            current_copies[at].wait()
+            padded[0, rows] = held_current[at, 0].astype(F32)
+            padded[1, rows] = held_current[at, 1].astype(F32)
 
     shift = shift_ref[0]
     for at in range(peers):
@@ -252,17 +265,21 @@
             mixed[one, aligned(at * 16, 16)] = jnp.concatenate([real, imag], axis=1).astype(BF16)
 
     loop(part // 16, mix)
-    table_copies[-1].wait()
-
-    def fold(at):
-        group, first = at // firsts, at % firsts
-        got = dot(held_tables[0][at], mixed[at])
-        real = (got[:part, :width] - got[part:, width:]).astype(BF16)
-        imag = (got[:part, width:] + got[part:, :width]).astype(BF16)
-        out_ref[:, group, first, 0] = real.reshape(rows_at, seconds, width)
-        out_ref[:, group, first, 1] = imag.reshape(rows_at, seconds, width)
-
-    loop(RADIX, fold, 8)
+    for group in range(cols_at):
+        table_copies[group].wait()
+
+        def fold(first, group=group):
+            at = group * firsts + first
+            got = dot(held_tables[0][at], mixed[at])
+            real = (got[:part, :width] - got[part:, width:]).astype(BF16)
+            imag = (got[:part, width:] + got[part:, :width]).astype(BF16)
+            held_out[:, group, first, 0] = real.reshape(rows_at, seconds, width)
+            held_out[:, group, first, 1] = imag.reshape(rows_at, seconds, width)
+
+        loop(firsts, fold, firsts)
+        fetch(held_out.at[:, group], out_ref.at[:, group])
+    for copy in copies[-cols_at:]:
+        copy.wait()
 
 
 def column_work(later, place, shift, current, mats, angles, tables, col_count):
@@ -272,7 +289,9 @@
     part = extent // RADIX
     groups = [[current] if later else current, *mats, angles, tables if later else tables[:1]]
     counts = [len(group) for group in groups]
-    copies = sum(counts[1:-2]) + peers + counts[-1]
+    sent = jax.ShapeDtypeStruct((peers, col_count, RADIX // col_count, 2, part // peers, width), BF16)
+    held = sent.shape if later else (peers, 2, height, width)
+    copies = sum(counts[1:-2]) + peers + (4 if later else 2) * col_count + peers
 
     def body(*refs):
         column_body(later, peers, counts, *refs)
@@ -280,15 +299,17 @@
     smem, anywhere = pl.BlockSpec(memory_space=pltpu.SMEM), pl.BlockSpec(memory_space=pl.ANY)
     return pl.pallas_call(
         body,
-        out_shape=jax.ShapeDtypeStruct((peers, col_count, RADIX // col_count, 2, part // peers, width), BF16),
-        in_specs=[smem, smem] + vmem(counts[0]) + [anywhere] * sum(counts[1:]),
-        out_specs=vmem(1)[0],
+        out_shape=sent,
+        in_specs=[smem, smem] + [anywhere] * sum(counts),
+        out_specs=anywhere,
         scratch_shapes=[
             pltpu.VMEM((2, extent + 2 * height, width), F32),
             pltpu.VMEM((2, extent, width), F32),
             pltpu.VMEM((RADIX, part, 2 * width), BF16),
+            pltpu.VMEM(held, BF16),
             pltpu.VMEM((peers, height // BLOCK, 2 * BLOCK, 3 * BLOCK), BF16),
             pltpu.VMEM((peers, height, width), angles[0].dtype),
+            pltpu.VMEM(sent.shape, BF16),
             *[pltpu.VMEM(table.shape, BF16) for table in groups[-1]],
             pltpu.SemaphoreType.DMA((copies,)),
         ],
@@ -297,7 +318,7 @@
     )(place, shift, *[one for group in groups for one in group])
 
 
-def row_mix(order, in_ref, turn_ref, mixed):
+def row_mix(order, in_ref, turn_ref, mixed, arrived):
     blocks, firsts, _, seconds, lanes = in_ref.shape
     radix, _, _, part = mixed.shape
     tiles = part // lanes
@@ -315,11 +336,13 @@
                 ]
                 for one, (real, imag) in enumerate(butterfly(values, 1)):
                     cosine, sine = turn_ref[one, 0, :, across], turn_ref[one, 1, :, across]
-                    down = pl.multiple_of(first * seconds + at, 16)
+                    down = first * seconds + at
                     mixed[one, 0, pl.ds(down, 16), across] = (real * cosine - imag * sine).astype(BF16)
                     mixed[one, 1, pl.ds(down, 16), across] = (real * sine + imag * cosine).astype(BF16)
 
-    loop(firsts, one_first, 4)
+    for first in range(firsts):
+        arrived(first)
+        one_first(first)
 
 
 def core_dot(left, tile_ref, sign):
@@ -332,13 +355,20 @@
     return first[..., :lanes] + second[..., lanes:], second[..., :lanes] - first[..., lanes:]
 
 
-def row_body(order, in_ref, mask_ref, core_ref, turn_ref, out_ref, mixed, passed, back):
+def row_body(order, in_any, mask_any, core_any, turn_ref, out_any, mixed, passed, back, in_ref, mask_ref, core_ref, out_ref, sems):
     blocks, firsts, _, seconds, lanes = in_ref.shape
+    copies = [pltpu.make_async_copy(in_any.at[:, one], in_ref.at[:, one], sems.at[one]) for one in range(firsts)]
+    copies.append(pltpu.make_async_copy(core_any, core_ref, sems.at[firsts]))
+    copies.append(pltpu.make_async_copy(mask_any, mask_ref, sems.at[firsts + 1]))
+    for copy in copies:
+        copy.start()
     radix, _, _, part = mixed.shape
     tiles = part // lanes
     rows = firsts * seconds
-    row_mix(order, in_ref, turn_ref, mixed)
+    row_mix(order, in_ref, turn_ref, mixed, lambda first: copies[first].wait())
     at_once = min(GROUP, radix)
+    copies[firsts].wait()
+    copies[firsts + 1].wait()
 
     for group in range(0, radix, at_once):
         these = pl.ds(group, at_once)
@@ -365,13 +395,20 @@
         for tile in range(tiles):
             across = pl.ds(tile * lanes, lanes)
             for at in range(0, seconds, 16):
-                down = aligned(first * seconds + at, 16)
+                down = pl.ds(first * seconds + at, 16)
                 values = [(back[one, 0, down, across], back[one, 1, down, across]) for one in range(radix)]
                 for one, (real, imag) in enumerate(butterfly(values, -1)):
                     out_ref[order[one * tiles + tile], first, 0, pl.ds(at, 16)] = real.astype(BF16)
                     out_ref[order[one * tiles + tile], first, 1, pl.ds(at, 16)] = imag.astype(BF16)
 
-    loop(firsts, close, 2)
+    back_copies = []
+    for first in range(firsts):
+        close(first)
+        copy = pltpu.make_async_copy(out_ref.at[:, first], out_any.at[:, first], sems.at[firsts + 2 + first])
+        copy.start()
+        back_copies.append(copy)
+    for copy in back_copies:
+        copy.wait()
 
 
 def row_work(order, received, mask, tables):
@@ -380,32 +417,45 @@
     radix, part = turns.shape[0], core.shape[1]
     rows = firsts * seconds
 
+    anywhere = pl.BlockSpec(memory_space=pl.ANY)
+
     def body(*refs):
         row_body(order, *refs)
 
     return pl.pallas_call(
         body,
         out_shape=jax.ShapeDtypeStruct(received.shape, BF16),
-        in_specs=vmem(4),
-        out_specs=vmem(1)[0],
+        in_specs=[anywhere, anywhere, anywhere, vmem(1)[0]],
+        out_specs=anywhere,
         scratch_shapes=[
             pltpu.VMEM((radix, 2, rows, part), BF16),
             pltpu.VMEM((radix, 2, rows, part), BF16),
             pltpu.VMEM((radix, 2, rows, part), F32),
+            *[pltpu.VMEM(one.shape, BF16) for one in (received, mask, core, received)],
+            pltpu.SemaphoreType.DMA((2 * firsts + 2,)),
         ],
         compiler_params=params(),
         name="row_both",
     )(received, mask, core, turns)
 
 
-def last_row_body(order, place_ref, in_ref, core_ref, turn_ref, *refs):
-    mixed = refs[-1]
+def last_row_body(order, number, place_ref, in_any, core_any, turn_ref, *refs):
+    outs, (mixed, in_ref, core_ref, sems) = refs[:-4], refs[-4:]
+    firsts, seconds = in_ref.shape[1], in_ref.shape[3]
+    these = pl.ds(number * seconds, seconds)
+    copies = [
+        pltpu.make_async_copy(in_any.at[:, one, :, these], in_ref.at[:, one], sems.at[one]) for one in range(firsts)
+    ]
+    copies.append(pltpu.make_async_copy(core_any, core_ref, sems.at[firsts]))
+    for copy in copies:
+        copy.start()
     radix = mixed.shape[0]
     at_once = min(GROUP, radix)
-    row_mix(order, in_ref, turn_ref, mixed)
+    row_mix(order, in_ref, turn_ref, mixed, lambda first: copies[first].wait())
+    copies[firsts].wait()
     for group in range(0, radix, at_once):
         these = pl.ds(group, at_once)
-        for distance, out_ref in enumerate(refs[:-1]):
+        for distance, out_ref in enumerate(outs):
             real, imag = core_dot(mixed[these], core_ref[place_ref[0] ^ distance], 1)
             out_ref[0, these] = real.astype(BF16)
             out_ref[1, these] = imag.astype(BF16)
@@ -419,20 +469,25 @@
     rows = firsts * seconds
 
     def body(*refs):
-        last_row_body(order, *refs)
+        last_row_body(order, number, *refs)
 
     def whole(array):
         return pl.BlockSpec(array.shape, lambda i: (0,) * array.ndim)
 
-    given = pl.BlockSpec((blocks, firsts, 2, seconds, lanes), lambda i: (0, 0, 0, number, 0))
+    anywhere = pl.BlockSpec(memory_space=pl.ANY)
     sent = jax.ShapeDtypeStruct((2, radix, rows, lanes), BF16)
     return pl.pallas_call(
         body,
         grid=(1,),
         out_shape=[sent] * (part // lanes),
-        in_specs=[pl.BlockSpec(memory_space=pltpu.SMEM), given, whole(core), whole(turns)],
+        in_specs=[pl.BlockSpec(memory_space=pltpu.SMEM), anywhere, anywhere, whole(turns)],
         out_specs=[whole(sent)] * (part // lanes),
-        scratch_shapes=[pltpu.VMEM((radix, 2, rows, part), BF16)],
+        scratch_shapes=[
+            pltpu.VMEM((radix, 2, rows, part), BF16),
+            pltpu.VMEM((blocks, firsts, 2, seconds, lanes), BF16),
+            pltpu.VMEM(core.shape, BF16),
+            pltpu.SemaphoreType.DMA((firsts + 1,)),
+        ],
         compiler_params=params(),
         cost_estimate=pl.CostEstimate(flops=8 * rows * part * part * radix, bytes_accessed=2**22, transcendentals=0),
         name="row_last",

time: 330 us -> 325 us (0.985)
  transfers between devices with their start and end apart: 30 -> 30, of which waited for: 15 -> 14; matrix products, arithmetic and copies ran while one was open for 7% -> 7% of each run, Pallas kernels for 8% -> 8%
where the time goes in v4:
time: 325 us; the launch traced here: 324 us
  waiting for transfers between devices  147 us (45%)
  Pallas kernels  57.6 us (18%)
  blocking collectives  52.9 us (16%)
  starting transfers between devices  35.9 us (11%)
  local copies, waits for them, and re-layouts  26.5 us (8%)
    ppermute x27, waiting for transfers between devices, swap(): lax.ppermute(value, axis, [(at, at ^ distance) for at in range(lax.axis_s...  86.3 us
    all_to_all x3, waiting for transfers between devices, exchange(): return lax.all_to_all(value, axis, split_axis=0, concat_axis=0, tiled=True)  61.1 us
    all_to_all x1, blocking collectives, exchange(): return lax.all_to_all(value, axis, split_axis=0, concat_axis=0, tiled=True)  52.9 us
    pallas_call x2, Pallas kernels, column_work(): pl.pallas_call(body, out_shape=sent, in_specs=[smem, smem] + [anywhere] *...  23.7 us
    ppermute x27, starting transfers between devices, swap(): lax.ppermute(value, axis, [(at, at ^ distance) for at in range(lax.axis_s...  22.4 us
    all_to_all x3, starting transfers between devices, exchange(): return lax.all_to_all(value, axis, split_axis=0, concat_axis=0, tiled=True)  13.4 us
    another operation x10, local copies, waits for them, and re-layouts, spread(): jnp.stack([part(piece, 1 - core) for piece in chips])  13.4 us
    pallas_call x2, Pallas kernels, closing_work(): pl.pallas_call(body, grid=(1,), out_shape=jax.ShapeDtypeStruct((2, height...  10.7 us
  transfers between devices with their start and end apart: 30, of which 14 were waited for; matrix products, arithmetic and copies ran while one was open for 7% of the time, Pallas kernels for 8%

profile of v4, /device:TPU:12, one launch (start us, length us, event | category | flops | bytes accessed | tf_op | source)
XLA Modules:
  0.0 323.9 jit_solution(5197098604822636434)
XLA Ops:
  0.0 2.6 constant_dynamic-slice_fusion.9
  2.6 1.5 collective-permute-start
  4.6 2.9 round-nearest-even_convert_fusion
  7.5 1.2 fusion
  8.6 0.9 dynamic-slice_bitcast_fusion.3
  10.1 1.5 collective-permute-start.14
  11.6 1.4 collective-permute-start.15
  13.1 5.2 %mask_order.1 = bf16[4,8,128,128]{3,2,1,0:T(8,128)(2,1)} custom-call(f32[512,1024]{1,0:T(8,128)} %refs_5_.3, bf16[512,512]{1,0:T(8,128)(2,1)} %constant.199.clone.down_ref, bf16[1024,1024]{1,0:T(8,128)(2,1)} %constant.200.clone.across_ref), custom_call_target="tpu_custom_call" | custom-call | tf_op jit(solution)/shard_map/mask_order/pallas_call | solution.py:510
  18.3 5.4 %all-to-all-start.1 = ((bf16[4,8,128,128]{3,2,1,0:T(8,128)(2,1)}), bf16[4,8,128,128]{3,2,1,0:T(8,128)(2,1)}, u32[]{:S(2)}, u32[]{:S(2)}) async-start(bf16[4,8,128,128]{3,2,1,0:T(8,128)(2,1)} %mask_order.1), calls=%async_computation.1 | async-start | bytes 2097152 | tf_op jit(solution)/shard_map/all_to_all | solution.py:572
  23.9 2.1 dynamic-slice_bitcast_fusion.9
  28.3 1.6 collective-permute-start.2
  29.9 1.7 dynamic-slice_bitcast_fusion.16
  31.5 1.6 dynamic-slice_bitcast_fusion.15
  33.2 1.5 collective-permute-start.5
  34.7 1.6 dynamic-slice_bitcast_fusion.14
  36.8 1.8 dynamic-slice_bitcast_fusion.8
  38.6 1.8 dynamic-slice_bitcast_fusion.7
  40.4 3.9 %collective-permute-done.2 = bf16[2,512,256]{2,1,0:T(8,128)(2,1)S(1)} collective-permute-done((bf16[2,512,256]{2,1,0:T(8,128)(2,1)}, bf16[2,512,256]{2,1,0:T(8,128)(2,1)S(1)}, u32[]{:S(2)}, u32[]{:S(2)}) %collective-permute-start.2) | collective-permute-done | bytes 524320 | tf_op jit(solution)/shard_map/ppermute | solution.py:578
  45.4 12.8 %collective-permute-done.5.refs_9_.refs_5_ = bf16[4,256,384]{2,1,0:T(8,128)(2,1)S(1)} collective-permute-done((bf16[4,256,384]{2,1,0:T(8,128)(2,1)S(1)}, bf16[4,256,384]{2,1,0:T(8,128)(2,1)S(1)}, u32[]{:S(2)}, u32[]{:S(2)}) %collective-permute-start.5) | collective-permute-done | bytes 786464 | tf_op jit(solution)/shard_map/ppermute | solution.py:578
  60.1 7.0 %collective-permute-done.9.refs_13_.refs_9_ = bf16[2,256,384]{2,1,0:T(8,128)(2,1)S(1)} collective-permute-done((bf16[2,256,384]{2,1,0:T(8,128)(2,1)S(1)}, bf16[2,256,384]{2,1,0:T(8,128)(2,1)S(1)}, u32[]{:S(2)}, u32[]{:S(2)}) %collective-permute-start.9) | collective-permute-done | bytes 393248 | tf_op jit(solution)/shard_map/ppermute | solution.py:578
  67.0 3.7 %collective-permute-done.10.refs_14_.refs_10_ = bf16[2,256,384]{2,1,0:T(8,128)(2,1)S(1)} collective-permute-done((bf16[2,256,384]{2,1,0:T(8,128)(2,1)S(1)}, bf16[2,256,384]{2,1,0:T(8,128)(2,1)S(1)}, u32[]{:S(2)}, u32[]{:S(2)}) %collective-permute-start.10) | collective-permute-done | bytes 393248 | tf_op jit(solution)/shard_map/ppermute | solution.py:578
  71.4 1.2 copy-done.5
  74.4 10.6 %column_first.1 = bf16[8,4,4,2,32,128]{5,4,3,2,1,0:T(8,128)(2,1)} custom-call(s32[1]{0:T(128)} %bitcast.1.refs_0_, s32[1]{0:T(128)} %get-tuple-element.56.refs_1_, bf16[2,512,128]{2,1,0:T(8,128)(2,1)} %get-tuple-element.24.refs_2_, bf16[2,512,128]{2,1,0:T(8,128)(2,1)} %get-tuple-element.39.refs_3_, bf16[2,512,128]{2,1,0:T(8,128)(2,1)} %get-tuple-element.41.refs_4_, ...), custom_call_target="tpu_custom_call" | custom-call | tf_op jit(solution)/shard_map/column_first/pallas_call | solution.py:300
  85.1 52.9 %all_to_all.20.refs_0_ = bf16[32,4,2,32,128]{4,3,2,1,0:T(8,128)(2,1)} all-to-all(bf16[32,4,2,32,128]{4,3,2,1,0:T(8,128)(2,1)} %bitcast.44), channel_id=1, replica_groups=mesh['rows'=8,'cols'=4] {'rows','cols'}, dimensions={0} | all-to-all | bytes 4194304 | tf_op jit(solution)/shard_map/all_to_all | solution.py:572
  138.0 9.1 %row_both.1 = bf16[32,4,2,32,128]{4,3,2,1,0:T(8,128)(2,1)} custom-call(bf16[32,4,2,32,128]{4,3,2,1,0:T(8,128)(2,1)} %all_to_all.20.refs_0_, bf16[4,8,128,128]{3,2,1,0:T(8,128)(2,1)} %all-to-all-done.1.refs_1_, bf16[4,512,256]{2,1,0:T(8,128)(2,1)} %constant.197.clone.refs_2_, f32[8,2,1,512]{3,2,1,0:T(1,128)} %constant.198.clone.refs_3_), custom_call_target="tpu_custom_call" | custom-call | tf_op jit(solution)/shard_map/row_both/pallas_call | solution.py:425
  147.1 4.1 %all-to-all-start.2 = ((bf16[32,4,2,32,128]{4,3,2,1,0:T(8,128)(2,1)}), bf16[32,4,2,32,128]{4,3,2,1,0:T(8,128)(2,1)}, u32[]{:S(2)}, u32[]{:S(2)}) async-start(bf16[32,4,2,32,128]{4,3,2,1,0:T(8,128)(2,1)} %row_both.1), calls=%async_computation.2 | async-start | bytes 4194304 | tf_op jit(solution)/shard_map/all_to_all | solution.py:572
  151.4 1.5 collective-permute-start.17
  153.5 1.5 collective-permute-start.19
  155.8 17.4 %collective-permute-done.17 = s16[512,256]{1,0:T(8,128)(2,1)S(1)} collective-permute-done((s16[512,256]{1,0:T(8,128)(2,1)S(1)}, s16[512,256]{1,0:T(8,128)(2,1)S(1)}, u32[]{:S(2)}, u32[]{:S(2)}) %collective-permute-start.17) | collective-permute-done | bytes 262176 | tf_op jit(solution)/shard_map/ppermute | solution.py:578
  174.5 8.9 %collective-permute-done.19 = s16[512,256]{1,0:T(8,128)(2,1)S(1)} collective-permute-done((s16[512,256]{1,0:T(8,128)(2,1)S(1)}, s16[512,256]{1,0:T(8,128)(2,1)S(1)}, u32[]{:S(2)}, u32[]{:S(2)}) %collective-permute-start.19) | collective-permute-done | bytes 262176 | tf_op jit(solution)/shard_map/ppermute | solution.py:578
  184.2 1.9 collective-permute-done.20.refs_17_
  186.1 13.1 %all-to-all-done.2 = bf16[32,4,2,32,128]{4,3,2,1,0:T(8,128)(2,1)} async-done(((bf16[32,4,2,32,128]{4,3,2,1,0:T(8,128)(2,1)}), bf16[32,4,2,32,128]{4,3,2,1,0:T(8,128)(2,1)}, u32[]{:S(2)}, u32[]{:S(2)}) %all-to-all-start.2) | async-done | bytes 2097184 | tf_op jit(solution)/shard_map/all_to_all | solution.py:572
  199.3 13.1 %column_later.1 = bf16[8,4,4,2,32,128]{5,4,3,2,1,0:T(8,128)(2,1)} custom-call(s32[1]{0:T(128)} %bitcast.1.refs_0_, s32[1]{0:T(128)} %get-tuple-element.57.refs_1_, bf16[8,4,4,2,32,128]{5,4,3,2,1,0:T(8,128)(2,1)} %bitcast.15.refs_2_, bf16[4,256,384]{2,1,0:T(8,128)(2,1)} %copy-done, bf16[4,256,384]{2,1,0:T(8,128)(2,1)} %copy-done.4, ...), custom_call_target="tpu_custom_call" | custom-call | tf_op jit(solution)/shard_map/column_later/pallas_call | solution.py:300
  212.4 3.9 %all-to-all-start.3 = ((bf16[32,4,2,32,128]{4,3,2,1,0:T(8,128)(2,1)}), bf16[32,4,2,32,128]{4,3,2,1,0:T(8,128)(2,1)}, u32[]{:S(2)}, u32[]{:S(2)}) async-start(bf16[32,4,2,32,128]{4,3,2,1,0:T(8,128)(2,1)} %bitcast.43), calls=%async_computation.3 | async-start | bytes 4194304 | tf_op jit(solution)/shard_map/all_to_all | solution.py:572
  216.2 48.0 %all-to-all-done.3.refs_1_ = bf16[32,4,2,32,128]{4,3,2,1,0:T(8,128)(2,1)} async-done(((bf16[32,4,2,32,128]{4,3,2,1,0:T(8,128)(2,1)}), bf16[32,4,2,32,128]{4,3,2,1,0:T(8,128)(2,1)}, u32[]{:S(2)}, u32[]{:S(2)}) %all-to-all-start.3) | async-done | bytes 2097184 | tf_op jit(solution)/shard_map/all_to_all | solution.py:572
  264.2 4.4 %row_last.3 = (bf16[2,8,64,128]{3,2,1,0:T(8,128)(2,1)}, bf16[2,8,64,128]{3,2,1,0:T(8,128)(2,1)}, bf16[2,8,64,128]{3,2,1,0:T(8,128)(2,1)}, bf16[2,8,64,128]{3,2,1,0:T(8,128)(2,1)}) custom-call(s32[1]{0:T(128)} %bitcast.refs_0_, bf16[32,4,2,32,128]{4,3,2,1,0:T(8,128)(2,1)} %all-to-all-done.3.refs_1_, bf16[4,512,256]{2,1,0:T(8,128)(2,1)} %constant.197.clone.refs_2_, ...), custom_call_target="tpu_custom_call" | custom-call | flops 1073741824 | bytes 4194304 | tf_op jit(solution)/shard_map/row_last/pallas_call | solution.py:479
  268.7 2.0 collective-permute-start.25
  270.7 1.5 collective-permute-start.26
  272.2 4.4 %row_last.2 = (bf16[2,8,64,128]{3,2,1,0:T(8,128)(2,1)}, bf16[2,8,64,128]{3,2,1,0:T(8,128)(2,1)}, bf16[2,8,64,128]{3,2,1,0:T(8,128)(2,1)}, bf16[2,8,64,128]{3,2,1,0:T(8,128)(2,1)}) custom-call(s32[1]{0:T(128)} %bitcast.refs_0_, bf16[32,4,2,32,128]{4,3,2,1,0:T(8,128)(2,1)} %all-to-all-done.3.refs_1_, bf16[4,512,256]{2,1,0:T(8,128)(2,1)} %constant.197.clone.refs_2_, ...), custom_call_target="tpu_custom_call" | custom-call | flops 1073741824 | bytes 4194304 | tf_op jit(solution)/shard_map/row_last/pallas_call | solution.py:479
  276.7 1.0 collective-permute-start.21
  277.7 1.0 collective-permute-start.22
  278.7 1.1 collective-permute-done.24.refs_2_
  279.8 2.5 collective-permute-start.23
  282.3 6.7 %collective-permute-done.25.refs_3_ = bf16[2,8,64,128]{3,2,1,0:T(8,128)(2,1)S(1)} collective-permute-done((bf16[2,8,64,128]{3,2,1,0:T(8,128)(2,1)}, bf16[2,8,64,128]{3,2,1,0:T(8,128)(2,1)S(1)}, u32[]{:S(2)}, u32[]{:S(2)}) %collective-permute-start.25) | collective-permute-done | bytes 262176 | tf_op jit(solution)/shard_map/ppermute | solution.py:578
  289.0 18.8 %collective-permute-done.26.refs_4_ = bf16[2,8,64,128]{3,2,1,0:T(8,128)(2,1)S(1)} collective-permute-done((bf16[2,8,64,128]{3,2,1,0:T(8,128)(2,1)}, bf16[2,8,64,128]{3,2,1,0:T(8,128)(2,1)S(1)}, u32[]{:S(2)}, u32[]{:S(2)}) %collective-permute-start.26) | collective-permute-done | bytes 262176 | tf_op jit(solution)/shard_map/ppermute | solution.py:578
  308.4 5.3 %closing_order.2.refs_8_ = f32[2,512,1024]{2,1,0:T(8,128)} custom-call(s32[1]{0:T(128)} %bitcast.refs_0_, bf16[2,8,64,128]{3,2,1,0:T(8,128)(2,1)} %get-tuple-element.17.refs_1_, bf16[2,8,64,128]{3,2,1,0:T(8,128)(2,1)} %copy-done.16, bf16[2,8,64,128]{3,2,1,0:T(8,128)(2,1)} %copy-done.18, bf16[2,8,64,128]{3,2,1,0:T(8,128)(2,1)} %copy-done.19, ...), custom_call_target="tpu_custom_call" | custom-call | flops 1073741824 | bytes 4194304 | tf_op jit(solution)/shard_map/closing_order/pallas_call | solution.py:557
  313.8 4.1 %collective-permute-done.23.refs_4_ = bf16[2,8,64,128]{3,2,1,0:T(8,128)(2,1)S(1)} collective-permute-done((bf16[2,8,64,128]{3,2,1,0:T(8,128)(2,1)}, bf16[2,8,64,128]{3,2,1,0:T(8,128)(2,1)S(1)}, u32[]{:S(2)}, u32[]{:S(2)}) %collective-permute-start.23) | collective-permute-done | bytes 262176 | tf_op jit(solution)/shard_map/ppermute | solution.py:578
  318.6 5.3 %closing_order.3 = f32[2,512,1024]{2,1,0:T(8,128)} custom-call(s32[1]{0:T(128)} %bitcast.refs_0_, bf16[2,8,64,128]{3,2,1,0:T(8,128)(2,1)} %get-tuple-element.13.refs_1_, bf16[2,8,64,128]{3,2,1,0:T(8,128)(2,1)} %copy-done.15, bf16[2,8,64,128]{3,2,1,0:T(8,128)(2,1)} %copy-done.17, bf16[2,8,64,128]{3,2,1,0:T(8,128)(2,1)} %copy-done.20, ...), custom_call_target="tpu_custom_call", output_to_operand_aliasing={{}: (8, {})} | custom-call | flops 1073741824 | bytes 4194304 | tf_op jit(solution)/shard_map/closing_order/pallas_call | solution.py:557
  (94 shorter events, 14.4 us)
Async XLA Ops:
  2.6 33.8 %collective-permute-start = (bf16[2,512,256]{2,1,0:T(8,128)(2,1)}, bf16[2,512,256]{2,1,0:T(8,128)(2,1)}, u32[]{:S(2)}, u32[]{:S(2)}) collective-permute-start(bf16[2,512,256]{2,1,0:T(8,128)(2,1)} %get-tuple-element.27), channel_id=1, source_target_pairs={{0,8},{4,12},{8,0},{12,4},{16,24},{20,28},{24,16},{28,20},{1,9},{5... | collective-permute-start | bytes 1572872 | tf_op jit(solution)/shard_map/ppermute | solution.py:578
  4.0 34.6 %collective-permute-start.1 = (bf16[2,512,256]{2,1,0:T(8,128)(2,1)}, bf16[2,512,256]{2,1,0:T(8,128)(2,1)}, u32[]{:S(2)}, u32[]{:S(2)}) collective-permute-start(bf16[2,512,256]{2,1,0:T(8,128)(2,1)} %get-tuple-element.26), channel_id=1, source_target_pairs={{0,16},{4,20},{8,24},{12,28},{16,0},{20,4},{24,8},{28,12},{1,17},{... | collective-permute-start | bytes 1572872 | tf_op jit(solution)/shard_map/ppermute | solution.py:578
  9.6 18.7 %collective-permute-start.13 = (s16[512,256]{1,0:T(8,128)(2,1)}, s16[512,256]{1,0:T(8,128)(2,1)}, u32[]{:S(2)}, u32[]{:S(2)}) collective-permute-start(s16[512,256]{1,0:T(8,128)(2,1)} %get-tuple-element.37), channel_id=1, source_target_pairs={{0,8},{4,12},{8,0},{12,4},{16,24},{20,28},{24,16},{28,20},{1,9},{5... | collective-permute-start | bytes 786440 | tf_op jit(solution)/shard_map/ppermute | solution.py:578
  10.1 21.4 %collective-permute-start.14 = (s16[512,256]{1,0:T(8,128)(2,1)}, s16[512,256]{1,0:T(8,128)(2,1)}, u32[]{:S(2)}, u32[]{:S(2)}) collective-permute-start(s16[512,256]{1,0:T(8,128)(2,1)} %get-tuple-element.36), channel_id=1, source_target_pairs={{0,16},{4,20},{8,24},{12,28},{16,0},{20,4},{24,8},{28,12},{1,17},{... | collective-permute-start | bytes 786440 | tf_op jit(solution)/shard_map/ppermute | solution.py:578
  11.6 21.5 %collective-permute-start.15 = (s16[512,256]{1,0:T(8,128)(2,1)}, s16[512,256]{1,0:T(8,128)(2,1)}, u32[]{:S(2)}, u32[]{:S(2)}) collective-permute-start(s16[512,256]{1,0:T(8,128)(2,1)} %get-tuple-element.35), channel_id=1, source_target_pairs={{0,24},{4,28},{8,16},{12,20},{16,8},{20,12},{24,0},{28,4},{1,25},{... | collective-permute-start | bytes 786440 | tf_op jit(solution)/shard_map/ppermute | solution.py:578
  18.3 5.5 %copy-start.21 = (s32[4,3]{1,0:T(4,128)S(1)}, s32[4,3]{1,0:T(4,128)}, u32[]{:S(2)}) copy-start(s32[4,3]{1,0:T(4,128)} %param.18) | copy-start | bytes 148
  18.3 5.5 %copy-start.12 = (bf16[2,4,3,128,128]{4,3,2,1,0:T(8,128)(2,1)S(1)}, bf16[2,4,3,128,128]{4,3,2,1,0:T(8,128)(2,1)}, u32[]{:S(2)}) copy-start(bf16[2,4,3,128,128]{4,3,2,1,0:T(8,128)(2,1)} %param.17) | copy-start | bytes 2359300
  18.3 66.8 %all-to-all-start.1 = ((bf16[4,8,128,128]{3,2,1,0:T(8,128)(2,1)}), bf16[4,8,128,128]{3,2,1,0:T(8,128)(2,1)}, u32[]{:S(2)}, u32[]{:S(2)}) async-start(bf16[4,8,128,128]{3,2,1,0:T(8,128)(2,1)} %mask_order.1), calls=%async_computation.1 | async-start | bytes 2097152 | tf_op jit(solution)/shard_map/all_to_all | solution.py:572
  28.3 12.1 %copy-start = (bf16[4,256,384]{2,1,0:T(8,128)(2,1)}, bf16[4,256,384]{2,1,0:T(8,128)(2,1)S(1)}, u32[]{:S(2)}) copy-start(bf16[4,256,384]{2,1,0:T(8,128)(2,1)S(1)} %reshape.39.refs_7_.refs_3_) | copy-start | bytes 2359300
  28.3 16.0 %collective-permute-start.2 = (bf16[2,512,256]{2,1,0:T(8,128)(2,1)}, bf16[2,512,256]{2,1,0:T(8,128)(2,1)S(1)}, u32[]{:S(2)}, u32[]{:S(2)}) collective-permute-start(bf16[2,512,256]{2,1,0:T(8,128)(2,1)} %get-tuple-element.25), channel_id=1, source_target_pairs={{0,24},{4,28},{8,16},{12,20},{16,8},{20,12},{24,0},{28,4},{1,25},{... | collective-permute-start | bytes 1572872 | tf_op jit(solution)/shard_map/ppermute | solution.py:578
  31.5 28.1 %collective-permute-start.4 = (bf16[4,256,384]{2,1,0:T(8,128)(2,1)S(1)}, bf16[4,256,384]{2,1,0:T(8,128)(2,1)S(1)}, u32[]{:S(2)}, u32[]{:S(2)}) collective-permute-start(bf16[4,256,384]{2,1,0:T(8,128)(2,1)S(1)} %reshape.39.refs_7_.refs_3_), channel_id=1, source_target_pairs={{0,4},{4,0},{8,12},{12,8},{16,20},{20,16},{24,28},{28,24},{1,5},{5... | collective-permute-start | bytes 2359304 | tf_op jit(solution)/shard_map/ppermute | solution.py:578
  33.2 25.0 %collective-permute-start.5 = (bf16[4,256,384]{2,1,0:T(8,128)(2,1)S(1)}, bf16[4,256,384]{2,1,0:T(8,128)(2,1)S(1)}, u32[]{:S(2)}, u32[]{:S(2)}) collective-permute-start(bf16[4,256,384]{2,1,0:T(8,128)(2,1)S(1)} %reshape.39.refs_7_.refs_3_), channel_id=1, source_target_pairs={{0,8},{4,12},{8,0},{12,4},{16,24},{20,28},{24,16},{28,20},{1,9},{5... | collective-permute-start | bytes 2359304 | tf_op jit(solution)/shard_map/ppermute | solution.py:578
  36.4 22.6 %collective-permute-start.7 = (bf16[4,256,384]{2,1,0:T(8,128)(2,1)S(1)}, bf16[4,256,384]{2,1,0:T(8,128)(2,1)S(1)}, u32[]{:S(2)}, u32[]{:S(2)}) collective-permute-start(bf16[4,256,384]{2,1,0:T(8,128)(2,1)S(1)} %reshape.39.refs_7_.refs_3_), channel_id=1, source_target_pairs={{0,16},{4,20},{8,24},{12,28},{16,0},{20,4},{24,8},{28,12},{1,17},{... | collective-permute-start | bytes 2359304 | tf_op jit(solution)/shard_map/ppermute | solution.py:578
  38.6 20.4 %collective-permute-start.16 = (s16[4,512,128]{2,1,0:T(8,128)(2,1)S(1)}, s16[4,512,128]{2,1,0:T(8,128)(2,1)S(1)}, u32[]{:S(2)}, u32[]{:S(2)}) collective-permute-start(s16[4,512,128]{2,1,0:T(8,128)(2,1)S(1)} %pad_add_fusion), channel_id=1, source_target_pairs={{0,4},{4,0},{8,12},{12,8},{16,20},{20,16},{24,28},{28,24},{1,5},{5... | collective-permute-start | bytes 1572872 | tf_op jit(solution)/shard_map/ppermute | solution.py:578
  45.1 25.6 %copy-start.22 = (s32[2]{0:T(128)S(1)}, s32[2]{0:T(128)}, u32[]{:S(2)}) copy-start(s32[2]{0:T(128)} %param.21) | copy-start | bytes 28
  45.3 26.1 %collective-permute-start.3 = (bf16[4,2,512,128]{3,2,1,0:T(8,128)(2,1)S(1)}, bf16[4,2,512,128]{3,2,1,0:T(8,128)(2,1)S(1)}, u32[]{:S(2)}, u32[]{:S(2)}) collective-permute-start(bf16[4,2,512,128]{3,2,1,0:T(8,128)(2,1)S(1)} %pad_maximum_fusion), channel_id=1, source_target_pairs={{0,4},{4,0},{8,12},{12,8},{16,20},{20,16},{24,28},{28,24},{1,5},{5... | collective-permute-start | bytes 3145736 | tf_op jit(solution)/shard_map/ppermute | solution.py:578
  58.2 16.3 %copy-start.1 = (bf16[4,256,384]{2,1,0:T(8,128)(2,1)}, bf16[4,256,384]{2,1,0:T(8,128)(2,1)S(1)}, u32[]{:S(2)}) copy-start(bf16[4,256,384]{2,1,0:T(8,128)(2,1)S(1)} %collective-permute-done.5.refs_9_.refs_5_) | copy-start | bytes 2359300
  58.2 8.8 %collective-permute-start.9 = (bf16[2,256,384]{2,1,0:T(8,128)(2,1)S(1)}, bf16[2,256,384]{2,1,0:T(8,128)(2,1)S(1)}, u32[]{:S(2)}, u32[]{:S(2)}) collective-permute-start(bf16[2,256,384]{2,1,0:T(8,128)(2,1)S(1)} %slice.24), channel_id=1, source_target_pairs={{0,16},{4,20},{8,24},{12,28},{16,0},{20,4},{24,8},{28,12},{1,17},{... | collective-permute-start | bytes 1179656 | tf_op jit(solution)/shard_map/ppermute | solution.py:578
  58.9 12.5 %copy-start.2 = (bf16[4,256,384]{2,1,0:T(8,128)(2,1)}, bf16[4,256,384]{2,1,0:T(8,128)(2,1)S(1)}, u32[]{:S(2)}) copy-start(bf16[4,256,384]{2,1,0:T(8,128)(2,1)S(1)} %collective-permute-done.7.refs_11_.refs_7_) | copy-start | bytes 2359300
  58.9 12.4 %collective-permute-start.6 = (bf16[4,256,384]{2,1,0:T(8,128)(2,1)S(1)}, bf16[4,256,384]{2,1,0:T(8,128)(2,1)S(1)}, u32[]{:S(2)}, u32[]{:S(2)}) collective-permute-start(bf16[4,256,384]{2,1,0:T(8,128)(2,1)S(1)} %collective-permute-done.5.refs_9_.refs_5_), channel_id=1, source_target_pairs={{0,4},{4,0},{8,12},{12,8},{16,20},{20,16},{24,28},{28,24},{1,5},{5... | collective-permute-start | bytes 2359304 | tf_op jit(solution)/shard_map/ppermute | solution.py:578
  59.0 15.4 %copy-start.13 = (s16[4,512,128]{2,1,0:T(8,128)(2,1)}, s16[4,512,128]{2,1,0:T(8,128)(2,1)S(1)}, u32[]{:S(2)}) copy-start(s16[4,512,128]{2,1,0:T(8,128)(2,1)S(1)} %collective-permute-done.16.refs_21_) | copy-start | bytes 1572868
  59.0 12.4 %collective-permute-start.8 = (bf16[4,256,384]{2,1,0:T(8,128)(2,1)S(1)}, bf16[4,256,384]{2,1,0:T(8,128)(2,1)S(1)}, u32[]{:S(2)}, u32[]{:S(2)}) collective-permute-start(bf16[4,256,384]{2,1,0:T(8,128)(2,1)S(1)} %collective-permute-done.7.refs_11_.refs_7_), channel_id=1, source_target_pairs={{0,4},{4,0},{8,12},{12,8},{16,20},{20,16},{24,28},{28,24},{1,5},{5... | collective-permute-start | bytes 2359304 | tf_op jit(solution)/shard_map/ppermute | solution.py:578
  59.6 14.8 %copy-start.4 = (bf16[4,256,384]{2,1,0:T(8,128)(2,1)}, bf16[4,256,384]{2,1,0:T(8,128)(2,1)S(1)}, u32[]{:S(2)}) copy-start(bf16[4,256,384]{2,1,0:T(8,128)(2,1)S(1)} %collective-permute-done.4.refs_8_.refs_4_) | copy-start | bytes 2359300
  59.6 11.1 %collective-permute-start.10 = (bf16[2,256,384]{2,1,0:T(8,128)(2,1)S(1)}, bf16[2,256,384]{2,1,0:T(8,128)(2,1)S(1)}, u32[]{:S(2)}, u32[]{:S(2)}) collective-permute-start(bf16[2,256,384]{2,1,0:T(8,128)(2,1)S(1)} %slice.25), channel_id=1, source_target_pairs={{0,8},{4,12},{8,0},{12,4},{16,24},{20,28},{24,16},{28,20},{1,9},{5... | collective-permute-start | bytes 1179656 | tf_op jit(solution)/shard_map/ppermute | solution.py:578
  67.0 7.4 %copy-start.7 = (bf16[2,256,384]{2,1,0:T(8,128)(2,1)}, bf16[2,256,384]{2,1,0:T(8,128)(2,1)S(1)}, u32[]{:S(2)}) copy-start(bf16[2,256,384]{2,1,0:T(8,128)(2,1)S(1)} %collective-permute-done.9.refs_13_.refs_9_) | copy-start | bytes 1179652
  67.0 5.6 %collective-permute-start.11 = (bf16[2,256,384]{2,1,0:T(8,128)(2,1)S(1)}, bf16[2,256,384]{2,1,0:T(8,128)(2,1)S(1)}, u32[]{:S(2)}, u32[]{:S(2)}) collective-permute-start(bf16[2,256,384]{2,1,0:T(8,128)(2,1)S(1)} %collective-permute-done.9.refs_13_.refs_9_), channel_id=1, source_target_pairs={{0,4},{4,0},{8,12},{12,8},{16,20},{20,16},{24,28},{28,24},{1,5},{5... | collective-permute-start | bytes 1179656 | tf_op jit(solution)/shard_map/ppermute | solution.py:578
  70.7 2.8 copy-start.8
  70.7 2.8 collective-permute-start.12
  71.4 3.0 copy-start.11
  71.4 1.3 copy-start.5
  147.1 4.2 %copy-start.3 = (s16[1,512,1024]{2,1,0:T(8,128)(2,1)S(1)}, s16[1,512,1024]{2,1,0:T(8,128)(2,1)}, u32[]{:S(2)}) copy-start(s16[1,512,1024]{2,1,0:T(8,128)(2,1)} %get-tuple-element.21) | copy-start | bytes 3145732
  147.1 52.1 %all-to-all-start.2 = ((bf16[32,4,2,32,128]{4,3,2,1,0:T(8,128)(2,1)}), bf16[32,4,2,32,128]{4,3,2,1,0:T(8,128)(2,1)}, u32[]{:S(2)}, u32[]{:S(2)}) async-start(bf16[32,4,2,32,128]{4,3,2,1,0:T(8,128)(2,1)} %row_both.1), calls=%async_computation.2 | async-start | bytes 4194304 | tf_op jit(solution)/shard_map/all_to_all | solution.py:572
  151.4 21.8 %collective-permute-start.17 = (s16[512,256]{1,0:T(8,128)(2,1)S(1)}, s16[512,256]{1,0:T(8,128)(2,1)S(1)}, u32[]{:S(2)}, u32[]{:S(2)}) collective-permute-start(s16[512,256]{1,0:T(8,128)(2,1)S(1)} %get-tuple-element.32), channel_id=1, source_target_pairs={{0,8},{4,12},{8,0},{12,4},{16,24},{20,28},{24,16},{28,20},{1,9},{5... | collective-permute-start | bytes 786440 | tf_op jit(solution)/shard_map/ppermute | solution.py:578
  152.9 20.9 %collective-permute-start.18 = (s16[512,256]{1,0:T(8,128)(2,1)S(1)}, s16[512,256]{1,0:T(8,128)(2,1)S(1)}, u32[]{:S(2)}, u32[]{:S(2)}) collective-permute-start(s16[512,256]{1,0:T(8,128)(2,1)S(1)} %get-tuple-element.31), channel_id=1, source_target_pairs={{0,16},{4,20},{8,24},{12,28},{16,0},{20,4},{24,8},{28,12},{1,17},{... | collective-permute-start | bytes 786440 | tf_op jit(solution)/shard_map/ppermute | solution.py:578
  153.5 29.9 %collective-permute-start.19 = (s16[512,256]{1,0:T(8,128)(2,1)S(1)}, s16[512,256]{1,0:T(8,128)(2,1)S(1)}, u32[]{:S(2)}, u32[]{:S(2)}) collective-permute-start(s16[512,256]{1,0:T(8,128)(2,1)S(1)} %get-tuple-element.30), channel_id=1, source_target_pairs={{0,24},{4,28},{8,16},{12,20},{16,8},{20,12},{24,0},{28,4},{1,25},{... | collective-permute-start | bytes 786440 | tf_op jit(solution)/shard_map/ppermute | solution.py:578
  184.1 2.0 collective-permute-start.20
  186.1 13.1 %copy-start.14 = (s16[4,512,128]{2,1,0:T(8,128)(2,1)}, s16[4,512,128]{2,1,0:T(8,128)(2,1)S(1)}, u32[]{:S(2)}) copy-start(s16[4,512,128]{2,1,0:T(8,128)(2,1)S(1)} %collective-permute-done.20.refs_17_) | copy-start | bytes 1572868
  212.4 51.8 %all-to-all-start.3 = ((bf16[32,4,2,32,128]{4,3,2,1,0:T(8,128)(2,1)}), bf16[32,4,2,32,128]{4,3,2,1,0:T(8,128)(2,1)}, u32[]{:S(2)}, u32[]{:S(2)}) async-start(bf16[32,4,2,32,128]{4,3,2,1,0:T(8,128)(2,1)} %bitcast.43), calls=%async_computation.3 | async-start | bytes 4194304 | tf_op jit(solution)/shard_map/all_to_all | solution.py:572
  268.6 11.1 %collective-permute-start.24 = (bf16[2,8,64,128]{3,2,1,0:T(8,128)(2,1)}, bf16[2,8,64,128]{3,2,1,0:T(8,128)(2,1)S(1)}, u32[]{:S(2)}, u32[]{:S(2)}) collective-permute-start(bf16[2,8,64,128]{3,2,1,0:T(8,128)(2,1)} %get-tuple-element.18), channel_id=1, source_target_pairs={{0,1},{1,0},{2,3},{3,2},{4,5},{5,4},{6,7},{7,6},{8,9},{9,8},{10,11... | collective-permute-start | bytes 786440 | tf_op jit(solution)/shard_map/ppermute | solution.py:578
  268.7 20.2 %collective-permute-start.25 = (bf16[2,8,64,128]{3,2,1,0:T(8,128)(2,1)}, bf16[2,8,64,128]{3,2,1,0:T(8,128)(2,1)S(1)}, u32[]{:S(2)}, u32[]{:S(2)}) collective-permute-start(bf16[2,8,64,128]{3,2,1,0:T(8,128)(2,1)} %get-tuple-element.19), channel_id=1, source_target_pairs={{0,2},{1,3},{2,0},{3,1},{4,6},{5,7},{6,4},{7,5},{8,10},{9,11},{10,... | collective-permute-start | bytes 786440 | tf_op jit(solution)/shard_map/ppermute | solution.py:578
  270.7 37.0 %collective-permute-start.26 = (bf16[2,8,64,128]{3,2,1,0:T(8,128)(2,1)}, bf16[2,8,64,128]{3,2,1,0:T(8,128)(2,1)S(1)}, u32[]{:S(2)}, u32[]{:S(2)}) collective-permute-start(bf16[2,8,64,128]{3,2,1,0:T(8,128)(2,1)} %get-tuple-element.20), channel_id=1, source_target_pairs={{0,3},{1,2},{2,1},{3,0},{4,7},{5,6},{6,5},{7,4},{8,11},{9,10},{10,... | collective-permute-start | bytes 786440 | tf_op jit(solution)/shard_map/ppermute | solution.py:578
  276.7 37.1 %collective-permute-start.21 = (bf16[2,8,64,128]{3,2,1,0:T(8,128)(2,1)}, bf16[2,8,64,128]{3,2,1,0:T(8,128)(2,1)S(1)}, u32[]{:S(2)}, u32[]{:S(2)}) collective-permute-start(bf16[2,8,64,128]{3,2,1,0:T(8,128)(2,1)} %get-tuple-element.14), channel_id=1, source_target_pairs={{0,1},{1,0},{2,3},{3,2},{4,5},{5,4},{6,7},{7,6},{8,9},{9,8},{10,11... | collective-permute-start | bytes 786440 | tf_op jit(solution)/shard_map/ppermute | solution.py:578
  277.7 36.1 %collective-permute-start.22 = (bf16[2,8,64,128]{3,2,1,0:T(8,128)(2,1)}, bf16[2,8,64,128]{3,2,1,0:T(8,128)(2,1)S(1)}, u32[]{:S(2)}, u32[]{:S(2)}) collective-permute-start(bf16[2,8,64,128]{3,2,1,0:T(8,128)(2,1)} %get-tuple-element.15), channel_id=1, source_target_pairs={{0,2},{1,3},{2,0},{3,1},{4,6},{5,7},{6,4},{7,5},{8,10},{9,11},{10,... | collective-permute-start | bytes 786440 | tf_op jit(solution)/shard_map/ppermute | solution.py:578
  279.8 27.9 %copy-start.16 = (bf16[2,8,64,128]{3,2,1,0:T(8,128)(2,1)}, bf16[2,8,64,128]{3,2,1,0:T(8,128)(2,1)S(1)}, u32[]{:S(2)}) copy-start(bf16[2,8,64,128]{3,2,1,0:T(8,128)(2,1)S(1)} %collective-permute-done.24.refs_2_) | copy-start | bytes 786436
  279.8 38.0 %collective-permute-start.23 = (bf16[2,8,64,128]{3,2,1,0:T(8,128)(2,1)}, bf16[2,8,64,128]{3,2,1,0:T(8,128)(2,1)S(1)}, u32[]{:S(2)}, u32[]{:S(2)}) collective-permute-start(bf16[2,8,64,128]{3,2,1,0:T(8,128)(2,1)} %get-tuple-element.16), channel_id=1, source_target_pairs={{0,3},{1,2},{2,1},{3,0},{4,7},{5,6},{6,5},{7,4},{8,11},{9,10},{10,... | collective-permute-start | bytes 786440 | tf_op jit(solution)/shard_map/ppermute | solution.py:578
  289.0 18.8 %copy-start.18 = (bf16[2,8,64,128]{3,2,1,0:T(8,128)(2,1)}, bf16[2,8,64,128]{3,2,1,0:T(8,128)(2,1)S(1)}, u32[]{:S(2)}) copy-start(bf16[2,8,64,128]{3,2,1,0:T(8,128)(2,1)S(1)} %collective-permute-done.25.refs_3_) | copy-start | bytes 786436
  313.8 4.1 %copy-start.15 = (bf16[2,8,64,128]{3,2,1,0:T(8,128)(2,1)}, bf16[2,8,64,128]{3,2,1,0:T(8,128)(2,1)S(1)}, u32[]{:S(2)}) copy-start(bf16[2,8,64,128]{3,2,1,0:T(8,128)(2,1)S(1)} %collective-permute-done.21.refs_2_) | copy-start | bytes 786436
  313.8 4.1 %copy-start.17 = (bf16[2,8,64,128]{3,2,1,0:T(8,128)(2,1)}, bf16[2,8,64,128]{3,2,1,0:T(8,128)(2,1)S(1)}, u32[]{:S(2)}) copy-start(bf16[2,8,64,128]{3,2,1,0:T(8,128)(2,1)S(1)} %collective-permute-done.22.refs_3_) | copy-start | bytes 786436
  (5 other events, 3.9 us)

commit v5 on v4

--- a/solution.py
+++ b/solution.py
@@ -20,8 +20,8 @@
 F32 = jnp.float32
 
 
-def params():
-    return pltpu.CompilerParams(vmem_limit_bytes=VMEM_LIMIT)
+def params(limit=VMEM_LIMIT):
+    return pltpu.CompilerParams(vmem_limit_bytes=limit)
 
 
 def vmem(count):
@@ -562,7 +562,7 @@
         out_specs=pl.BlockSpec((2, height, width), lambda i: (0, number, 0)),
         scratch_shapes=[pltpu.VMEM((2, height, width), BF16), pltpu.VMEM((2, height, width), BF16)],
         input_output_aliases=aliases,
-        compiler_params=params(),
+        compiler_params=params(24 * 1024 * 1024),
         cost_estimate=pl.CostEstimate(flops=4 * height * width * width, bytes_accessed=2**22, transcendentals=0),
         name="closing_order",
     )(*arguments)

time: 325 us -> 322 us (level)
  Pallas kernels: 57.6 us -> 53 us
    pallas_call x2, Pallas kernels: 10.7 us -> 6.09 us  [closing_work(): pl.pallas_call(body, grid=(1,), out_shape=jax.ShapeDtypeStruct((2, height...]
  transfers between devices with their start and end apart: 30 -> 30, of which waited for: 14 -> 14; matrix products, arithmetic and copies ran while one was open for 7% -> 7% of each run, Pallas kernels for 8% -> 7%
where the time goes in v5:
time: 322 us; the launch traced here: 321 us
  waiting for transfers between devices  147 us (46%)
  Pallas kernels  53 us (16%)
  blocking collectives  52.9 us (16%)
  starting transfers between devices  35.9 us (11%)
  local copies, waits for them, and re-layouts  28.3 us (9%)
    ppermute x27, waiting for transfers between devices, swap(): lax.ppermute(value, axis, [(at, at ^ distance) for at in range(lax.axis_s...  86.1 us
    all_to_all x3, waiting for transfers between devices, exchange(): return lax.all_to_all(value, axis, split_axis=0, concat_axis=0, tiled=True)  61.1 us
    all_to_all x1, blocking collectives, exchange(): return lax.all_to_all(value, axis, split_axis=0, concat_axis=0, tiled=True)  52.9 us
    pallas_call x2, Pallas kernels, column_work(): pl.pallas_call(body, out_shape=sent, in_specs=[smem, smem] + [anywhere] *...  23.8 us
    ppermute x27, starting transfers between devices, swap(): lax.ppermute(value, axis, [(at, at ^ distance) for at in range(lax.axis_s...  22.4 us
    all_to_all x3, starting transfers between devices, exchange(): return lax.all_to_all(value, axis, split_axis=0, concat_axis=0, tiled=True)  13.4 us
    another operation x10, local copies, waits for them, and re-layouts, spread(): jnp.stack([part(piece, 1 - core) for piece in chips])  13.4 us
    pallas_call x1, Pallas kernels, row_work(): pl.pallas_call(body, out_shape=jax.ShapeDtypeStruct(received.shape, BF16)...  9.11 us
  transfers between devices with their start and end apart: 30, of which 14 were waited for; matrix products, arithmetic and copies ran while one was open for 7% of the time, Pallas kernels for 7%

profile of v5, /device:TPU:12, one launch (start us, length us, event | category | flops | bytes accessed | tf_op | source)
XLA Modules:
  0.0 320.9 jit_solution(14258110715383518843)
XLA Ops:
  0.0 2.6 constant_dynamic-slice_fusion.9
  2.6 1.5 collective-permute-start
  4.6 2.9 round-nearest-even_convert_fusion
  7.5 1.2 fusion
  10.1 1.5 collective-permute-start.14
  11.6 1.4 collective-permute-start.15
  13.1 5.2 %mask_order.1 = bf16[4,8,128,128]{3,2,1,0:T(8,128)(2,1)} custom-call(f32[512,1024]{1,0:T(8,128)} %refs_5_.3, bf16[512,512]{1,0:T(8,128)(2,1)} %constant.199.clone.down_ref, bf16[1024,1024]{1,0:T(8,128)(2,1)} %constant.200.clone.across_ref), custom_call_target="tpu_custom_call" | custom-call | tf_op jit(solution)/shard_map/mask_order/pallas_call | solution.py:510
  18.3 5.4 %all-to-all-start.1 = ((bf16[4,8,128,128]{3,2,1,0:T(8,128)(2,1)}), bf16[4,8,128,128]{3,2,1,0:T(8,128)(2,1)}, u32[]{:S(2)}, u32[]{:S(2)}) async-start(bf16[4,8,128,128]{3,2,1,0:T(8,128)(2,1)} %mask_order.1), calls=%async_computation.1 | async-start | bytes 2097152 | tf_op jit(solution)/shard_map/all_to_all | solution.py:572
  23.9 2.1 dynamic-slice_bitcast_fusion.9
  28.3 1.6 collective-permute-start.2
  29.9 1.7 dynamic-slice_bitcast_fusion.16
  31.5 1.6 dynamic-slice_bitcast_fusion.15
  33.2 1.5 collective-permute-start.5
  34.7 1.6 dynamic-slice_bitcast_fusion.14
  36.8 1.8 dynamic-slice_bitcast_fusion.8
  38.6 1.8 dynamic-slice_bitcast_fusion.7
  40.4 3.9 %collective-permute-done.2 = bf16[2,512,256]{2,1,0:T(8,128)(2,1)S(1)} collective-permute-done((bf16[2,512,256]{2,1,0:T(8,128)(2,1)}, bf16[2,512,256]{2,1,0:T(8,128)(2,1)S(1)}, u32[]{:S(2)}, u32[]{:S(2)}) %collective-permute-start.2) | collective-permute-done | bytes 524320 | tf_op jit(solution)/shard_map/ppermute | solution.py:578
  45.4 12.8 %collective-permute-done.5.refs_9_.refs_5_ = bf16[4,256,384]{2,1,0:T(8,128)(2,1)S(1)} collective-permute-done((bf16[4,256,384]{2,1,0:T(8,128)(2,1)S(1)}, bf16[4,256,384]{2,1,0:T(8,128)(2,1)S(1)}, u32[]{:S(2)}, u32[]{:S(2)}) %collective-permute-start.5) | collective-permute-done | bytes 786464 | tf_op jit(solution)/shard_map/ppermute | solution.py:578
  60.1 7.0 %collective-permute-done.9.refs_13_.refs_9_ = bf16[2,256,384]{2,1,0:T(8,128)(2,1)S(1)} collective-permute-done((bf16[2,256,384]{2,1,0:T(8,128)(2,1)S(1)}, bf16[2,256,384]{2,1,0:T(8,128)(2,1)S(1)}, u32[]{:S(2)}, u32[]{:S(2)}) %collective-permute-start.9) | collective-permute-done | bytes 393248 | tf_op jit(solution)/shard_map/ppermute | solution.py:578
  67.0 3.7 %collective-permute-done.10.refs_14_.refs_10_ = bf16[2,256,384]{2,1,0:T(8,128)(2,1)S(1)} collective-permute-done((bf16[2,256,384]{2,1,0:T(8,128)(2,1)S(1)}, bf16[2,256,384]{2,1,0:T(8,128)(2,1)S(1)}, u32[]{:S(2)}, u32[]{:S(2)}) %collective-permute-start.10) | collective-permute-done | bytes 393248 | tf_op jit(solution)/shard_map/ppermute | solution.py:578
  71.4 1.2 copy-done.11
  74.4 10.5 %column_first.1 = bf16[8,4,4,2,32,128]{5,4,3,2,1,0:T(8,128)(2,1)} custom-call(s32[1]{0:T(128)} %bitcast.1.refs_0_, s32[1]{0:T(128)} %get-tuple-element.56.refs_1_, bf16[2,512,128]{2,1,0:T(8,128)(2,1)} %get-tuple-element.24.refs_2_, bf16[2,512,128]{2,1,0:T(8,128)(2,1)} %get-tuple-element.39.refs_3_, bf16[2,512,128]{2,1,0:T(8,128)(2,1)} %get-tuple-element.41.refs_4_, ...), custom_call_target="tpu_custom_call" | custom-call | tf_op jit(solution)/shard_map/column_first/pallas_call | solution.py:300
  85.0 52.9 %all_to_all.20.refs_0_ = bf16[32,4,2,32,128]{4,3,2,1,0:T(8,128)(2,1)} all-to-all(bf16[32,4,2,32,128]{4,3,2,1,0:T(8,128)(2,1)} %bitcast.44), channel_id=1, replica_groups=mesh['rows'=8,'cols'=4] {'rows','cols'}, dimensions={0} | all-to-all | bytes 4194304 | tf_op jit(solution)/shard_map/all_to_all | solution.py:572
  137.9 9.1 %row_both.1 = bf16[32,4,2,32,128]{4,3,2,1,0:T(8,128)(2,1)} custom-call(bf16[32,4,2,32,128]{4,3,2,1,0:T(8,128)(2,1)} %all_to_all.20.refs_0_, bf16[4,8,128,128]{3,2,1,0:T(8,128)(2,1)} %all-to-all-done.1.refs_1_, bf16[4,512,256]{2,1,0:T(8,128)(2,1)} %constant.197.clone.refs_2_, f32[8,2,1,512]{3,2,1,0:T(1,128)} %constant.198.clone.refs_3_), custom_call_target="tpu_custom_call" | custom-call | tf_op jit(solution)/shard_map/row_both/pallas_call | solution.py:425
  147.0 4.1 %all-to-all-start.2 = ((bf16[32,4,2,32,128]{4,3,2,1,0:T(8,128)(2,1)}), bf16[32,4,2,32,128]{4,3,2,1,0:T(8,128)(2,1)}, u32[]{:S(2)}, u32[]{:S(2)}) async-start(bf16[32,4,2,32,128]{4,3,2,1,0:T(8,128)(2,1)} %row_both.1), calls=%async_computation.2 | async-start | bytes 4194304 | tf_op jit(solution)/shard_map/all_to_all | solution.py:572
  151.3 1.5 collective-permute-start.17
  153.4 1.5 collective-permute-start.19
  155.7 17.4 %collective-permute-done.17 = s16[512,256]{1,0:T(8,128)(2,1)S(1)} collective-permute-done((s16[512,256]{1,0:T(8,128)(2,1)S(1)}, s16[512,256]{1,0:T(8,128)(2,1)S(1)}, u32[]{:S(2)}, u32[]{:S(2)}) %collective-permute-start.17) | collective-permute-done | bytes 262176 | tf_op jit(solution)/shard_map/ppermute | solution.py:578
  174.4 8.9 %collective-permute-done.19 = s16[512,256]{1,0:T(8,128)(2,1)S(1)} collective-permute-done((s16[512,256]{1,0:T(8,128)(2,1)S(1)}, s16[512,256]{1,0:T(8,128)(2,1)S(1)}, u32[]{:S(2)}, u32[]{:S(2)}) %collective-permute-start.19) | collective-permute-done | bytes 262176 | tf_op jit(solution)/shard_map/ppermute | solution.py:578
  184.1 1.9 collective-permute-done.20.refs_17_
  186.0 13.1 %all-to-all-done.2 = bf16[32,4,2,32,128]{4,3,2,1,0:T(8,128)(2,1)} async-done(((bf16[32,4,2,32,128]{4,3,2,1,0:T(8,128)(2,1)}), bf16[32,4,2,32,128]{4,3,2,1,0:T(8,128)(2,1)}, u32[]{:S(2)}, u32[]{:S(2)}) %all-to-all-start.2) | async-done | bytes 2097184 | tf_op jit(solution)/shard_map/all_to_all | solution.py:572
  199.1 13.2 %column_later.1 = bf16[8,4,4,2,32,128]{5,4,3,2,1,0:T(8,128)(2,1)} custom-call(s32[1]{0:T(128)} %bitcast.1.refs_0_, s32[1]{0:T(128)} %get-tuple-element.57.refs_1_, bf16[8,4,4,2,32,128]{5,4,3,2,1,0:T(8,128)(2,1)} %bitcast.15.refs_2_, bf16[4,256,384]{2,1,0:T(8,128)(2,1)} %copy-done.6, bf16[4,256,384]{2,1,0:T(8,128)(2,1)} %copy-done.10, ...), custom_call_target="tpu_custom_call" | custom-call | tf_op jit(solution)/shard_map/column_later/pallas_call | solution.py:300
  212.4 3.8 %all-to-all-start.3 = ((bf16[32,4,2,32,128]{4,3,2,1,0:T(8,128)(2,1)}), bf16[32,4,2,32,128]{4,3,2,1,0:T(8,128)(2,1)}, u32[]{:S(2)}, u32[]{:S(2)}) async-start(bf16[32,4,2,32,128]{4,3,2,1,0:T(8,128)(2,1)} %bitcast.43), calls=%async_computation.3 | async-start | bytes 4194304 | tf_op jit(solution)/shard_map/all_to_all | solution.py:572
  216.2 48.0 %all-to-all-done.3.refs_1_ = bf16[32,4,2,32,128]{4,3,2,1,0:T(8,128)(2,1)} async-done(((bf16[32,4,2,32,128]{4,3,2,1,0:T(8,128)(2,1)}), bf16[32,4,2,32,128]{4,3,2,1,0:T(8,128)(2,1)}, u32[]{:S(2)}, u32[]{:S(2)}) %all-to-all-start.3) | async-done | bytes 2097184 | tf_op jit(solution)/shard_map/all_to_all | solution.py:572
  264.2 4.4 %row_last.3 = (bf16[2,8,64,128]{3,2,1,0:T(8,128)(2,1)}, bf16[2,8,64,128]{3,2,1,0:T(8,128)(2,1)}, bf16[2,8,64,128]{3,2,1,0:T(8,128)(2,1)}, bf16[2,8,64,128]{3,2,1,0:T(8,128)(2,1)}) custom-call(s32[1]{0:T(128)} %bitcast.refs_0_, bf16[32,4,2,32,128]{4,3,2,1,0:T(8,128)(2,1)} %all-to-all-done.3.refs_1_, bf16[4,512,256]{2,1,0:T(8,128)(2,1)} %constant.197.clone.refs_2_, ...), custom_call_target="tpu_custom_call" | custom-call | flops 1073741824 | bytes 4194304 | tf_op jit(solution)/shard_map/row_last/pallas_call | solution.py:479
  268.7 2.0 collective-permute-start.25
  270.8 1.5 collective-permute-start.26
  272.2 4.4 %row_last.2 = (bf16[2,8,64,128]{3,2,1,0:T(8,128)(2,1)}, bf16[2,8,64,128]{3,2,1,0:T(8,128)(2,1)}, bf16[2,8,64,128]{3,2,1,0:T(8,128)(2,1)}, bf16[2,8,64,128]{3,2,1,0:T(8,128)(2,1)}) custom-call(s32[1]{0:T(128)} %bitcast.refs_0_, bf16[32,4,2,32,128]{4,3,2,1,0:T(8,128)(2,1)} %all-to-all-done.3.refs_1_, bf16[4,512,256]{2,1,0:T(8,128)(2,1)} %constant.197.clone.refs_2_, ...), custom_call_target="tpu_custom_call" | custom-call | flops 1073741824 | bytes 4194304 | tf_op jit(solution)/shard_map/row_last/pallas_call | solution.py:479
  277.7 1.0 collective-permute-start.22
  278.7 1.1 collective-permute-done.24.refs_2_
  279.8 2.5 collective-permute-start.23
  282.3 6.7 %collective-permute-done.25.refs_3_ = bf16[2,8,64,128]{3,2,1,0:T(8,128)(2,1)S(1)} collective-permute-done((bf16[2,8,64,128]{3,2,1,0:T(8,128)(2,1)}, bf16[2,8,64,128]{3,2,1,0:T(8,128)(2,1)S(1)}, u32[]{:S(2)}, u32[]{:S(2)}) %collective-permute-start.25) | collective-permute-done | bytes 262176 | tf_op jit(solution)/shard_map/ppermute | solution.py:578
  289.0 18.8 %collective-permute-done.26.refs_4_ = bf16[2,8,64,128]{3,2,1,0:T(8,128)(2,1)S(1)} collective-permute-done((bf16[2,8,64,128]{3,2,1,0:T(8,128)(2,1)}, bf16[2,8,64,128]{3,2,1,0:T(8,128)(2,1)S(1)}, u32[]{:S(2)}, u32[]{:S(2)}) %collective-permute-start.26) | collective-permute-done | bytes 262176 | tf_op jit(solution)/shard_map/ppermute | solution.py:578
  307.7 1.6 copy-done
  309.3 1.6 copy-done.1
  310.9 3.0 closing_order.2.refs_8_
  314.0 3.9 %collective-permute-done.23.refs_4_ = bf16[2,8,64,128]{3,2,1,0:T(8,128)(2,1)S(1)} collective-permute-done((bf16[2,8,64,128]{3,2,1,0:T(8,128)(2,1)}, bf16[2,8,64,128]{3,2,1,0:T(8,128)(2,1)S(1)}, u32[]{:S(2)}, u32[]{:S(2)}) %collective-permute-start.23) | collective-permute-done | bytes 262176 | tf_op jit(solution)/shard_map/ppermute | solution.py:578
  317.9 3.0 closing_order.3
  (94 shorter events, 15.0 us)
Async XLA Ops:
  2.6 33.8 %collective-permute-start = (bf16[2,512,256]{2,1,0:T(8,128)(2,1)}, bf16[2,512,256]{2,1,0:T(8,128)(2,1)}, u32[]{:S(2)}, u32[]{:S(2)}) collective-permute-start(bf16[2,512,256]{2,1,0:T(8,128)(2,1)} %get-tuple-element.27), channel_id=1, source_target_pairs={{0,8},{4,12},{8,0},{12,4},{16,24},{20,28},{24,16},{28,20},{1,9},{5... | collective-permute-start | bytes 1572872 | tf_op jit(solution)/shard_map/ppermute | solution.py:578
  4.0 34.6 %collective-permute-start.1 = (bf16[2,512,256]{2,1,0:T(8,128)(2,1)}, bf16[2,512,256]{2,1,0:T(8,128)(2,1)}, u32[]{:S(2)}, u32[]{:S(2)}) collective-permute-start(bf16[2,512,256]{2,1,0:T(8,128)(2,1)} %get-tuple-element.26), channel_id=1, source_target_pairs={{0,16},{4,20},{8,24},{12,28},{16,0},{20,4},{24,8},{28,12},{1,17},{... | collective-permute-start | bytes 1572872 | tf_op jit(solution)/shard_map/ppermute | solution.py:578
  9.6 18.7 %collective-permute-start.13 = (s16[512,256]{1,0:T(8,128)(2,1)}, s16[512,256]{1,0:T(8,128)(2,1)}, u32[]{:S(2)}, u32[]{:S(2)}) collective-permute-start(s16[512,256]{1,0:T(8,128)(2,1)} %get-tuple-element.37), channel_id=1, source_target_pairs={{0,8},{4,12},{8,0},{12,4},{16,24},{20,28},{24,16},{28,20},{1,9},{5... | collective-permute-start | bytes 786440 | tf_op jit(solution)/shard_map/ppermute | solution.py:578
  10.1 21.4 %collective-permute-start.14 = (s16[512,256]{1,0:T(8,128)(2,1)}, s16[512,256]{1,0:T(8,128)(2,1)}, u32[]{:S(2)}, u32[]{:S(2)}) collective-permute-start(s16[512,256]{1,0:T(8,128)(2,1)} %get-tuple-element.36), channel_id=1, source_target_pairs={{0,16},{4,20},{8,24},{12,28},{16,0},{20,4},{24,8},{28,12},{1,17},{... | collective-permute-start | bytes 786440 | tf_op jit(solution)/shard_map/ppermute | solution.py:578
  11.6 21.5 %collective-permute-start.15 = (s16[512,256]{1,0:T(8,128)(2,1)}, s16[512,256]{1,0:T(8,128)(2,1)}, u32[]{:S(2)}, u32[]{:S(2)}) collective-permute-start(s16[512,256]{1,0:T(8,128)(2,1)} %get-tuple-element.35), channel_id=1, source_target_pairs={{0,24},{4,28},{8,16},{12,20},{16,8},{20,12},{24,0},{28,4},{1,25},{... | collective-permute-start | bytes 786440 | tf_op jit(solution)/shard_map/ppermute | solution.py:578
  18.3 5.5 %copy-start.21 = (s32[4,3]{1,0:T(4,128)S(1)}, s32[4,3]{1,0:T(4,128)}, u32[]{:S(2)}) copy-start(s32[4,3]{1,0:T(4,128)} %param.18) | copy-start | bytes 148
  18.3 5.5 %copy-start.18 = (bf16[2,4,3,128,128]{4,3,2,1,0:T(8,128)(2,1)S(1)}, bf16[2,4,3,128,128]{4,3,2,1,0:T(8,128)(2,1)}, u32[]{:S(2)}) copy-start(bf16[2,4,3,128,128]{4,3,2,1,0:T(8,128)(2,1)} %param.17) | copy-start | bytes 2359300
  18.3 66.7 %all-to-all-start.1 = ((bf16[4,8,128,128]{3,2,1,0:T(8,128)(2,1)}), bf16[4,8,128,128]{3,2,1,0:T(8,128)(2,1)}, u32[]{:S(2)}, u32[]{:S(2)}) async-start(bf16[4,8,128,128]{3,2,1,0:T(8,128)(2,1)} %mask_order.1), calls=%async_computation.1 | async-start | bytes 2097152 | tf_op jit(solution)/shard_map/all_to_all | solution.py:572
  28.3 12.1 %copy-start.6 = (bf16[4,256,384]{2,1,0:T(8,128)(2,1)}, bf16[4,256,384]{2,1,0:T(8,128)(2,1)S(1)}, u32[]{:S(2)}) copy-start(bf16[4,256,384]{2,1,0:T(8,128)(2,1)S(1)} %reshape.39.refs_7_.refs_3_) | copy-start | bytes 2359300
  28.3 16.0 %collective-permute-start.2 = (bf16[2,512,256]{2,1,0:T(8,128)(2,1)}, bf16[2,512,256]{2,1,0:T(8,128)(2,1)S(1)}, u32[]{:S(2)}, u32[]{:S(2)}) collective-permute-start(bf16[2,512,256]{2,1,0:T(8,128)(2,1)} %get-tuple-element.25), channel_id=1, source_target_pairs={{0,24},{4,28},{8,16},{12,20},{16,8},{20,12},{24,0},{28,4},{1,25},{... | collective-permute-start | bytes 1572872 | tf_op jit(solution)/shard_map/ppermute | solution.py:578
  31.5 28.1 %collective-permute-start.4 = (bf16[4,256,384]{2,1,0:T(8,128)(2,1)S(1)}, bf16[4,256,384]{2,1,0:T(8,128)(2,1)S(1)}, u32[]{:S(2)}, u32[]{:S(2)}) collective-permute-start(bf16[4,256,384]{2,1,0:T(8,128)(2,1)S(1)} %reshape.39.refs_7_.refs_3_), channel_id=1, source_target_pairs={{0,4},{4,0},{8,12},{12,8},{16,20},{20,16},{24,28},{28,24},{1,5},{5... | collective-permute-start | bytes 2359304 | tf_op jit(solution)/shard_map/ppermute | solution.py:578
  33.2 25.0 %collective-permute-start.5 = (bf16[4,256,384]{2,1,0:T(8,128)(2,1)S(1)}, bf16[4,256,384]{2,1,0:T(8,128)(2,1)S(1)}, u32[]{:S(2)}, u32[]{:S(2)}) collective-permute-start(bf16[4,256,384]{2,1,0:T(8,128)(2,1)S(1)} %reshape.39.refs_7_.refs_3_), channel_id=1, source_target_pairs={{0,8},{4,12},{8,0},{12,4},{16,24},{20,28},{24,16},{28,20},{1,9},{5... | collective-permute-start | bytes 2359304 | tf_op jit(solution)/shard_map/ppermute | solution.py:578
  36.4 22.6 %collective-permute-start.7 = (bf16[4,256,384]{2,1,0:T(8,128)(2,1)S(1)}, bf16[4,256,384]{2,1,0:T(8,128)(2,1)S(1)}, u32[]{:S(2)}, u32[]{:S(2)}) collective-permute-start(bf16[4,256,384]{2,1,0:T(8,128)(2,1)S(1)} %reshape.39.refs_7_.refs_3_), channel_id=1, source_target_pairs={{0,16},{4,20},{8,24},{12,28},{16,0},{20,4},{24,8},{28,12},{1,17},{... | collective-permute-start | bytes 2359304 | tf_op jit(solution)/shard_map/ppermute | solution.py:578
  38.6 20.4 %collective-permute-start.16 = (s16[4,512,128]{2,1,0:T(8,128)(2,1)S(1)}, s16[4,512,128]{2,1,0:T(8,128)(2,1)S(1)}, u32[]{:S(2)}, u32[]{:S(2)}) collective-permute-start(s16[4,512,128]{2,1,0:T(8,128)(2,1)S(1)} %pad_add_fusion), channel_id=1, source_target_pairs={{0,4},{4,0},{8,12},{12,8},{16,20},{20,16},{24,28},{28,24},{1,5},{5... | collective-permute-start | bytes 1572872 | tf_op jit(solution)/shard_map/ppermute | solution.py:578
  45.1 25.6 %copy-start.22 = (s32[2]{0:T(128)S(1)}, s32[2]{0:T(128)}, u32[]{:S(2)}) copy-start(s32[2]{0:T(128)} %param.21) | copy-start | bytes 28
  45.3 26.1 %collective-permute-start.3 = (bf16[4,2,512,128]{3,2,1,0:T(8,128)(2,1)S(1)}, bf16[4,2,512,128]{3,2,1,0:T(8,128)(2,1)S(1)}, u32[]{:S(2)}, u32[]{:S(2)}) collective-permute-start(bf16[4,2,512,128]{3,2,1,0:T(8,128)(2,1)S(1)} %pad_maximum_fusion), channel_id=1, source_target_pairs={{0,4},{4,0},{8,12},{12,8},{16,20},{20,16},{24,28},{28,24},{1,5},{5... | collective-permute-start | bytes 3145736 | tf_op jit(solution)/shard_map/ppermute | solution.py:578
  58.2 16.3 %copy-start.7 = (bf16[4,256,384]{2,1,0:T(8,128)(2,1)}, bf16[4,256,384]{2,1,0:T(8,128)(2,1)S(1)}, u32[]{:S(2)}) copy-start(bf16[4,256,384]{2,1,0:T(8,128)(2,1)S(1)} %collective-permute-done.5.refs_9_.refs_5_) | copy-start | bytes 2359300
  58.2 8.8 %collective-permute-start.9 = (bf16[2,256,384]{2,1,0:T(8,128)(2,1)S(1)}, bf16[2,256,384]{2,1,0:T(8,128)(2,1)S(1)}, u32[]{:S(2)}, u32[]{:S(2)}) collective-permute-start(bf16[2,256,384]{2,1,0:T(8,128)(2,1)S(1)} %slice.24), channel_id=1, source_target_pairs={{0,16},{4,20},{8,24},{12,28},{16,0},{20,4},{24,8},{28,12},{1,17},{... | collective-permute-start | bytes 1179656 | tf_op jit(solution)/shard_map/ppermute | solution.py:578
  58.9 12.5 %copy-start.8 = (bf16[4,256,384]{2,1,0:T(8,128)(2,1)}, bf16[4,256,384]{2,1,0:T(8,128)(2,1)S(1)}, u32[]{:S(2)}) copy-start(bf16[4,256,384]{2,1,0:T(8,128)(2,1)S(1)} %collective-permute-done.7.refs_11_.refs_7_) | copy-start | bytes 2359300
  58.9 12.4 %collective-permute-start.6 = (bf16[4,256,384]{2,1,0:T(8,128)(2,1)S(1)}, bf16[4,256,384]{2,1,0:T(8,128)(2,1)S(1)}, u32[]{:S(2)}, u32[]{:S(2)}) collective-permute-start(bf16[4,256,384]{2,1,0:T(8,128)(2,1)S(1)} %collective-permute-done.5.refs_9_.refs_5_), channel_id=1, source_target_pairs={{0,4},{4,0},{8,12},{12,8},{16,20},{20,16},{24,28},{28,24},{1,5},{5... | collective-permute-start | bytes 2359304 | tf_op jit(solution)/shard_map/ppermute | solution.py:578
  59.0 15.4 %copy-start.19 = (s16[4,512,128]{2,1,0:T(8,128)(2,1)}, s16[4,512,128]{2,1,0:T(8,128)(2,1)S(1)}, u32[]{:S(2)}) copy-start(s16[4,512,128]{2,1,0:T(8,128)(2,1)S(1)} %collective-permute-done.16.refs_21_) | copy-start | bytes 1572868
  59.0 12.4 %collective-permute-start.8 = (bf16[4,256,384]{2,1,0:T(8,128)(2,1)S(1)}, bf16[4,256,384]{2,1,0:T(8,128)(2,1)S(1)}, u32[]{:S(2)}, u32[]{:S(2)}) collective-permute-start(bf16[4,256,384]{2,1,0:T(8,128)(2,1)S(1)} %collective-permute-done.7.refs_11_.refs_7_), channel_id=1, source_target_pairs={{0,4},{4,0},{8,12},{12,8},{16,20},{20,16},{24,28},{28,24},{1,5},{5... | collective-permute-start | bytes 2359304 | tf_op jit(solution)/shard_map/ppermute | solution.py:578
  59.6 14.8 %copy-start.10 = (bf16[4,256,384]{2,1,0:T(8,128)(2,1)}, bf16[4,256,384]{2,1,0:T(8,128)(2,1)S(1)}, u32[]{:S(2)}) copy-start(bf16[4,256,384]{2,1,0:T(8,128)(2,1)S(1)} %collective-permute-done.4.refs_8_.refs_4_) | copy-start | bytes 2359300
  59.6 11.1 %collective-permute-start.10 = (bf16[2,256,384]{2,1,0:T(8,128)(2,1)S(1)}, bf16[2,256,384]{2,1,0:T(8,128)(2,1)S(1)}, u32[]{:S(2)}, u32[]{:S(2)}) collective-permute-start(bf16[2,256,384]{2,1,0:T(8,128)(2,1)S(1)} %slice.25), channel_id=1, source_target_pairs={{0,8},{4,12},{8,0},{12,4},{16,24},{20,28},{24,16},{28,20},{1,9},{5... | collective-permute-start | bytes 1179656 | tf_op jit(solution)/shard_map/ppermute | solution.py:578
  67.0 7.4 %copy-start.13 = (bf16[2,256,384]{2,1,0:T(8,128)(2,1)}, bf16[2,256,384]{2,1,0:T(8,128)(2,1)S(1)}, u32[]{:S(2)}) copy-start(bf16[2,256,384]{2,1,0:T(8,128)(2,1)S(1)} %collective-permute-done.9.refs_13_.refs_9_) | copy-start | bytes 1179652
  67.0 5.6 %collective-permute-start.11 = (bf16[2,256,384]{2,1,0:T(8,128)(2,1)S(1)}, bf16[2,256,384]{2,1,0:T(8,128)(2,1)S(1)}, u32[]{:S(2)}, u32[]{:S(2)}) collective-permute-start(bf16[2,256,384]{2,1,0:T(8,128)(2,1)S(1)} %collective-permute-done.9.refs_13_.refs_9_), channel_id=1, source_target_pairs={{0,4},{4,0},{8,12},{12,8},{16,20},{20,16},{24,28},{28,24},{1,5},{5... | collective-permute-start | bytes 1179656 | tf_op jit(solution)/shard_map/ppermute | solution.py:578
  70.7 2.8 copy-start.14
  70.7 2.8 collective-permute-start.12
  71.4 3.0 copy-start.17
  147.0 4.2 %copy-start.9 = (s16[1,512,1024]{2,1,0:T(8,128)(2,1)S(1)}, s16[1,512,1024]{2,1,0:T(8,128)(2,1)}, u32[]{:S(2)}) copy-start(s16[1,512,1024]{2,1,0:T(8,128)(2,1)} %get-tuple-element.21) | copy-start | bytes 3145732
  147.0 52.1 %all-to-all-start.2 = ((bf16[32,4,2,32,128]{4,3,2,1,0:T(8,128)(2,1)}), bf16[32,4,2,32,128]{4,3,2,1,0:T(8,128)(2,1)}, u32[]{:S(2)}, u32[]{:S(2)}) async-start(bf16[32,4,2,32,128]{4,3,2,1,0:T(8,128)(2,1)} %row_both.1), calls=%async_computation.2 | async-start | bytes 4194304 | tf_op jit(solution)/shard_map/all_to_all | solution.py:572
  151.3 21.8 %collective-permute-start.17 = (s16[512,256]{1,0:T(8,128)(2,1)S(1)}, s16[512,256]{1,0:T(8,128)(2,1)S(1)}, u32[]{:S(2)}, u32[]{:S(2)}) collective-permute-start(s16[512,256]{1,0:T(8,128)(2,1)S(1)} %get-tuple-element.32), channel_id=1, source_target_pairs={{0,8},{4,12},{8,0},{12,4},{16,24},{20,28},{24,16},{28,20},{1,9},{5... | collective-permute-start | bytes 786440 | tf_op jit(solution)/shard_map/ppermute | solution.py:578
  152.8 20.9 %collective-permute-start.18 = (s16[512,256]{1,0:T(8,128)(2,1)S(1)}, s16[512,256]{1,0:T(8,128)(2,1)S(1)}, u32[]{:S(2)}, u32[]{:S(2)}) collective-permute-start(s16[512,256]{1,0:T(8,128)(2,1)S(1)} %get-tuple-element.31), channel_id=1, source_target_pairs={{0,16},{4,20},{8,24},{12,28},{16,0},{20,4},{24,8},{28,12},{1,17},{... | collective-permute-start | bytes 786440 | tf_op jit(solution)/shard_map/ppermute | solution.py:578
  153.4 29.9 %collective-permute-start.19 = (s16[512,256]{1,0:T(8,128)(2,1)S(1)}, s16[512,256]{1,0:T(8,128)(2,1)S(1)}, u32[]{:S(2)}, u32[]{:S(2)}) collective-permute-start(s16[512,256]{1,0:T(8,128)(2,1)S(1)} %get-tuple-element.30), channel_id=1, source_target_pairs={{0,24},{4,28},{8,16},{12,20},{16,8},{20,12},{24,0},{28,4},{1,25},{... | collective-permute-start | bytes 786440 | tf_op jit(solution)/shard_map/ppermute | solution.py:578
  184.0 2.0 collective-permute-start.20
  186.0 13.1 %copy-start.20 = (s16[4,512,128]{2,1,0:T(8,128)(2,1)}, s16[4,512,128]{2,1,0:T(8,128)(2,1)S(1)}, u32[]{:S(2)}) copy-start(s16[4,512,128]{2,1,0:T(8,128)(2,1)S(1)} %collective-permute-done.20.refs_17_) | copy-start | bytes 1572868
  212.4 51.8 %all-to-all-start.3 = ((bf16[32,4,2,32,128]{4,3,2,1,0:T(8,128)(2,1)}), bf16[32,4,2,32,128]{4,3,2,1,0:T(8,128)(2,1)}, u32[]{:S(2)}, u32[]{:S(2)}) async-start(bf16[32,4,2,32,128]{4,3,2,1,0:T(8,128)(2,1)} %bitcast.43), calls=%async_computation.3 | async-start | bytes 4194304 | tf_op jit(solution)/shard_map/all_to_all | solution.py:572
  268.6 39.1 %copy-start.3 = (bf16[256,256]{1,0:T(8,128)(2,1)S(1)}, bf16[256,256]{1,0:T(8,128)(2,1)}, u32[]{:S(2)}) copy-start(bf16[256,256]{1,0:T(8,128)(2,1)} %constant.201.clone.refs_6_) | copy-start | bytes 393220
  268.7 39.1 %copy-start.5 = (bf16[2,8,64,128]{3,2,1,0:T(8,128)(2,1)S(1)}, bf16[2,8,64,128]{3,2,1,0:T(8,128)(2,1)}, u32[]{:S(2)}) copy-start(bf16[2,8,64,128]{3,2,1,0:T(8,128)(2,1)} %get-tuple-element.17.refs_1_) | copy-start | bytes 786436
  268.7 11.1 %collective-permute-start.24 = (bf16[2,8,64,128]{3,2,1,0:T(8,128)(2,1)}, bf16[2,8,64,128]{3,2,1,0:T(8,128)(2,1)S(1)}, u32[]{:S(2)}, u32[]{:S(2)}) collective-permute-start(bf16[2,8,64,128]{3,2,1,0:T(8,128)(2,1)} %get-tuple-element.18), channel_id=1, source_target_pairs={{0,1},{1,0},{2,3},{3,2},{4,5},{5,4},{6,7},{7,6},{8,9},{9,8},{10,11... | collective-permute-start | bytes 786440 | tf_op jit(solution)/shard_map/ppermute | solution.py:578
  268.7 20.2 %collective-permute-start.25 = (bf16[2,8,64,128]{3,2,1,0:T(8,128)(2,1)}, bf16[2,8,64,128]{3,2,1,0:T(8,128)(2,1)S(1)}, u32[]{:S(2)}, u32[]{:S(2)}) collective-permute-start(bf16[2,8,64,128]{3,2,1,0:T(8,128)(2,1)} %get-tuple-element.19), channel_id=1, source_target_pairs={{0,2},{1,3},{2,0},{3,1},{4,6},{5,7},{6,4},{7,5},{8,10},{9,11},{10,... | collective-permute-start | bytes 786440 | tf_op jit(solution)/shard_map/ppermute | solution.py:578
  270.8 37.0 %collective-permute-start.26 = (bf16[2,8,64,128]{3,2,1,0:T(8,128)(2,1)}, bf16[2,8,64,128]{3,2,1,0:T(8,128)(2,1)S(1)}, u32[]{:S(2)}, u32[]{:S(2)}) collective-permute-start(bf16[2,8,64,128]{3,2,1,0:T(8,128)(2,1)} %get-tuple-element.20), channel_id=1, source_target_pairs={{0,3},{1,2},{2,1},{3,0},{4,7},{5,6},{6,5},{7,4},{8,11},{9,10},{10,... | collective-permute-start | bytes 786440 | tf_op jit(solution)/shard_map/ppermute | solution.py:578
  276.7 37.3 %collective-permute-start.21 = (bf16[2,8,64,128]{3,2,1,0:T(8,128)(2,1)}, bf16[2,8,64,128]{3,2,1,0:T(8,128)(2,1)S(1)}, u32[]{:S(2)}, u32[]{:S(2)}) collective-permute-start(bf16[2,8,64,128]{3,2,1,0:T(8,128)(2,1)} %get-tuple-element.14), channel_id=1, source_target_pairs={{0,1},{1,0},{2,3},{3,2},{4,5},{5,4},{6,7},{7,6},{8,9},{9,8},{10,11... | collective-permute-start | bytes 786440 | tf_op jit(solution)/shard_map/ppermute | solution.py:578
  277.7 36.3 %collective-permute-start.22 = (bf16[2,8,64,128]{3,2,1,0:T(8,128)(2,1)}, bf16[2,8,64,128]{3,2,1,0:T(8,128)(2,1)S(1)}, u32[]{:S(2)}, u32[]{:S(2)}) collective-permute-start(bf16[2,8,64,128]{3,2,1,0:T(8,128)(2,1)} %get-tuple-element.15), channel_id=1, source_target_pairs={{0,2},{1,3},{2,0},{3,1},{4,6},{5,7},{6,4},{7,5},{8,10},{9,11},{10,... | collective-permute-start | bytes 786440 | tf_op jit(solution)/shard_map/ppermute | solution.py:578
  279.8 38.1 %collective-permute-start.23 = (bf16[2,8,64,128]{3,2,1,0:T(8,128)(2,1)}, bf16[2,8,64,128]{3,2,1,0:T(8,128)(2,1)S(1)}, u32[]{:S(2)}, u32[]{:S(2)}) collective-permute-start(bf16[2,8,64,128]{3,2,1,0:T(8,128)(2,1)} %get-tuple-element.16), channel_id=1, source_target_pairs={{0,3},{1,2},{2,1},{3,0},{4,7},{5,6},{6,5},{7,4},{8,11},{9,10},{10,... | collective-permute-start | bytes 786440 | tf_op jit(solution)/shard_map/ppermute | solution.py:578
  307.7 1.6 copy-start
  310.9 7.0 %copy-start.2 = (bf16[1024,1024]{1,0:T(8,128)(2,1)S(1)}, bf16[1024,1024]{1,0:T(8,128)(2,1)}, u32[]{:S(2)}) copy-start(bf16[1024,1024]{1,0:T(8,128)(2,1)} %constant.202.clone.refs_7_) | copy-start | bytes 6291460
  310.9 7.0 %copy-start.4 = (bf16[2,8,64,128]{3,2,1,0:T(8,128)(2,1)S(1)}, bf16[2,8,64,128]{3,2,1,0:T(8,128)(2,1)}, u32[]{:S(2)}) copy-start(bf16[2,8,64,128]{3,2,1,0:T(8,128)(2,1)} %get-tuple-element.13.refs_1_) | copy-start | bytes 786436
  (5 other events, 5.3 us)

commit v6 on v5

--- a/solution.py
+++ b/solution.py
@@ -264,7 +264,7 @@
             real, imag = (jnp.concatenate([parts[0][one][c], parts[1][one][c]], axis=0) for c in range(2))
             mixed[one, aligned(at * 16, 16)] = jnp.concatenate([real, imag], axis=1).astype(BF16)
 
-    loop(part // 16, mix)
+    loop(part // 16, mix, 2)
     for group in range(cols_at):
         table_copies[group].wait()
 

time: 322 us -> 322 us (level)
  no operation moved by 1% of the time
where the time goes in v6:
time: 322 us; the launch traced here: 321 us
  waiting for transfers between devices  147 us (46%)
  Pallas kernels  52.9 us (16%)
  blocking collectives  52.9 us (16%)
  starting transfers between devices  35.9 us (11%)
  local copies, waits for them, and re-layouts  28.3 us (9%)
    ppermute x27, waiting for transfers between devices, swap(): lax.ppermute(value, axis, [(at, at ^ distance) for at in range(lax.axis_s...  86.2 us
    all_to_all x3, waiting for transfers between devices, exchange(): return lax.all_to_all(value, axis, split_axis=0, concat_axis=0, tiled=True)  61.1 us
    all_to_all x1, blocking collectives, exchange(): return lax.all_to_all(value, axis, split_axis=0, concat_axis=0, tiled=True)  52.9 us
    pallas_call x2, Pallas kernels, column_work(): pl.pallas_call(body, out_shape=sent, in_specs=[smem, smem] + [anywhere] *...  23.6 us
    ppermute x27, starting transfers between devices, swap(): lax.ppermute(value, axis, [(at, at ^ distance) for at in range(lax.axis_s...  22.4 us
    all_to_all x3, starting transfers between devices, exchange(): return lax.all_to_all(value, axis, split_axis=0, concat_axis=0, tiled=True)  13.4 us
    another operation x10, local copies, waits for them, and re-layouts, spread(): jnp.stack([part(piece, 1 - core) for piece in chips])  13.4 us
    pallas_call x1, Pallas kernels, row_work(): pl.pallas_call(body, out_shape=jax.ShapeDtypeStruct(received.shape, BF16)...  9.12 us
  transfers between devices with their start and end apart: 30, of which 14 were waited for; matrix products, arithmetic and copies ran while one was open for 7% of the time, Pallas kernels for 7%

profile of v6, /device:TPU:12, one launch (start us, length us, event | category | flops | bytes accessed | tf_op | source)
XLA Modules:
  0.0 320.8 jit_solution(13356843470804567229)
XLA Ops:
  0.0 2.6 constant_dynamic-slice_fusion.9
  2.6 1.5 collective-permute-start
  4.6 2.9 round-nearest-even_convert_fusion
  7.5 1.2 fusion
  10.1 1.5 collective-permute-start.14
  11.6 1.4 collective-permute-start.15
  13.1 5.2 %mask_order.1 = bf16[4,8,128,128]{3,2,1,0:T(8,128)(2,1)} custom-call(f32[512,1024]{1,0:T(8,128)} %refs_5_.3, bf16[512,512]{1,0:T(8,128)(2,1)} %constant.199.clone.down_ref, bf16[1024,1024]{1,0:T(8,128)(2,1)} %constant.200.clone.across_ref), custom_call_target="tpu_custom_call" | custom-call | tf_op jit(solution)/shard_map/mask_order/pallas_call | solution.py:510
  18.3 5.4 %all-to-all-start.1 = ((bf16[4,8,128,128]{3,2,1,0:T(8,128)(2,1)}), bf16[4,8,128,128]{3,2,1,0:T(8,128)(2,1)}, u32[]{:S(2)}, u32[]{:S(2)}) async-start(bf16[4,8,128,128]{3,2,1,0:T(8,128)(2,1)} %mask_order.1), calls=%async_computation.1 | async-start | bytes 2097152 | tf_op jit(solution)/shard_map/all_to_all | solution.py:572
  23.9 2.1 dynamic-slice_bitcast_fusion.9
  28.3 1.6 collective-permute-start.2
  29.9 1.7 dynamic-slice_bitcast_fusion.16
  31.5 1.6 dynamic-slice_bitcast_fusion.15
  33.2 1.5 collective-permute-start.5
  34.7 1.6 dynamic-slice_bitcast_fusion.14
  36.8 1.8 dynamic-slice_bitcast_fusion.8
  38.6 1.8 dynamic-slice_bitcast_fusion.7
  40.4 3.9 %collective-permute-done.2 = bf16[2,512,256]{2,1,0:T(8,128)(2,1)S(1)} collective-permute-done((bf16[2,512,256]{2,1,0:T(8,128)(2,1)}, bf16[2,512,256]{2,1,0:T(8,128)(2,1)S(1)}, u32[]{:S(2)}, u32[]{:S(2)}) %collective-permute-start.2) | collective-permute-done | bytes 524320 | tf_op jit(solution)/shard_map/ppermute | solution.py:578
  45.4 12.8 %collective-permute-done.5.refs_9_.refs_5_ = bf16[4,256,384]{2,1,0:T(8,128)(2,1)S(1)} collective-permute-done((bf16[4,256,384]{2,1,0:T(8,128)(2,1)S(1)}, bf16[4,256,384]{2,1,0:T(8,128)(2,1)S(1)}, u32[]{:S(2)}, u32[]{:S(2)}) %collective-permute-start.5) | collective-permute-done | bytes 786464 | tf_op jit(solution)/shard_map/ppermute | solution.py:578
  60.1 7.0 %collective-permute-done.9.refs_13_.refs_9_ = bf16[2,256,384]{2,1,0:T(8,128)(2,1)S(1)} collective-permute-done((bf16[2,256,384]{2,1,0:T(8,128)(2,1)S(1)}, bf16[2,256,384]{2,1,0:T(8,128)(2,1)S(1)}, u32[]{:S(2)}, u32[]{:S(2)}) %collective-permute-start.9) | collective-permute-done | bytes 393248 | tf_op jit(solution)/shard_map/ppermute | solution.py:578
  67.0 3.7 %collective-permute-done.10.refs_14_.refs_10_ = bf16[2,256,384]{2,1,0:T(8,128)(2,1)S(1)} collective-permute-done((bf16[2,256,384]{2,1,0:T(8,128)(2,1)S(1)}, bf16[2,256,384]{2,1,0:T(8,128)(2,1)S(1)}, u32[]{:S(2)}, u32[]{:S(2)}) %collective-permute-start.10) | collective-permute-done | bytes 393248 | tf_op jit(solution)/shard_map/ppermute | solution.py:578
  71.4 1.2 copy-done.11
  74.4 10.6 %column_first.1 = bf16[8,4,4,2,32,128]{5,4,3,2,1,0:T(8,128)(2,1)} custom-call(s32[1]{0:T(128)} %bitcast.1.refs_0_, s32[1]{0:T(128)} %get-tuple-element.56.refs_1_, bf16[2,512,128]{2,1,0:T(8,128)(2,1)} %get-tuple-element.24.refs_2_, bf16[2,512,128]{2,1,0:T(8,128)(2,1)} %get-tuple-element.39.refs_3_, bf16[2,512,128]{2,1,0:T(8,128)(2,1)} %get-tuple-element.41.refs_4_, ...), custom_call_target="tpu_custom_call" | custom-call | tf_op jit(solution)/shard_map/column_first/pallas_call | solution.py:300
  85.0 52.9 %all_to_all.20.refs_0_ = bf16[32,4,2,32,128]{4,3,2,1,0:T(8,128)(2,1)} all-to-all(bf16[32,4,2,32,128]{4,3,2,1,0:T(8,128)(2,1)} %bitcast.44), channel_id=1, replica_groups=mesh['rows'=8,'cols'=4] {'rows','cols'}, dimensions={0} | all-to-all | bytes 4194304 | tf_op jit(solution)/shard_map/all_to_all | solution.py:572
  138.0 9.1 %row_both.1 = bf16[32,4,2,32,128]{4,3,2,1,0:T(8,128)(2,1)} custom-call(bf16[32,4,2,32,128]{4,3,2,1,0:T(8,128)(2,1)} %all_to_all.20.refs_0_, bf16[4,8,128,128]{3,2,1,0:T(8,128)(2,1)} %all-to-all-done.1.refs_1_, bf16[4,512,256]{2,1,0:T(8,128)(2,1)} %constant.197.clone.refs_2_, f32[8,2,1,512]{3,2,1,0:T(1,128)} %constant.198.clone.refs_3_), custom_call_target="tpu_custom_call" | custom-call | tf_op jit(solution)/shard_map/row_both/pallas_call | solution.py:425
  147.1 4.1 %all-to-all-start.2 = ((bf16[32,4,2,32,128]{4,3,2,1,0:T(8,128)(2,1)}), bf16[32,4,2,32,128]{4,3,2,1,0:T(8,128)(2,1)}, u32[]{:S(2)}, u32[]{:S(2)}) async-start(bf16[32,4,2,32,128]{4,3,2,1,0:T(8,128)(2,1)} %row_both.1), calls=%async_computation.2 | async-start | bytes 4194304 | tf_op jit(solution)/shard_map/all_to_all | solution.py:572
  151.4 1.5 collective-permute-start.17
  153.5 1.5 collective-permute-start.19
  155.8 17.4 %collective-permute-done.17 = s16[512,256]{1,0:T(8,128)(2,1)S(1)} collective-permute-done((s16[512,256]{1,0:T(8,128)(2,1)S(1)}, s16[512,256]{1,0:T(8,128)(2,1)S(1)}, u32[]{:S(2)}, u32[]{:S(2)}) %collective-permute-start.17) | collective-permute-done | bytes 262176 | tf_op jit(solution)/shard_map/ppermute | solution.py:578
  174.5 8.9 %collective-permute-done.19 = s16[512,256]{1,0:T(8,128)(2,1)S(1)} collective-permute-done((s16[512,256]{1,0:T(8,128)(2,1)S(1)}, s16[512,256]{1,0:T(8,128)(2,1)S(1)}, u32[]{:S(2)}, u32[]{:S(2)}) %collective-permute-start.19) | collective-permute-done | bytes 262176 | tf_op jit(solution)/shard_map/ppermute | solution.py:578
  184.2 1.9 collective-permute-done.20.refs_17_
  186.1 13.1 %all-to-all-done.2 = bf16[32,4,2,32,128]{4,3,2,1,0:T(8,128)(2,1)} async-done(((bf16[32,4,2,32,128]{4,3,2,1,0:T(8,128)(2,1)}), bf16[32,4,2,32,128]{4,3,2,1,0:T(8,128)(2,1)}, u32[]{:S(2)}, u32[]{:S(2)}) %all-to-all-start.2) | async-done | bytes 2097184 | tf_op jit(solution)/shard_map/all_to_all | solution.py:572
  199.2 13.1 %column_later.1 = bf16[8,4,4,2,32,128]{5,4,3,2,1,0:T(8,128)(2,1)} custom-call(s32[1]{0:T(128)} %bitcast.1.refs_0_, s32[1]{0:T(128)} %get-tuple-element.57.refs_1_, bf16[8,4,4,2,32,128]{5,4,3,2,1,0:T(8,128)(2,1)} %bitcast.15.refs_2_, bf16[4,256,384]{2,1,0:T(8,128)(2,1)} %copy-done.6, bf16[4,256,384]{2,1,0:T(8,128)(2,1)} %copy-done.10, ...), custom_call_target="tpu_custom_call" | custom-call | tf_op jit(solution)/shard_map/column_later/pallas_call | solution.py:300
  212.3 3.9 %all-to-all-start.3 = ((bf16[32,4,2,32,128]{4,3,2,1,0:T(8,128)(2,1)}), bf16[32,4,2,32,128]{4,3,2,1,0:T(8,128)(2,1)}, u32[]{:S(2)}, u32[]{:S(2)}) async-start(bf16[32,4,2,32,128]{4,3,2,1,0:T(8,128)(2,1)} %bitcast.43), calls=%async_computation.3 | async-start | bytes 4194304 | tf_op jit(solution)/shard_map/all_to_all | solution.py:572
  216.1 48.0 %all-to-all-done.3.refs_1_ = bf16[32,4,2,32,128]{4,3,2,1,0:T(8,128)(2,1)} async-done(((bf16[32,4,2,32,128]{4,3,2,1,0:T(8,128)(2,1)}), bf16[32,4,2,32,128]{4,3,2,1,0:T(8,128)(2,1)}, u32[]{:S(2)}, u32[]{:S(2)}) %all-to-all-start.3) | async-done | bytes 2097184 | tf_op jit(solution)/shard_map/all_to_all | solution.py:572
  264.1 4.4 %row_last.3 = (bf16[2,8,64,128]{3,2,1,0:T(8,128)(2,1)}, bf16[2,8,64,128]{3,2,1,0:T(8,128)(2,1)}, bf16[2,8,64,128]{3,2,1,0:T(8,128)(2,1)}, bf16[2,8,64,128]{3,2,1,0:T(8,128)(2,1)}) custom-call(s32[1]{0:T(128)} %bitcast.refs_0_, bf16[32,4,2,32,128]{4,3,2,1,0:T(8,128)(2,1)} %all-to-all-done.3.refs_1_, bf16[4,512,256]{2,1,0:T(8,128)(2,1)} %constant.197.clone.refs_2_, ...), custom_call_target="tpu_custom_call" | custom-call | flops 1073741824 | bytes 4194304 | tf_op jit(solution)/shard_map/row_last/pallas_call | solution.py:479
  268.6 2.0 collective-permute-start.25
  270.6 1.5 collective-permute-start.26
  272.1 4.4 %row_last.2 = (bf16[2,8,64,128]{3,2,1,0:T(8,128)(2,1)}, bf16[2,8,64,128]{3,2,1,0:T(8,128)(2,1)}, bf16[2,8,64,128]{3,2,1,0:T(8,128)(2,1)}, bf16[2,8,64,128]{3,2,1,0:T(8,128)(2,1)}) custom-call(s32[1]{0:T(128)} %bitcast.refs_0_, bf16[32,4,2,32,128]{4,3,2,1,0:T(8,128)(2,1)} %all-to-all-done.3.refs_1_, bf16[4,512,256]{2,1,0:T(8,128)(2,1)} %constant.197.clone.refs_2_, ...), custom_call_target="tpu_custom_call" | custom-call | flops 1073741824 | bytes 4194304 | tf_op jit(solution)/shard_map/row_last/pallas_call | solution.py:479
  277.6 1.0 collective-permute-start.22
  278.6 1.1 collective-permute-done.24.refs_2_
  279.7 2.5 collective-permute-start.23
  282.2 6.7 %collective-permute-done.25.refs_3_ = bf16[2,8,64,128]{3,2,1,0:T(8,128)(2,1)S(1)} collective-permute-done((bf16[2,8,64,128]{3,2,1,0:T(8,128)(2,1)}, bf16[2,8,64,128]{3,2,1,0:T(8,128)(2,1)S(1)}, u32[]{:S(2)}, u32[]{:S(2)}) %collective-permute-start.25) | collective-permute-done | bytes 262176 | tf_op jit(solution)/shard_map/ppermute | solution.py:578
  288.9 18.8 %collective-permute-done.26.refs_4_ = bf16[2,8,64,128]{3,2,1,0:T(8,128)(2,1)S(1)} collective-permute-done((bf16[2,8,64,128]{3,2,1,0:T(8,128)(2,1)}, bf16[2,8,64,128]{3,2,1,0:T(8,128)(2,1)S(1)}, u32[]{:S(2)}, u32[]{:S(2)}) %collective-permute-start.26) | collective-permute-done | bytes 262176 | tf_op jit(solution)/shard_map/ppermute | solution.py:578
  307.6 1.6 copy-done
  309.2 1.6 copy-done.1
  310.8 3.0 closing_order.2.refs_8_
  313.9 3.9 %collective-permute-done.23.refs_4_ = bf16[2,8,64,128]{3,2,1,0:T(8,128)(2,1)S(1)} collective-permute-done((bf16[2,8,64,128]{3,2,1,0:T(8,128)(2,1)}, bf16[2,8,64,128]{3,2,1,0:T(8,128)(2,1)S(1)}, u32[]{:S(2)}, u32[]{:S(2)}) %collective-permute-start.23) | collective-permute-done | bytes 262176 | tf_op jit(solution)/shard_map/ppermute | solution.py:578
  317.8 3.0 closing_order.3
  (94 shorter events, 15.0 us)
Async XLA Ops:
  2.6 33.8 %collective-permute-start = (bf16[2,512,256]{2,1,0:T(8,128)(2,1)}, bf16[2,512,256]{2,1,0:T(8,128)(2,1)}, u32[]{:S(2)}, u32[]{:S(2)}) collective-permute-start(bf16[2,512,256]{2,1,0:T(8,128)(2,1)} %get-tuple-element.27), channel_id=1, source_target_pairs={{0,8},{4,12},{8,0},{12,4},{16,24},{20,28},{24,16},{28,20},{1,9},{5... | collective-permute-start | bytes 1572872 | tf_op jit(solution)/shard_map/ppermute | solution.py:578
  4.0 34.6 %collective-permute-start.1 = (bf16[2,512,256]{2,1,0:T(8,128)(2,1)}, bf16[2,512,256]{2,1,0:T(8,128)(2,1)}, u32[]{:S(2)}, u32[]{:S(2)}) collective-permute-start(bf16[2,512,256]{2,1,0:T(8,128)(2,1)} %get-tuple-element.26), channel_id=1, source_target_pairs={{0,16},{4,20},{8,24},{12,28},{16,0},{20,4},{24,8},{28,12},{1,17},{... | collective-permute-start | bytes 1572872 | tf_op jit(solution)/shard_map/ppermute | solution.py:578
  9.6 18.7 %collective-permute-start.13 = (s16[512,256]{1,0:T(8,128)(2,1)}, s16[512,256]{1,0:T(8,128)(2,1)}, u32[]{:S(2)}, u32[]{:S(2)}) collective-permute-start(s16[512,256]{1,0:T(8,128)(2,1)} %get-tuple-element.37), channel_id=1, source_target_pairs={{0,8},{4,12},{8,0},{12,4},{16,24},{20,28},{24,16},{28,20},{1,9},{5... | collective-permute-start | bytes 786440 | tf_op jit(solution)/shard_map/ppermute | solution.py:578
  10.1 21.4 %collective-permute-start.14 = (s16[512,256]{1,0:T(8,128)(2,1)}, s16[512,256]{1,0:T(8,128)(2,1)}, u32[]{:S(2)}, u32[]{:S(2)}) collective-permute-start(s16[512,256]{1,0:T(8,128)(2,1)} %get-tuple-element.36), channel_id=1, source_target_pairs={{0,16},{4,20},{8,24},{12,28},{16,0},{20,4},{24,8},{28,12},{1,17},{... | collective-permute-start | bytes 786440 | tf_op jit(solution)/shard_map/ppermute | solution.py:578
  11.6 21.5 %collective-permute-start.15 = (s16[512,256]{1,0:T(8,128)(2,1)}, s16[512,256]{1,0:T(8,128)(2,1)}, u32[]{:S(2)}, u32[]{:S(2)}) collective-permute-start(s16[512,256]{1,0:T(8,128)(2,1)} %get-tuple-element.35), channel_id=1, source_target_pairs={{0,24},{4,28},{8,16},{12,20},{16,8},{20,12},{24,0},{28,4},{1,25},{... | collective-permute-start | bytes 786440 | tf_op jit(solution)/shard_map/ppermute | solution.py:578
  18.3 5.5 %copy-start.21 = (s32[4,3]{1,0:T(4,128)S(1)}, s32[4,3]{1,0:T(4,128)}, u32[]{:S(2)}) copy-start(s32[4,3]{1,0:T(4,128)} %param.18) | copy-start | bytes 148
  18.3 5.5 %copy-start.18 = (bf16[2,4,3,128,128]{4,3,2,1,0:T(8,128)(2,1)S(1)}, bf16[2,4,3,128,128]{4,3,2,1,0:T(8,128)(2,1)}, u32[]{:S(2)}) copy-start(bf16[2,4,3,128,128]{4,3,2,1,0:T(8,128)(2,1)} %param.17) | copy-start | bytes 2359300
  18.3 66.8 %all-to-all-start.1 = ((bf16[4,8,128,128]{3,2,1,0:T(8,128)(2,1)}), bf16[4,8,128,128]{3,2,1,0:T(8,128)(2,1)}, u32[]{:S(2)}, u32[]{:S(2)}) async-start(bf16[4,8,128,128]{3,2,1,0:T(8,128)(2,1)} %mask_order.1), calls=%async_computation.1 | async-start | bytes 2097152 | tf_op jit(solution)/shard_map/all_to_all | solution.py:572
  28.3 12.1 %copy-start.6 = (bf16[4,256,384]{2,1,0:T(8,128)(2,1)}, bf16[4,256,384]{2,1,0:T(8,128)(2,1)S(1)}, u32[]{:S(2)}) copy-start(bf16[4,256,384]{2,1,0:T(8,128)(2,1)S(1)} %reshape.39.refs_7_.refs_3_) | copy-start | bytes 2359300
  28.3 16.0 %collective-permute-start.2 = (bf16[2,512,256]{2,1,0:T(8,128)(2,1)}, bf16[2,512,256]{2,1,0:T(8,128)(2,1)S(1)}, u32[]{:S(2)}, u32[]{:S(2)}) collective-permute-start(bf16[2,512,256]{2,1,0:T(8,128)(2,1)} %get-tuple-element.25), channel_id=1, source_target_pairs={{0,24},{4,28},{8,16},{12,20},{16,8},{20,12},{24,0},{28,4},{1,25},{... | collective-permute-start | bytes 1572872 | tf_op jit(solution)/shard_map/ppermute | solution.py:578
  31.5 28.1 %collective-permute-start.4 = (bf16[4,256,384]{2,1,0:T(8,128)(2,1)S(1)}, bf16[4,256,384]{2,1,0:T(8,128)(2,1)S(1)}, u32[]{:S(2)}, u32[]{:S(2)}) collective-permute-start(bf16[4,256,384]{2,1,0:T(8,128)(2,1)S(1)} %reshape.39.refs_7_.refs_3_), channel_id=1, source_target_pairs={{0,4},{4,0},{8,12},{12,8},{16,20},{20,16},{24,28},{28,24},{1,5},{5... | collective-permute-start | bytes 2359304 | tf_op jit(solution)/shard_map/ppermute | solution.py:578
  33.2 25.0 %collective-permute-start.5 = (bf16[4,256,384]{2,1,0:T(8,128)(2,1)S(1)}, bf16[4,256,384]{2,1,0:T(8,128)(2,1)S(1)}, u32[]{:S(2)}, u32[]{:S(2)}) collective-permute-start(bf16[4,256,384]{2,1,0:T(8,128)(2,1)S(1)} %reshape.39.refs_7_.refs_3_), channel_id=1, source_target_pairs={{0,8},{4,12},{8,0},{12,4},{16,24},{20,28},{24,16},{28,20},{1,9},{5... | collective-permute-start | bytes 2359304 | tf_op jit(solution)/shard_map/ppermute | solution.py:578
  36.4 22.6 %collective-permute-start.7 = (bf16[4,256,384]{2,1,0:T(8,128)(2,1)S(1)}, bf16[4,256,384]{2,1,0:T(8,128)(2,1)S(1)}, u32[]{:S(2)}, u32[]{:S(2)}) collective-permute-start(bf16[4,256,384]{2,1,0:T(8,128)(2,1)S(1)} %reshape.39.refs_7_.refs_3_), channel_id=1, source_target_pairs={{0,16},{4,20},{8,24},{12,28},{16,0},{20,4},{24,8},{28,12},{1,17},{... | collective-permute-start | bytes 2359304 | tf_op jit(solution)/shard_map/ppermute | solution.py:578
  38.6 20.4 %collective-permute-start.16 = (s16[4,512,128]{2,1,0:T(8,128)(2,1)S(1)}, s16[4,512,128]{2,1,0:T(8,128)(2,1)S(1)}, u32[]{:S(2)}, u32[]{:S(2)}) collective-permute-start(s16[4,512,128]{2,1,0:T(8,128)(2,1)S(1)} %pad_add_fusion), channel_id=1, source_target_pairs={{0,4},{4,0},{8,12},{12,8},{16,20},{20,16},{24,28},{28,24},{1,5},{5... | collective-permute-start | bytes 1572872 | tf_op jit(solution)/shard_map/ppermute | solution.py:578
  45.1 25.6 %copy-start.22 = (s32[2]{0:T(128)S(1)}, s32[2]{0:T(128)}, u32[]{:S(2)}) copy-start(s32[2]{0:T(128)} %param.21) | copy-start | bytes 28
  45.3 26.1 %collective-permute-start.3 = (bf16[4,2,512,128]{3,2,1,0:T(8,128)(2,1)S(1)}, bf16[4,2,512,128]{3,2,1,0:T(8,128)(2,1)S(1)}, u32[]{:S(2)}, u32[]{:S(2)}) collective-permute-start(bf16[4,2,512,128]{3,2,1,0:T(8,128)(2,1)S(1)} %pad_maximum_fusion), channel_id=1, source_target_pairs={{0,4},{4,0},{8,12},{12,8},{16,20},{20,16},{24,28},{28,24},{1,5},{5... | collective-permute-start | bytes 3145736 | tf_op jit(solution)/shard_map/ppermute | solution.py:578
  58.2 16.3 %copy-start.7 = (bf16[4,256,384]{2,1,0:T(8,128)(2,1)}, bf16[4,256,384]{2,1,0:T(8,128)(2,1)S(1)}, u32[]{:S(2)}) copy-start(bf16[4,256,384]{2,1,0:T(8,128)(2,1)S(1)} %collective-permute-done.5.refs_9_.refs_5_) | copy-start | bytes 2359300
  58.2 8.8 %collective-permute-start.9 = (bf16[2,256,384]{2,1,0:T(8,128)(2,1)S(1)}, bf16[2,256,384]{2,1,0:T(8,128)(2,1)S(1)}, u32[]{:S(2)}, u32[]{:S(2)}) collective-permute-start(bf16[2,256,384]{2,1,0:T(8,128)(2,1)S(1)} %slice.24), channel_id=1, source_target_pairs={{0,16},{4,20},{8,24},{12,28},{16,0},{20,4},{24,8},{28,12},{1,17},{... | collective-permute-start | bytes 1179656 | tf_op jit(solution)/shard_map/ppermute | solution.py:578
  58.9 12.5 %copy-start.8 = (bf16[4,256,384]{2,1,0:T(8,128)(2,1)}, bf16[4,256,384]{2,1,0:T(8,128)(2,1)S(1)}, u32[]{:S(2)}) copy-start(bf16[4,256,384]{2,1,0:T(8,128)(2,1)S(1)} %collective-permute-done.7.refs_11_.refs_7_) | copy-start | bytes 2359300
  58.9 12.4 %collective-permute-start.6 = (bf16[4,256,384]{2,1,0:T(8,128)(2,1)S(1)}, bf16[4,256,384]{2,1,0:T(8,128)(2,1)S(1)}, u32[]{:S(2)}, u32[]{:S(2)}) collective-permute-start(bf16[4,256,384]{2,1,0:T(8,128)(2,1)S(1)} %collective-permute-done.5.refs_9_.refs_5_), channel_id=1, source_target_pairs={{0,4},{4,0},{8,12},{12,8},{16,20},{20,16},{24,28},{28,24},{1,5},{5... | collective-permute-start | bytes 2359304 | tf_op jit(solution)/shard_map/ppermute | solution.py:578
  59.0 15.4 %copy-start.19 = (s16[4,512,128]{2,1,0:T(8,128)(2,1)}, s16[4,512,128]{2,1,0:T(8,128)(2,1)S(1)}, u32[]{:S(2)}) copy-start(s16[4,512,128]{2,1,0:T(8,128)(2,1)S(1)} %collective-permute-done.16.refs_21_) | copy-start | bytes 1572868
  59.0 12.4 %collective-permute-start.8 = (bf16[4,256,384]{2,1,0:T(8,128)(2,1)S(1)}, bf16[4,256,384]{2,1,0:T(8,128)(2,1)S(1)}, u32[]{:S(2)}, u32[]{:S(2)}) collective-permute-start(bf16[4,256,384]{2,1,0:T(8,128)(2,1)S(1)} %collective-permute-done.7.refs_11_.refs_7_), channel_id=1, source_target_pairs={{0,4},{4,0},{8,12},{12,8},{16,20},{20,16},{24,28},{28,24},{1,5},{5... | collective-permute-start | bytes 2359304 | tf_op jit(solution)/shard_map/ppermute | solution.py:578
  59.6 14.8 %copy-start.10 = (bf16[4,256,384]{2,1,0:T(8,128)(2,1)}, bf16[4,256,384]{2,1,0:T(8,128)(2,1)S(1)}, u32[]{:S(2)}) copy-start(bf16[4,256,384]{2,1,0:T(8,128)(2,1)S(1)} %collective-permute-done.4.refs_8_.refs_4_) | copy-start | bytes 2359300
  59.6 11.1 %collective-permute-start.10 = (bf16[2,256,384]{2,1,0:T(8,128)(2,1)S(1)}, bf16[2,256,384]{2,1,0:T(8,128)(2,1)S(1)}, u32[]{:S(2)}, u32[]{:S(2)}) collective-permute-start(bf16[2,256,384]{2,1,0:T(8,128)(2,1)S(1)} %slice.25), channel_id=1, source_target_pairs={{0,8},{4,12},{8,0},{12,4},{16,24},{20,28},{24,16},{28,20},{1,9},{5... | collective-permute-start | bytes 1179656 | tf_op jit(solution)/shard_map/ppermute | solution.py:578
  67.0 7.4 %copy-start.13 = (bf16[2,256,384]{2,1,0:T(8,128)(2,1)}, bf16[2,256,384]{2,1,0:T(8,128)(2,1)S(1)}, u32[]{:S(2)}) copy-start(bf16[2,256,384]{2,1,0:T(8,128)(2,1)S(1)} %collective-permute-done.9.refs_13_.refs_9_) | copy-start | bytes 1179652
  67.0 5.6 %collective-permute-start.11 = (bf16[2,256,384]{2,1,0:T(8,128)(2,1)S(1)}, bf16[2,256,384]{2,1,0:T(8,128)(2,1)S(1)}, u32[]{:S(2)}, u32[]{:S(2)}) collective-permute-start(bf16[2,256,384]{2,1,0:T(8,128)(2,1)S(1)} %collective-permute-done.9.refs_13_.refs_9_), channel_id=1, source_target_pairs={{0,4},{4,0},{8,12},{12,8},{16,20},{20,16},{24,28},{28,24},{1,5},{5... | collective-permute-start | bytes 1179656 | tf_op jit(solution)/shard_map/ppermute | solution.py:578
  70.7 2.8 copy-start.14
  70.7 2.8 collective-permute-start.12
  71.4 3.0 copy-start.17
  147.1 4.2 %copy-start.9 = (s16[1,512,1024]{2,1,0:T(8,128)(2,1)S(1)}, s16[1,512,1024]{2,1,0:T(8,128)(2,1)}, u32[]{:S(2)}) copy-start(s16[1,512,1024]{2,1,0:T(8,128)(2,1)} %get-tuple-element.21) | copy-start | bytes 3145732
  147.1 52.1 %all-to-all-start.2 = ((bf16[32,4,2,32,128]{4,3,2,1,0:T(8,128)(2,1)}), bf16[32,4,2,32,128]{4,3,2,1,0:T(8,128)(2,1)}, u32[]{:S(2)}, u32[]{:S(2)}) async-start(bf16[32,4,2,32,128]{4,3,2,1,0:T(8,128)(2,1)} %row_both.1), calls=%async_computation.2 | async-start | bytes 4194304 | tf_op jit(solution)/shard_map/all_to_all | solution.py:572
  151.4 21.8 %collective-permute-start.17 = (s16[512,256]{1,0:T(8,128)(2,1)S(1)}, s16[512,256]{1,0:T(8,128)(2,1)S(1)}, u32[]{:S(2)}, u32[]{:S(2)}) collective-permute-start(s16[512,256]{1,0:T(8,128)(2,1)S(1)} %get-tuple-element.32), channel_id=1, source_target_pairs={{0,8},{4,12},{8,0},{12,4},{16,24},{20,28},{24,16},{28,20},{1,9},{5... | collective-permute-start | bytes 786440 | tf_op jit(solution)/shard_map/ppermute | solution.py:578
  152.9 20.9 %collective-permute-start.18 = (s16[512,256]{1,0:T(8,128)(2,1)S(1)}, s16[512,256]{1,0:T(8,128)(2,1)S(1)}, u32[]{:S(2)}, u32[]{:S(2)}) collective-permute-start(s16[512,256]{1,0:T(8,128)(2,1)S(1)} %get-tuple-element.31), channel_id=1, source_target_pairs={{0,16},{4,20},{8,24},{12,28},{16,0},{20,4},{24,8},{28,12},{1,17},{... | collective-permute-start | bytes 786440 | tf_op jit(solution)/shard_map/ppermute | solution.py:578
  153.5 29.9 %collective-permute-start.19 = (s16[512,256]{1,0:T(8,128)(2,1)S(1)}, s16[512,256]{1,0:T(8,128)(2,1)S(1)}, u32[]{:S(2)}, u32[]{:S(2)}) collective-permute-start(s16[512,256]{1,0:T(8,128)(2,1)S(1)} %get-tuple-element.30), channel_id=1, source_target_pairs={{0,24},{4,28},{8,16},{12,20},{16,8},{20,12},{24,0},{28,4},{1,25},{... | collective-permute-start | bytes 786440 | tf_op jit(solution)/shard_map/ppermute | solution.py:578
  184.1 2.0 collective-permute-start.20
  186.1 13.1 %copy-start.20 = (s16[4,512,128]{2,1,0:T(8,128)(2,1)}, s16[4,512,128]{2,1,0:T(8,128)(2,1)S(1)}, u32[]{:S(2)}) copy-start(s16[4,512,128]{2,1,0:T(8,128)(2,1)S(1)} %collective-permute-done.20.refs_17_) | copy-start | bytes 1572868
  212.3 51.8 %all-to-all-start.3 = ((bf16[32,4,2,32,128]{4,3,2,1,0:T(8,128)(2,1)}), bf16[32,4,2,32,128]{4,3,2,1,0:T(8,128)(2,1)}, u32[]{:S(2)}, u32[]{:S(2)}) async-start(bf16[32,4,2,32,128]{4,3,2,1,0:T(8,128)(2,1)} %bitcast.43), calls=%async_computation.3 | async-start | bytes 4194304 | tf_op jit(solution)/shard_map/all_to_all | solution.py:572
  268.5 39.1 %copy-start.3 = (bf16[256,256]{1,0:T(8,128)(2,1)S(1)}, bf16[256,256]{1,0:T(8,128)(2,1)}, u32[]{:S(2)}) copy-start(bf16[256,256]{1,0:T(8,128)(2,1)} %constant.201.clone.refs_6_) | copy-start | bytes 393220
  268.5 39.1 %copy-start.5 = (bf16[2,8,64,128]{3,2,1,0:T(8,128)(2,1)S(1)}, bf16[2,8,64,128]{3,2,1,0:T(8,128)(2,1)}, u32[]{:S(2)}) copy-start(bf16[2,8,64,128]{3,2,1,0:T(8,128)(2,1)} %get-tuple-element.17.refs_1_) | copy-start | bytes 786436
  268.6 11.1 %collective-permute-start.24 = (bf16[2,8,64,128]{3,2,1,0:T(8,128)(2,1)}, bf16[2,8,64,128]{3,2,1,0:T(8,128)(2,1)S(1)}, u32[]{:S(2)}, u32[]{:S(2)}) collective-permute-start(bf16[2,8,64,128]{3,2,1,0:T(8,128)(2,1)} %get-tuple-element.18), channel_id=1, source_target_pairs={{0,1},{1,0},{2,3},{3,2},{4,5},{5,4},{6,7},{7,6},{8,9},{9,8},{10,11... | collective-permute-start | bytes 786440 | tf_op jit(solution)/shard_map/ppermute | solution.py:578
  268.6 20.2 %collective-permute-start.25 = (bf16[2,8,64,128]{3,2,1,0:T(8,128)(2,1)}, bf16[2,8,64,128]{3,2,1,0:T(8,128)(2,1)S(1)}, u32[]{:S(2)}, u32[]{:S(2)}) collective-permute-start(bf16[2,8,64,128]{3,2,1,0:T(8,128)(2,1)} %get-tuple-element.19), channel_id=1, source_target_pairs={{0,2},{1,3},{2,0},{3,1},{4,6},{5,7},{6,4},{7,5},{8,10},{9,11},{10,... | collective-permute-start | bytes 786440 | tf_op jit(solution)/shard_map/ppermute | solution.py:578
  270.6 37.0 %collective-permute-start.26 = (bf16[2,8,64,128]{3,2,1,0:T(8,128)(2,1)}, bf16[2,8,64,128]{3,2,1,0:T(8,128)(2,1)S(1)}, u32[]{:S(2)}, u32[]{:S(2)}) collective-permute-start(bf16[2,8,64,128]{3,2,1,0:T(8,128)(2,1)} %get-tuple-element.20), channel_id=1, source_target_pairs={{0,3},{1,2},{2,1},{3,0},{4,7},{5,6},{6,5},{7,4},{8,11},{9,10},{10,... | collective-permute-start | bytes 786440 | tf_op jit(solution)/shard_map/ppermute | solution.py:578
  276.5 37.3 %collective-permute-start.21 = (bf16[2,8,64,128]{3,2,1,0:T(8,128)(2,1)}, bf16[2,8,64,128]{3,2,1,0:T(8,128)(2,1)S(1)}, u32[]{:S(2)}, u32[]{:S(2)}) collective-permute-start(bf16[2,8,64,128]{3,2,1,0:T(8,128)(2,1)} %get-tuple-element.14), channel_id=1, source_target_pairs={{0,1},{1,0},{2,3},{3,2},{4,5},{5,4},{6,7},{7,6},{8,9},{9,8},{10,11... | collective-permute-start | bytes 786440 | tf_op jit(solution)/shard_map/ppermute | solution.py:578
  277.6 36.3 %collective-permute-start.22 = (bf16[2,8,64,128]{3,2,1,0:T(8,128)(2,1)}, bf16[2,8,64,128]{3,2,1,0:T(8,128)(2,1)S(1)}, u32[]{:S(2)}, u32[]{:S(2)}) collective-permute-start(bf16[2,8,64,128]{3,2,1,0:T(8,128)(2,1)} %get-tuple-element.15), channel_id=1, source_target_pairs={{0,2},{1,3},{2,0},{3,1},{4,6},{5,7},{6,4},{7,5},{8,10},{9,11},{10,... | collective-permute-start | bytes 786440 | tf_op jit(solution)/shard_map/ppermute | solution.py:578
  279.7 38.0 %collective-permute-start.23 = (bf16[2,8,64,128]{3,2,1,0:T(8,128)(2,1)}, bf16[2,8,64,128]{3,2,1,0:T(8,128)(2,1)S(1)}, u32[]{:S(2)}, u32[]{:S(2)}) collective-permute-start(bf16[2,8,64,128]{3,2,1,0:T(8,128)(2,1)} %get-tuple-element.16), channel_id=1, source_target_pairs={{0,3},{1,2},{2,1},{3,0},{4,7},{5,6},{6,5},{7,4},{8,11},{9,10},{10,... | collective-permute-start | bytes 786440 | tf_op jit(solution)/shard_map/ppermute | solution.py:578
  307.6 1.6 copy-start
  310.8 6.9 %copy-start.2 = (bf16[1024,1024]{1,0:T(8,128)(2,1)S(1)}, bf16[1024,1024]{1,0:T(8,128)(2,1)}, u32[]{:S(2)}) copy-start(bf16[1024,1024]{1,0:T(8,128)(2,1)} %constant.202.clone.refs_7_) | copy-start | bytes 6291460
  310.8 6.9 %copy-start.4 = (bf16[2,8,64,128]{3,2,1,0:T(8,128)(2,1)S(1)}, bf16[2,8,64,128]{3,2,1,0:T(8,128)(2,1)}, u32[]{:S(2)}) copy-start(bf16[2,8,64,128]{3,2,1,0:T(8,128)(2,1)} %get-tuple-element.13.refs_1_) | copy-start | bytes 786436
  (5 other events, 5.3 us)
